TPU v7x, 512 devices: a whole 4x4x16 slice. The times are simulated.
512 devices in a mesh: row: 32 (over y, z_hi, core), col: 16 (over x, z_lo).
Axes of the slice: x: 4, y: 4, z: 16 (z_hi: 4, z_lo: 4; z = z_hi * 4 + z_lo), core: 2. Of those that a mesh axis runs over, the one named last changes fastest.
Arguments:
- panels: bfloat16 [32768, 16384], P('row', 'col'), may hold values from -6 to 6
- self_factors: bfloat16 [4, 32768, 128], P(None, 'row'), may hold values from -0.375 to 0.375
- partner_factors: bfloat16 [4, 32768, 128], P(None, 'row'), may hold values from -0.375 to 0.375
- link_mask: int32 [4, 256], P(None, 'row'), may hold values 0 or 1
- block_ranks: int32 [256], P('row'), may hold values from 64 to 128, as said below
Outputs:
- coefficients: float32 [32768, 128], P('row')
Inputs may be any that keep to these rules, and one draw needn't show every extreme that they name: `block_ranks`: number of leading basis rows used by each row block; both ends occur in every draw.
All inputs are finite; a program needn't handle non-finite values. No bound on the sum of `link_mask` on one device may be relied on, other than what follows from the above.
Results may differ from a plain program's by a relative error of at most 0.0012.
Values may be sent and summed in bfloat16 or wider, within the bound.
No kernel may reach another device: no remote copies, remote signals or barrier semaphores. Data moves between devices by JAX's collectives and lax.ppermute only.
A program may use at most 64 MiB of HBM per device.

v0:
```python
import math

import jax
import jax.numpy as jnp
from jax import lax
from jax.sharding import PartitionSpec as P

RANK = 128
LEVELS = 4


def partner(block, axis, stride):
    count = lax.axis_size(axis)
    route = []
    for low in range(count):
        high = low | 1 << stride
        if high != low and high < count:
            route += [(low, high), (high, low)]
    return lax.ppermute(block, axis, route)


def settle(cross_sum, gram_sum, block_ranks):
    kept_mask = (jnp.arange(RANK, dtype=jnp.int32)[None, :] < block_ranks[:, None]).astype(
        jnp.float32
    )
    cross_sum = cross_sum * kept_mask[:, None, :]
    identity = jnp.eye(RANK, dtype=jnp.float32)
    gram_sum = (
        gram_sum * kept_mask[:, :, None] * kept_mask[:, None, :]
        + identity * (1.0 - kept_mask)[:, None, :]
    )
    cholesky_factor = jnp.linalg.cholesky(gram_sum)
    halfway = lax.linalg.triangular_solve(
        cholesky_factor, cross_sum, left_side=False, lower=True, transpose_a=True
    )
    result = lax.linalg.triangular_solve(
        cholesky_factor, halfway, left_side=False, lower=True, transpose_a=False
    )
    return 4.0 * math.sqrt(RANK) * result.reshape(-1, RANK)


def partner_of(present_level, bit_level):
    return partner(present_level, "row", bit_level)


def body(panels, self_factors, partner_factors, link_mask, block_ranks):
    top_precision = lax.Precision.HIGHEST
    local_rows, local_cols = panels.shape
    blocks = local_rows // RANK
    log_rows = lax.axis_size("row").bit_length() - 1
    level_bits = [(2 * tree_depth + 1) % log_rows for tree_depth in range(LEVELS)]
    random_projection = panels.reshape(blocks, RANK, local_cols)
    own_blocks = self_factors.reshape(LEVELS, blocks, RANK, RANK)
    paired_blocks = partner_factors.reshape(LEVELS, blocks, RANK, RANK)
    coupling_weight = link_mask.astype(jnp.float32)
    local_gram_matrix = jnp.einsum(
        "hni,hei->hne", random_projection, random_projection, preferred_element_type=jnp.float32
    )
    present_level = random_projection
    for tree_depth in range(LEVELS - 1):
        paired_index = partner_of(present_level, level_bits[tree_depth])
        blended_rows = jnp.einsum(
            "nrf,nfe->nre",
            own_blocks[tree_depth],
            present_level,
            preferred_element_type=jnp.float32,
        )
        blended_rows = blended_rows + coupling_weight[tree_depth][:, None, None] * jnp.einsum(
            "nrf,nfe->nre",
            paired_blocks[tree_depth],
            paired_index,
            preferred_element_type=jnp.float32,
        )
        present_level = blended_rows.astype(jnp.bfloat16)
    inner_adjacent = jnp.einsum(
        "hni,hei->hne", present_level, random_projection, preferred_element_type=jnp.float32
    )
    paired_index = partner_of(present_level, level_bits[-1])
    inner_distant = jnp.einsum(
        "hni,hei->hne", paired_index, random_projection, preferred_element_type=jnp.float32
    )
    cross_local = jnp.einsum(
        "gab,gbc->gac", own_blocks[-1].astype(jnp.float32), inner_adjacent, precision=top_precision
    )
    cross_local = cross_local + coupling_weight[-1][:, None, None] * jnp.einsum(
        "gab,gbc->gac",
        paired_blocks[-1].astype(jnp.float32),
        inner_distant,
        precision=top_precision,
    )
    cross_total, gram_total = lax.psum((cross_local, local_gram_matrix), "col")
    return settle(cross_total, gram_total, block_ranks)


def solution(mesh):
    return jax.shard_map(
        body,
        mesh=mesh,
        in_specs=(
            P("row", "col"),
            P(None, "row", None),
            P(None, "row", None),
            P(None, "row"),
            P("row"),
        ),
        out_specs=P("row", None),
        check_vma=False,
    )
```

profile of v0, /device:TPU:24, one launch (start us, length us, event | category | flops | bytes accessed | tf_op | source)
XLA Modules:
  0.0 767.4 jit_solution(2368580084914610051)
XLA Ops:
  6.5 9.2 %collective-permute-start = (bf16[8,128,1024]{2,1,0:T(8,128)(2,1)}, bf16[8,128,1024]{2,1,0:T(8,128)(2,1)S(1)}, u32[]{:S(2)}, u32[]{:S(2)}) collective-permute-start(bf16[8,128,1024]{2,1,0:T(8,128)(2,1)} %bitcast.56), channel_id=1, source_target_pairs={{0,32},{32,0},{16,48},{48,16},{64,96},{96,64},{80,112},{112,80},{1... | collective-permute-start | bytes 6291464 | tf_op jit(solution)/shard_map/ppermute | solution.py:19
  16.5 1.4 fusion.11
  19.1 177.4 %collective-permute-done = bf16[8,128,1024]{2,1,0:T(8,128)(2,1)S(1)} collective-permute-done((bf16[8,128,1024]{2,1,0:T(8,128)(2,1)}, bf16[8,128,1024]{2,1,0:T(8,128)(2,1)S(1)}, u32[]{:S(2)}, u32[]{:S(2)}) %collective-permute-start) | collective-permute-done | bytes 2097184 | tf_op jit(solution)/shard_map/ppermute | solution.py:19
  196.4 0.8 add_convert_fusion.2
  197.2 2.7 collective-permute-start.1
  199.8 0.8 fusion.13
  200.7 45.2 %collective-permute-done.1 = bf16[8,128,1024]{2,1,0:T(8,128)(2,1)S(1)} collective-permute-done((bf16[8,128,1024]{2,1,0:T(8,128)(2,1)S(1)}, bf16[8,128,1024]{2,1,0:T(8,128)(2,1)S(1)}, u32[]{:S(2)}, u32[]{:S(2)}) %collective-permute-start.1) | collective-permute-done | bytes 2097184 | tf_op jit(solution)/shard_map/ppermute | solution.py:19
  245.9 1.3 add_convert_fusion.1
  247.2 1.9 collective-permute-start.2
  249.1 0.7 fusion.14
  249.8 3.4 collective-permute-done.2
  253.2 0.7 add_convert_fusion
  253.9 14.4 %collective-permute-start.3 = (bf16[8,128,1024]{1,2,0:T(8,128)(2,1)S(1)}, bf16[8,128,1024]{1,2,0:T(8,128)(2,1)S(1)}, u32[]{:S(2)}, u32[]{:S(2)}) collective-permute-start(bf16[8,128,1024]{1,2,0:T(8,128)(2,1)S(1)} %bitcast.62), channel_id=1, source_target_pairs={{0,64},{64,0},{16,80},{80,16},{32,96},{96,32},{48,112},{112,48},{1... | collective-permute-start | bytes 6291464 | tf_op jit(solution)/shard_map/ppermute | solution.py:19
  268.4 1.5 fusion.18
  269.9 0.8 fusion.15
  271.3 138.0 %collective-permute-done.3 = bf16[8,128,1024]{1,2,0:T(8,128)(2,1)S(1)} collective-permute-done((bf16[8,128,1024]{1,2,0:T(8,128)(2,1)S(1)}, bf16[8,128,1024]{1,2,0:T(8,128)(2,1)S(1)}, u32[]{:S(2)}, u32[]{:S(2)}) %collective-permute-start.3) | collective-permute-done | bytes 2097184 | tf_op jit(solution)/shard_map/ppermute | solution.py:19
  409.3 0.8 fusion.17
  410.1 1.4 fusion.1
  411.9 170.6 %all-reduce.3.cloned.1.call-done = (f32[8,128,128]{1,2,0:T(8,128)}, f32[8,128,128]{1,2,0:T(8,128)}) async-done(((f32[8,128,128]{1,2,0:T(8,128)}, f32[8,128,128]{1,2,0:T(8,128)}), (f32[8,128,128]{1,2,0:T(8,128)}, f32[8,128,128]{1,2,0:T(8,128)})) %all-reduce.3.cloned.1.call-update) | async-done | bytes 1048592 | tf_op jit(solution)/shard_map/psum | solution.py:91
  582.5 1.4 multiply_add_fusion
  584.5 94.0 %custom-call.9 = f32[8,128,128]{2,1,0:T(8,128)S(1)} custom-call(f32[8,128,128]{2,1,0:T(8,128)S(1)} %fusion.5), custom_call_target="Cholesky" | custom-call | tf_op jit(solution)/shard_map/jit(cholesky)/cholesky | solution.py:32
  678.8 78.6 %custom-call.10 = f32[8,1,128,128]{2,3,1,0:T(8,128)S(1)} custom-call(f32[8,1,128,128]{3,2,1,0:T(8,128)S(1)} %select_bitcast_fusion), custom_call_target="InvertDiagBlocksLowerTriangular" | custom-call | tf_op jit(solution)/shard_map/triangular_solve | solution.py:33
  757.4 1.2 fusion.3
  758.6 2.0 convolution_multiply_fusion
  (28 shorter events, 3.6 us)
Async XLA Ops:
  6.5 11.3 %copy-start.2 = (bf16[4,1024,128]{2,1,0:T(8,128)(2,1)S(1)}, bf16[4,1024,128]{2,1,0:T(8,128)(2,1)}, u32[]{:S(2)}) copy-start(bf16[4,1024,128]{2,1,0:T(8,128)(2,1)} %param.7) | copy-start | bytes 3145732
  6.5 576.0 %all-reduce.3.cloned.1.call-start = ((), (), s32[]{:S(2)}) async-start(), calls=%async_computation | async-start | bytes 2097152 | tf_op jit(solution)/shard_map/psum | solution.py:91
  6.5 189.9 %collective-permute-start = (bf16[8,128,1024]{2,1,0:T(8,128)(2,1)}, bf16[8,128,1024]{2,1,0:T(8,128)(2,1)S(1)}, u32[]{:S(2)}, u32[]{:S(2)}) collective-permute-start(bf16[8,128,1024]{2,1,0:T(8,128)(2,1)} %bitcast.56), channel_id=1, source_target_pairs={{0,32},{32,0},{16,48},{48,16},{64,96},{96,64},{80,112},{112,80},{1... | collective-permute-start | bytes 6291464 | tf_op jit(solution)/shard_map/ppermute | solution.py:19
  16.5 1.9 copy-start
  197.2 48.7 %collective-permute-start.1 = (bf16[8,128,1024]{2,1,0:T(8,128)(2,1)S(1)}, bf16[8,128,1024]{2,1,0:T(8,128)(2,1)S(1)}, u32[]{:S(2)}, u32[]{:S(2)}) collective-permute-start(bf16[8,128,1024]{2,1,0:T(8,128)(2,1)S(1)} %add_convert_fusion.2), channel_id=1, source_target_pairs={{0,128},{128,0},{16,144},{144,16},{32,160},{160,32},{48,176},{176,... | collective-permute-start | bytes 6291464 | tf_op jit(solution)/shard_map/ppermute | solution.py:19
  247.2 6.1 collective-permute-start.2
  253.9 155.4 %collective-permute-start.3 = (bf16[8,128,1024]{1,2,0:T(8,128)(2,1)S(1)}, bf16[8,128,1024]{1,2,0:T(8,128)(2,1)S(1)}, u32[]{:S(2)}, u32[]{:S(2)}) collective-permute-start(bf16[8,128,1024]{1,2,0:T(8,128)(2,1)S(1)} %bitcast.62), channel_id=1, source_target_pairs={{0,64},{64,0},{16,80},{80,16},{32,96},{96,32},{48,112},{112,48},{1... | collective-permute-start | bytes 6291464 | tf_op jit(solution)/shard_map/ppermute | solution.py:19
  410.1 1.6 copy-start.4
  582.5 1.7 copy-start.1
  584.0 173.4 %copy-start.3 = (f32[8,128,128]{1,2,0:T(8,128)S(1)}, f32[8,128,128]{1,2,0:T(8,128)}, u32[]{:S(2)}) copy-start(f32[8,128,128]{1,2,0:T(8,128)} %get-tuple-element.6) | copy-start | bytes 1572868
Sparse Core Ops, SparseCore 0:
  411.7 170.7 all-reduce.2
where the time goes:
time: 768 us; the launch traced here: 767 us
  waiting for transfers between devices  535 us (70%)
  other arithmetic  176 us (23%)
  starting transfers between devices  28.2 us (4%)
  between operations  13.6 us (2%)
  matrix products  13.3 us (2%)
    ppermute x4, waiting for transfers between devices, partner(): return lax.ppermute(block, axis, route)  364 us
    psum x1, waiting for transfers between devices, body(): cross_total, gram_total = lax.psum((cross_local, local_gram_matrix), 'col')  171 us
    another operation x4, other arithmetic, settle(): cholesky_factor = jnp.linalg.cholesky(gram_sum)  94.1 us
    another operation x3, other arithmetic, settle(): lax.linalg.triangular_solve(cholesky_factor, cross_sum, left_side=False,...  78.7 us
    ppermute x4, starting transfers between devices, partner(): return lax.ppermute(block, axis, route)  28.2 us
  transfers between devices with their start and end apart: 5, of which 5 were waited for; matrix products, arithmetic and copies ran while one was open for 1% of the time, Pallas kernels for 0%

commit v1 on v0

v1 whole, which is shorter than its diff:
```python
import functools
import math

import jax
import jax.numpy as jnp
from jax import lax
from jax.experimental import pallas as pl
from jax.experimental.pallas import tpu as pltpu
from jax.sharding import Mesh, PartitionSpec as P

RANK = 128
LEVELS = 4
SLOTS = 8
ROW = ("yh", "yl", "zh", "core")
COL = ("x", "zl")
PEERS = ("yl", "zh")
HIGHEST = lax.Precision.HIGHEST


def invert_kernel(gram_ref, keep_ref, out_ref):
    lane = lax.broadcasted_iota(jnp.int32, (8, RANK), 1)
    sub = lax.broadcasted_iota(jnp.int32, (8, RANK), 0)
    rows = lax.broadcasted_iota(jnp.int32, (RANK, RANK), 0)
    cols = lax.broadcasted_iota(jnp.int32, (RANK, RANK), 1)
    blocks = gram_ref.shape[0]
    tiles = []
    for b in range(blocks):
        tiles.append([gram_ref[b, 8 * g : 8 * g + 8, :] for g in range(RANK // 8)])
    for k in range(RANK):
        first, at = k // 8, k % 8
        for b in range(blocks):
            tile = tiles[b]
            row = tile[first][at : at + 1, :]
            scaled = jnp.where(lane[:1] == k, 1.0, row) / row[:, k : k + 1]
            for g in range(first, RANK // 8):
                column = tile[g][:, k : k + 1]
                clear = lane == k
                if g == first:
                    column = jnp.where(sub[:, :1] > at, column, 0.0)
                    clear = clear & (sub > at)
                tile[g] = jnp.where(clear, 0.0, tile[g]) - column * scaled
    for b in range(blocks):
        done = jnp.concatenate(tiles[b], axis=0)
        pivots = jnp.sum(jnp.where(rows == cols, done, 0.0), axis=1, keepdims=True)
        lower = jnp.where(rows > cols, done, jnp.where(rows == cols, 1.0, 0.0))
        inverse = lax.dot_general(
            lower,
            lower / pivots,
            (((0,), (0,)), ((), ())),
            precision=HIGHEST,
            preferred_element_type=jnp.float32,
        )
        out_ref[b] = inverse * keep_ref[b] * (4.0 * math.sqrt(RANK))


def invert(gram, keep):
    return pl.pallas_call(
        invert_kernel,
        out_shape=jax.ShapeDtypeStruct(gram.shape, jnp.float32),
        in_specs=[pl.BlockSpec(memory_space=pltpu.VMEM)] * 2,
        out_specs=pl.BlockSpec(memory_space=pltpu.VMEM),
        compiler_params=pltpu.CompilerParams(vmem_limit_bytes=32 * 2**20),
    )(gram, jnp.broadcast_to(keep[:, :, None], gram.shape))


def pick(blocks, index):
    return lax.dynamic_index_in_dim(blocks, index, 0, keepdims=False)


def body(panels, self_factors, partner_factors, link_mask, block_ranks):
    local_cols = panels.shape[1]
    me = lax.axis_index("yl") * 4 + lax.axis_index("zh")
    x_at, zl_at = lax.axis_index("x"), lax.axis_index("zl")
    own = panels.reshape(SLOTS, RANK, local_cols)

    base = [pick(own, me)]
    for r in range(1, SLOTS):
        base.append(
            lax.ppermute(pick(own, me ^ r), PEERS, [(i, i ^ r) for i in range(SLOTS)])
        )

    quarter = RANK // 4
    start = x_at, 0, zl_at * quarter, 0
    shape = 1, SLOTS, quarter, RANK
    mask = lax.dynamic_index_in_dim(link_mask, x_at, 0, keepdims=False).astype(jnp.bfloat16)
    own_rows = lax.dynamic_slice(
        self_factors.reshape(LEVELS, SLOTS, RANK, RANK), start, shape
    )[0]
    paired_rows = lax.dynamic_slice(
        partner_factors.reshape(LEVELS, SLOTS, RANK, RANK), start, shape
    )[0]
    pair = jnp.concatenate([own_rows, paired_rows * mask[:, None, None]], axis=2)
    pair = lax.all_to_all(pair, PEERS, 0, 0, tiled=True)
    pair = jnp.stack([pick(pair, me ^ r) for r in range(SLOTS)])
    pair = lax.all_gather(pair, "zl", axis=1, tiled=True)
    factors = lax.all_gather(pair, "x", axis=0)

    gram = jnp.einsum("hni,hei->hne", own, own, preferred_element_type=jnp.float32)
    gram = lax.all_to_all(gram.reshape(4, 2, RANK, RANK), "x", 0, 0, tiled=True).sum(0)
    gram = lax.all_gather(gram, "zl", axis=0).sum(0)
    ranks = lax.dynamic_slice_in_dim(block_ranks, x_at * 2, 2, 0)
    keep = (jnp.arange(RANK, dtype=jnp.int32)[None, :] < ranks[:, None]).astype(jnp.float32)
    identity = jnp.eye(RANK, dtype=jnp.float32)
    gram = gram * keep[:, :, None] * keep[:, None, :] + identity * (1.0 - keep)[:, None, :]
    inverse = lax.all_gather(invert(gram, keep), "x", axis=0, tiled=True)

    base = jnp.stack(base)
    flip = lambda level, bit: jnp.stack([level[r ^ bit] for r in range(SLOTS)])
    mix = lambda depth, level, paired: jnp.einsum(
        "hnf,hfe->hne",
        factors[depth],
        jnp.concatenate([level, paired], axis=1),
        preferred_element_type=jnp.float32,
    ).astype(jnp.bfloat16)
    level = mix(0, base, flip(base, 1))
    level = mix(1, level, flip(level, 4))
    level = mix(2, level, lax.ppermute(level, "core", [(0, 1), (1, 0)]))
    dots = functools.partial(jnp.einsum, "hni,hei->hne", preferred_element_type=jnp.float32)
    near = dots(level, base)
    far = dots(flip(level, 2), base)
    cross = jnp.einsum(
        "gab,gbc->gac",
        factors[3].astype(jnp.float32),
        jnp.concatenate([near, far], axis=1),
        precision=HIGHEST,
    )

    cross = cross.reshape(SLOTS, 16, 8, RANK).transpose(1, 0, 2, 3)
    cross = lax.all_to_all(cross, COL, 0, 0, tiled=True).sum(0)
    cross = jnp.stack([pick(cross, me ^ r) for r in range(SLOTS)])
    cross = lax.all_to_all(cross, PEERS, 0, 0, tiled=True)
    solved = jnp.einsum("jrk,jkm->jrm", cross, inverse, precision=HIGHEST)
    solved = jnp.broadcast_to(solved[None], (16,) + solved.shape)
    solved = lax.all_to_all(solved, COL, 0, 0, tiled=True)
    return solved.transpose(1, 0, 2, 3).reshape(-1, RANK)


def solution(mesh):
    split = Mesh(mesh.devices.reshape(2, 2, 4, 2, 4, 4), ROW + COL)
    return jax.shard_map(
        body,
        mesh=split,
        in_specs=(P(ROW, COL), P(None, ROW, None), P(None, ROW, None), P(None, ROW), P(ROW)),
        out_specs=P(ROW, None),
        check_vma=False,
    )
```

time: 768 us -> 305 us (0.40)
  waiting for transfers between devices: 535 us -> 91.9 us
  other arithmetic: 176 us -> 3.83 us
  blocking collectives: 0 us -> 72.8 us
  starting transfers between devices: 28.2 us -> 78.8 us
  local copies, waits for them, and re-layouts: 2.19 us -> 16.5 us
  Pallas kernels: 0 us -> 11.1 us
    ppermute x4 -> x8, waiting for transfers between devices: 364 us -> 77.8 us  [the longest x7 77.8 us: body(): lax.ppermute(pick(own, me ^ r), PEERS, [(i, i ^ r) for i in range(SLOTS)])]
    another operation x7 -> x0, other arithmetic: 173 us -> none  [the longest x4 94.1 us: settle(): cholesky_factor = jnp.linalg.cholesky(gram_sum)]
    psum x1 -> x0, waiting for transfers between devices: 171 us -> none  [body(): cross_total, gram_total = lax.psum((cross_local, local_gram_matrix), 'col')]
    all_gather x0 -> x3, blocking collectives: none -> 53.7 us  [the longest x1 22.9 us: body(): gram = lax.all_gather(gram, 'zl', axis=0).sum(0)]
    all_to_all x0 -> x4, starting transfers between devices: none -> 47.9 us  [the longest x1 23.7 us: body(): cross = lax.all_to_all(cross, COL, 0, 0, tiled=True).sum(0)]
    all_to_all x0 -> x1, blocking collectives: none -> 19.1 us  [body(): solved = lax.all_to_all(solved, COL, 0, 0, tiled=True)]
    all_to_all x0 -> x4, waiting for transfers between devices: none -> 14.2 us  [the longest x1 13.7 us: body(): pair = lax.all_to_all(pair, PEERS, 0, 0, tiled=True)]
    unnamed x10 -> x36, local copies, waits for them, and re-layouts: 0.43 us -> 12 us
  transfers between devices with their start and end apart: 5 -> 13, of which waited for: 5 -> 6; matrix products, arithmetic and copies ran while one was open for 1% -> 6% of each run, Pallas kernels for 0% -> 4%
where the time goes in v1:
time: 305 us
  waiting for transfers between devices  91.9 us (30%)
  starting transfers between devices  78.8 us (26%)
  blocking collectives  72.8 us (24%)
  local copies, waits for them, and re-layouts  16.5 us (5%)
  matrix products  15.9 us (5%)
  between operations  13.7 us (4%)
  Pallas kernels  11.1 us (4%)
  other arithmetic  3.83 us (1%)
    ppermute x7, waiting for transfers between devices, body(): lax.ppermute(pick(own, me ^ r), PEERS, [(i, i ^ r) for i in range(SLOTS)])  77.8 us
    ppermute x7, starting transfers between devices, body(): lax.ppermute(pick(own, me ^ r), PEERS, [(i, i ^ r) for i in range(SLOTS)])  29 us
    all_to_all x1, starting transfers between devices, body(): cross = lax.all_to_all(cross, COL, 0, 0, tiled=True).sum(0)  23.7 us
    all_gather x1, blocking collectives, body(): gram = lax.all_gather(gram, 'zl', axis=0).sum(0)  22.9 us
    all_to_all x1, blocking collectives, body(): solved = lax.all_to_all(solved, COL, 0, 0, tiled=True)  19.1 us
    all_gather x1, blocking collectives, body(): pair = lax.all_gather(pair, 'zl', axis=1, tiled=True)  17.2 us
    all_to_all x1, starting transfers between devices, body(): pair = lax.all_to_all(pair, PEERS, 0, 0, tiled=True)  16.5 us
    all_to_all x1, waiting for transfers between devices, body(): pair = lax.all_to_all(pair, PEERS, 0, 0, tiled=True)  13.7 us
  transfers between devices with their start and end apart: 13, of which 6 were waited for; matrix products, arithmetic and copies ran while one was open for 6% of the time, Pallas kernels for 4%

profile of v1, /device:TPU:24, one launch (start us, length us, event | category | flops | bytes accessed | tf_op | source)
XLA Modules:
  0.0 304.5 jit_solution(12783837438233987648)
XLA Ops:
  9.4 16.5 %all-to-all-start = ((bf16[8,32,256]{2,1,0:T(8,128)(2,1)}), bf16[8,32,256]{2,1,0:T(8,128)(2,1)S(1)}, u32[]{:S(2)}, u32[]{:S(2)}) async-start(bf16[8,32,256]{2,1,0:T(8,128)(2,1)} %pad_maximum_fusion), calls=%async_computation | async-start | bytes 262144 | tf_op jit(solution)/shard_map/all_to_all | solution.py:93
  25.9 13.7 %all-to-all-done = bf16[8,32,256]{2,1,0:T(8,128)(2,1)S(1)} async-done(((bf16[8,32,256]{2,1,0:T(8,128)(2,1)}), bf16[8,32,256]{2,1,0:T(8,128)(2,1)S(1)}, u32[]{:S(2)}, u32[]{:S(2)}) %all-to-all-start) | async-done | bytes 131104 | tf_op jit(solution)/shard_map/all_to_all | solution.py:93
  39.7 17.2 %all_gather.18 = bf16[8,128,256]{2,1,0:T(8,128)(2,1)} all-gather(bf16[8,32,256]{2,1,0:T(8,128)(2,1)S(1)} %constant_dynamic-update-slice_fusion), channel_id=1, replica_groups=mesh['yh'=2,'yl'=2,'zh'=4,'core'=2,'x'=4,'zl'=4] {'zl'}, dimensions={1}, use_global_device_ids=true | all-gather | bytes 655360 | tf_op jit(solution)/shard_map/all_gather | solution.py:95
  57.0 4.3 %collective-permute-start = (bf16[128,1024]{1,0:T(8,128)(2,1)S(1)}, bf16[128,1024]{1,0:T(8,128)(2,1)S(1)}, u32[]{:S(2)}, u32[]{:S(2)}) collective-permute-start(bf16[128,1024]{1,0:T(8,128)(2,1)S(1)} %dynamic-slice_bitcast_fusion.6), channel_id=1, source_target_pairs={{0,32},{32,0},{64,96},{96,64},{128,160},{160,128},{192,224},{224,1... | collective-permute-start | bytes 786440 | tf_op jit(solution)/shard_map/ppermute | solution.py:79
  61.3 21.1 %collective-permute-done = bf16[128,1024]{1,0:T(8,128)(2,1)S(1)} collective-permute-done((bf16[128,1024]{1,0:T(8,128)(2,1)S(1)}, bf16[128,1024]{1,0:T(8,128)(2,1)S(1)}, u32[]{:S(2)}, u32[]{:S(2)}) %collective-permute-start) | collective-permute-done | bytes 262176 | tf_op jit(solution)/shard_map/ppermute | solution.py:79
  85.3 6.7 %collective-permute-start.1 = (bf16[128,1024]{1,0:T(8,128)(2,1)S(1)}, bf16[128,1024]{1,0:T(8,128)(2,1)S(1)}, u32[]{:S(2)}, u32[]{:S(2)}) collective-permute-start(bf16[128,1024]{1,0:T(8,128)(2,1)S(1)} %get-tuple-element.17), channel_id=1, source_target_pairs={{0,64},{32,96},{64,0},{96,32},{128,192},{160,224},{192,128},{224,1... | collective-permute-start | bytes 786440 | tf_op jit(solution)/shard_map/ppermute | solution.py:79
  92.0 8.8 %collective-permute-start.4 = (bf16[128,1024]{1,0:T(8,128)(2,1)S(1)}, bf16[128,1024]{1,0:T(8,128)(2,1)S(1)}, u32[]{:S(2)}, u32[]{:S(2)}) collective-permute-start(bf16[128,1024]{1,0:T(8,128)(2,1)S(1)} %get-tuple-element.14), channel_id=1, source_target_pairs={{0,160},{32,128},{64,224},{96,192},{128,32},{160,0},{192,96},{224,... | collective-permute-start | bytes 786440 | tf_op jit(solution)/shard_map/ppermute | solution.py:79
  100.9 2.9 collective-permute-start.3
  103.8 2.4 collective-permute-start.6
  106.9 23.7 %collective-permute-done.2 = bf16[128,1024]{1,0:T(8,128)(2,1)S(1)} collective-permute-done((bf16[128,1024]{1,0:T(8,128)(2,1)S(1)}, bf16[128,1024]{1,0:T(8,128)(2,1)S(1)}, u32[]{:S(2)}, u32[]{:S(2)}) %collective-permute-start.2) | collective-permute-done | bytes 262176 | tf_op jit(solution)/shard_map/ppermute | solution.py:79
  134.1 3.3 %collective-permute-done.4 = bf16[128,1024]{1,0:T(8,128)(2,1)S(1)} collective-permute-done((bf16[128,1024]{1,0:T(8,128)(2,1)S(1)}, bf16[128,1024]{1,0:T(8,128)(2,1)S(1)}, u32[]{:S(2)}, u32[]{:S(2)}) %collective-permute-start.4) | collective-permute-done | bytes 262176 | tf_op jit(solution)/shard_map/ppermute | solution.py:79
  138.8 29.6 %collective-permute-done.6 = bf16[128,1024]{1,0:T(8,128)(2,1)S(1)} collective-permute-done((bf16[128,1024]{1,0:T(8,128)(2,1)S(1)}, bf16[128,1024]{1,0:T(8,128)(2,1)S(1)}, u32[]{:S(2)}, u32[]{:S(2)}) %collective-permute-start.6) | collective-permute-done | bytes 262176 | tf_op jit(solution)/shard_map/ppermute | solution.py:79
  171.3 3.2 %fusion.28 = bf16[8,128,1024]{2,1,0:T(8,128)(2,1)S(1)} fusion(bf16[32,128,256]{2,1,0:T(8,128)(2,1)} %all-gather.4.cloned.1.call-done, bf16[8,128,1024]{2,1,0:T(8,128)(2,1)} %copy-done.4, bf16[8,128,1024]{2,1,0:T(8,128)(2,1)} %bitcast_dynamic-update-slice_fusion.1), kind=kOutput, calls=%fused_computation.24 | convolution fusion | flops 546308096 | bytes 8388608 | tf_op jit(solution)/shard_map/hnf,hfe->hne/dot_general | solution.py:109
  176.1 2.0 fusion.25
  181.5 4.3 %all-to-all-start.3 = ((f32[4,2,128,128]{3,2,1,0:T(8,128)}), f32[4,2,128,128]{3,2,1,0:T(8,128)}, u32[]{:S(2)}, u32[]{:S(2)}) async-start(f32[4,2,128,128]{3,2,1,0:T(8,128)} %bitcast.69), calls=%async_computation.3 | async-start | bytes 1048576 | tf_op jit(solution)/shard_map/all_to_all | solution.py:99
  185.8 3.2 %fusion.22 = bf16[8,128,1024]{2,1,0:T(8,128)(2,1)S(1)} fusion(bf16[32,128,256]{2,1,0:T(8,128)(2,1)} %all-gather.4.cloned.1.call-done, bf16[8,128,1024]{2,1,0:T(8,128)(2,1)} %collective-permute-done.7, bf16[8,128,1024]{2,1,0:T(8,128)(2,1)} %fusion.25), kind=kOutput, calls=%fused_computation.22 | convolution fusion | flops 546308096 | bytes 8388608 | tf_op jit(solution)/shard_map/hnf,hfe->hne/dot_general | solution.py:109
  189.3 2.3 fusion.14
  191.6 2.4 fusion.44
  196.1 23.7 %all-to-all-start.1 = ((f32[16,8,8,128]{3,2,1,0:T(8,128)}), f32[16,8,8,128]{3,2,1,0:T(8,128)S(1)}, u32[]{:S(2)}, u32[]{:S(2)}) async-start(f32[16,8,8,128]{3,2,1,0:T(8,128)} %bitcast.64), calls=%async_computation.1 | async-start | bytes 1048576 | tf_op jit(solution)/shard_map/all_to_all | solution.py:129
  221.2 22.9 %all-gather.1 = f32[8,128,128]{2,1,0:T(8,128)S(1)} all-gather(f32[2,128,128]{2,1,0:T(8,128)S(1)} %reduce_sum.28), channel_id=3, replica_groups=mesh['yh'=2,'yl'=2,'zh'=4,'core'=2,'x'=4,'zl'=4] {'zl'}, dimensions={0}, use_global_device_ids=true | all-gather | bytes 655360 | tf_op jit(solution)/shard_map/all_gather | solution.py:100
  244.3 11.1 %shard_map.55 = f32[2,128,128]{2,1,0:T(8,128)S(1)} custom-call(f32[2,128,128]{2,1,0:T(8,128)S(1)} %multiply_add_fusion.gram_ref, f32[2,128,128]{2,1,0:T(8,128)S(1)} %mul.51.keep_ref), custom_call_target="tpu_custom_call" | custom-call | tf_op jit(solution)/shard_map/pallas_call | solution.py:57
  260.3 3.3 %all-to-all-start.2 = ((f32[8,8,128]{2,1,0:T(8,128)}), f32[8,8,128]{2,1,0:T(8,128)S(1)}, u32[]{:S(2)}, u32[]{:S(2)}) async-start(f32[8,8,128]{2,1,0:T(8,128)} %constant_dynamic-update-slice_fusion.8), calls=%async_computation.2 | async-start | bytes 65536 | tf_op jit(solution)/shard_map/all_to_all | solution.py:131
  263.6 13.6 %all_gather.23 = f32[8,128,128]{2,1,0:T(8,128)S(1)} all-gather(f32[2,128,128]{2,1,0:T(8,128)S(1)} %shard_map.55), channel_id=1, replica_groups=mesh['yh'=2,'yl'=2,'zh'=4,'core'=2,'x'=4,'zl'=4] {'x'}, dimensions={0}, use_global_device_ids=true | all-gather | bytes 655360 | tf_op jit(solution)/shard_map/all_gather | solution.py:105
  277.8 19.1 %all_to_all.25 = f32[16,8,8,128]{3,2,1,0:T(8,128)S(1)} all-to-all(f32[16,8,8,128]{3,2,1,0:T(8,128)S(1)} %broadcast_in_dim.2), channel_id=1, replica_groups=mesh['yh'=2,'yl'=2,'zh'=4,'core'=2,'x'=4,'zl'=4] {'x','zl'}, dimensions={0} | all-to-all | bytes 1048576 | tf_op jit(solution)/shard_map/all_to_all | solution.py:134
  (75 shorter events, 29.3 us)
Async XLA Ops:
  6.5 1.2 copy-start
  6.5 50.4 %copy-start.1 = (bf16[1024,1024]{1,0:T(8,128)(2,1)S(1)}, bf16[1024,1024]{1,0:T(8,128)(2,1)}, u32[]{:S(2)}) copy-start(bf16[1024,1024]{1,0:T(8,128)(2,1)} %param.5) | copy-start | bytes 6291460
  9.4 30.2 %all-to-all-start = ((bf16[8,32,256]{2,1,0:T(8,128)(2,1)}), bf16[8,32,256]{2,1,0:T(8,128)(2,1)S(1)}, u32[]{:S(2)}, u32[]{:S(2)}) async-start(bf16[8,32,256]{2,1,0:T(8,128)(2,1)} %pad_maximum_fusion), calls=%async_computation | async-start | bytes 262144 | tf_op jit(solution)/shard_map/all_to_all | solution.py:93
  25.9 145.4 %all-gather.4.cloned.1.call-start = ((), (), s32[]{:S(2)}) async-start(), calls=%async_computation.5 | async-start | bytes 2621440 | tf_op jit(solution)/shard_map/all_gather | solution.py:96
  57.0 25.4 %collective-permute-start = (bf16[128,1024]{1,0:T(8,128)(2,1)S(1)}, bf16[128,1024]{1,0:T(8,128)(2,1)S(1)}, u32[]{:S(2)}, u32[]{:S(2)}) collective-permute-start(bf16[128,1024]{1,0:T(8,128)(2,1)S(1)} %dynamic-slice_bitcast_fusion.6), channel_id=1, source_target_pairs={{0,32},{32,0},{64,96},{96,64},{128,160},{160,128},{192,224},{224,1... | collective-permute-start | bytes 786440 | tf_op jit(solution)/shard_map/ppermute | solution.py:79
  83.4 47.2 %collective-permute-start.2 = (bf16[128,1024]{1,0:T(8,128)(2,1)S(1)}, bf16[128,1024]{1,0:T(8,128)(2,1)S(1)}, u32[]{:S(2)}, u32[]{:S(2)}) collective-permute-start(bf16[128,1024]{1,0:T(8,128)(2,1)S(1)} %get-tuple-element.16), channel_id=1, source_target_pairs={{0,96},{32,64},{64,32},{96,0},{128,224},{160,192},{192,160},{224,1... | collective-permute-start | bytes 786440 | tf_op jit(solution)/shard_map/ppermute | solution.py:79
  85.3 47.3 %collective-permute-start.1 = (bf16[128,1024]{1,0:T(8,128)(2,1)S(1)}, bf16[128,1024]{1,0:T(8,128)(2,1)S(1)}, u32[]{:S(2)}, u32[]{:S(2)}) collective-permute-start(bf16[128,1024]{1,0:T(8,128)(2,1)S(1)} %get-tuple-element.17), channel_id=1, source_target_pairs={{0,64},{32,96},{64,0},{96,32},{128,192},{160,224},{192,128},{224,1... | collective-permute-start | bytes 786440 | tf_op jit(solution)/shard_map/ppermute | solution.py:79
  92.0 45.3 %collective-permute-start.4 = (bf16[128,1024]{1,0:T(8,128)(2,1)S(1)}, bf16[128,1024]{1,0:T(8,128)(2,1)S(1)}, u32[]{:S(2)}, u32[]{:S(2)}) collective-permute-start(bf16[128,1024]{1,0:T(8,128)(2,1)S(1)} %get-tuple-element.14), channel_id=1, source_target_pairs={{0,160},{32,128},{64,224},{96,192},{128,32},{160,0},{192,96},{224,... | collective-permute-start | bytes 786440 | tf_op jit(solution)/shard_map/ppermute | solution.py:79
  100.9 36.5 %collective-permute-start.3 = (bf16[128,1024]{1,0:T(8,128)(2,1)S(1)}, bf16[128,1024]{1,0:T(8,128)(2,1)S(1)}, u32[]{:S(2)}, u32[]{:S(2)}) collective-permute-start(bf16[128,1024]{1,0:T(8,128)(2,1)S(1)} %get-tuple-element.15), channel_id=1, source_target_pairs={{0,128},{32,160},{64,192},{96,224},{128,0},{160,32},{192,64},{224,... | collective-permute-start | bytes 786440 | tf_op jit(solution)/shard_map/ppermute | solution.py:79
  103.8 64.6 %collective-permute-start.6 = (bf16[128,1024]{1,0:T(8,128)(2,1)S(1)}, bf16[128,1024]{1,0:T(8,128)(2,1)S(1)}, u32[]{:S(2)}, u32[]{:S(2)}) collective-permute-start(bf16[128,1024]{1,0:T(8,128)(2,1)S(1)} %get-tuple-element.12), channel_id=1, source_target_pairs={{0,224},{32,192},{64,160},{96,128},{128,96},{160,64},{192,32},{224... | collective-permute-start | bytes 786440 | tf_op jit(solution)/shard_map/ppermute | solution.py:79
  130.6 37.8 %collective-permute-start.5 = (bf16[128,1024]{1,0:T(8,128)(2,1)S(1)}, bf16[128,1024]{1,0:T(8,128)(2,1)S(1)}, u32[]{:S(2)}, u32[]{:S(2)}) collective-permute-start(bf16[128,1024]{1,0:T(8,128)(2,1)S(1)} %get-tuple-element.13), channel_id=1, source_target_pairs={{0,192},{32,224},{64,128},{96,160},{128,64},{160,96},{192,0},{224,... | collective-permute-start | bytes 786440 | tf_op jit(solution)/shard_map/ppermute | solution.py:79
  169.3 1.3 copy-start.4
  174.5 1.6 copy-start.2
  178.1 7.7 %collective-permute-start.7 = (bf16[8,128,1024]{2,1,0:T(8,128)(2,1)}, bf16[8,128,1024]{2,1,0:T(8,128)(2,1)}, u32[]{:S(2)}, u32[]{:S(2)}) collective-permute-start(bf16[8,128,1024]{2,1,0:T(8,128)(2,1)} %fusion.25), channel_id=1, source_target_pairs={{0,16},{16,0},{1,17},{17,1},{2,18},{18,2},{3,19},{19,3},{4,20},{20... | collective-permute-start | bytes 6291464 | tf_op jit(solution)/shard_map/ppermute | solution.py:117
  181.5 14.6 %all-to-all-start.3 = ((f32[4,2,128,128]{3,2,1,0:T(8,128)}), f32[4,2,128,128]{3,2,1,0:T(8,128)}, u32[]{:S(2)}, u32[]{:S(2)}) async-start(f32[4,2,128,128]{3,2,1,0:T(8,128)} %bitcast.69), calls=%async_computation.3 | async-start | bytes 1048576 | tf_op jit(solution)/shard_map/all_to_all | solution.py:99
  191.6 2.5 copy-start.3
  194.8 25.1 %copy-start.5 = (s32[8]{0:T(128)S(1)}, s32[8]{0:T(128)}, u32[]{:S(2)}) copy-start(s32[8]{0:T(128)} %param.9) | copy-start | bytes 100
  196.1 59.3 %all-to-all-start.1 = ((f32[16,8,8,128]{3,2,1,0:T(8,128)}), f32[16,8,8,128]{3,2,1,0:T(8,128)S(1)}, u32[]{:S(2)}, u32[]{:S(2)}) async-start(f32[16,8,8,128]{3,2,1,0:T(8,128)} %bitcast.64), calls=%async_computation.1 | async-start | bytes 1048576 | tf_op jit(solution)/shard_map/all_to_all | solution.py:129
  260.3 16.9 %all-to-all-start.2 = ((f32[8,8,128]{2,1,0:T(8,128)}), f32[8,8,128]{2,1,0:T(8,128)S(1)}, u32[]{:S(2)}, u32[]{:S(2)}) async-start(f32[8,8,128]{2,1,0:T(8,128)} %constant_dynamic-update-slice_fusion.8), calls=%async_computation.2 | async-start | bytes 65536 | tf_op jit(solution)/shard_map/all_to_all | solution.py:131
Sparse Core Ops, SparseCore 0:
  57.1 32.5 all-gather.3

commit v2 on v1

v2 whole, which is shorter than its diff:
```python
import math

import jax
import jax.numpy as jnp
from jax import lax
from jax.experimental import pallas as pl
from jax.experimental.pallas import tpu as pltpu
from jax.sharding import Mesh, PartitionSpec as P

RANK = 128
LEVELS = 4
SLOTS = 8
ROW = ("yh", "yl", "zh", "core")
COL = ("x", "zl")
PEERS = ("yl", "zh")
HIGHEST = lax.Precision.HIGHEST


def gram_kernel(panels_ref, out_ref):
    rows = lax.broadcasted_iota(jnp.int32, (RANK, RANK), 0)
    cols = lax.broadcasted_iota(jnp.int32, (RANK, RANK), 1)

    def gram(block):
        value = panels_ref[block * RANK : (block + 1) * RANK]
        return lax.dot_general(
            value, value, (((1,), (1,)), ((), ())), preferred_element_type=jnp.float32
        )

    for pair in range(out_ref.shape[0]):
        below, above = gram(2 * pair), gram(2 * pair + 1)
        out_ref[pair, :RANK] = jnp.where(rows >= cols, below, above)
        diagonal = jnp.sum(jnp.where(rows == cols, above, 0.0), axis=0, keepdims=True)
        out_ref[pair, RANK:] = jnp.broadcast_to(diagonal, (8, RANK))


def local_grams(panels):
    return pl.pallas_call(
        gram_kernel,
        out_shape=jax.ShapeDtypeStruct((SLOTS // 2, RANK + 8, RANK), jnp.float32),
        in_specs=[pl.BlockSpec(memory_space=pltpu.VMEM)],
        out_specs=pl.BlockSpec(memory_space=pltpu.VMEM),
        compiler_params=pltpu.CompilerParams(vmem_limit_bytes=32 * 2**20),
    )(panels)


def invert_kernel(place_ref, ranks_ref, packed_ref, out_ref):
    lane = lax.broadcasted_iota(jnp.int32, (8, RANK), 1)
    sub = lax.broadcasted_iota(jnp.int32, (8, RANK), 0)
    rows = lax.broadcasted_iota(jnp.int32, (RANK, RANK), 0)
    cols = lax.broadcasted_iota(jnp.int32, (RANK, RANK), 1)
    blocks = out_ref.shape[0]
    packed = packed_ref[0, :RANK]
    turned = packed.T
    above = jnp.where(rows < cols, packed, turned)
    grams = (
        jnp.where(rows >= cols, packed, turned),
        jnp.where(rows == cols, packed_ref[0, RANK : RANK + 1], above),
    )
    ranks = [ranks_ref[place_ref[0] * blocks + b] for b in range(blocks)]
    tiles = []
    for b in range(blocks):
        kept = (rows < ranks[b]) & (cols < ranks[b])
        gram = jnp.where(kept, grams[b], jnp.where(rows == cols, 1.0, 0.0))
        tiles.append([gram[8 * g : 8 * g + 8] for g in range(RANK // 8)])
    for k in range(RANK):
        first, at = k // 8, k % 8
        for b in range(blocks):
            tile = tiles[b]
            row = tile[first][at : at + 1, :]
            scaled = jnp.where(lane[:1] == k, 1.0, row) / row[:, k : k + 1]
            for g in range(first, RANK // 8):
                column = tile[g][:, k : k + 1]
                clear = lane == k
                if g == first:
                    column = jnp.where(sub[:, :1] > at, column, 0.0)
                    clear = clear & (sub > at)
                tile[g] = jnp.where(clear, 0.0, tile[g]) - column * scaled
    for b in range(blocks):
        done = jnp.concatenate(tiles[b], axis=0)
        pivots = jnp.sum(jnp.where(rows == cols, done, 0.0), axis=1, keepdims=True)
        lower = jnp.where(rows > cols, done, jnp.where(rows == cols, 1.0, 0.0))
        inverse = lax.dot_general(
            lower,
            lower / pivots,
            (((0,), (0,)), ((), ())),
            precision=HIGHEST,
            preferred_element_type=jnp.float32,
        )
        out_ref[b] = jnp.where(rows < ranks[b], inverse * (4.0 * math.sqrt(RANK)), 0.0)


def invert(place, block_ranks, packed):
    smem = pl.BlockSpec(memory_space=pltpu.SMEM)
    return pl.pallas_call(
        invert_kernel,
        out_shape=jax.ShapeDtypeStruct((2, RANK, RANK), jnp.float32),
        in_specs=[smem, smem, pl.BlockSpec(memory_space=pltpu.VMEM)],
        out_specs=pl.BlockSpec(memory_space=pltpu.VMEM),
        compiler_params=pltpu.CompilerParams(vmem_limit_bytes=32 * 2**20),
    )(place, block_ranks, packed)


def factor_of(factors_ref, place_ref, level, slot, flipped=False):
    factor = factors_ref[(level + 4 - place_ref[0]) % 4, slot]
    if flipped:
        factor = jnp.concatenate([factor[:, RANK:], factor[:, :RANK]], axis=1)
    return factor


def joint(factors_ref, place_ref, level, slot, other):
    return jnp.concatenate(
        [
            factor_of(factors_ref, place_ref, level, slot),
            factor_of(factors_ref, place_ref, level, other, True),
        ],
        axis=0,
    )


def matmul(left, right):
    return jnp.dot(left, right, preferred_element_type=jnp.float32)


def near_levels_kernel(place_ref, base_ref, factors_ref, *rest):
    out_ref, mid_ref = rest[-2:]
    columns = out_ref.shape[2]
    for source, target, level, bit in ((base_ref, mid_ref, 0, 1), (mid_ref, out_ref, 1, 4)):
        for slot in range(SLOTS):
            other = slot ^ bit
            if slot < other:
                rows = jnp.concatenate([source[slot, :, :columns], source[other, :, :columns]], axis=0)
                mixed = matmul(joint(factors_ref, place_ref, level, slot, other), rows)
                mixed = mixed.astype(jnp.bfloat16)
                target[slot] = mixed[:RANK]
                target[other] = mixed[RANK:]


def near_levels(place, base, factors, columns, *after):
    vmem = pl.BlockSpec(memory_space=pltpu.VMEM)
    smem = pl.BlockSpec(memory_space=pltpu.SMEM)
    shape = SLOTS, RANK, columns
    return pl.pallas_call(
        near_levels_kernel,
        out_shape=jax.ShapeDtypeStruct(shape, base.dtype),
        in_specs=[smem, vmem, vmem] + [pl.BlockSpec(memory_space=pl.ANY)] * len(after),
        out_specs=vmem,
        scratch_shapes=[pltpu.VMEM(shape, base.dtype)],
        compiler_params=pltpu.CompilerParams(vmem_limit_bytes=32 * 2**20),
    )(place, base, factors, *after)


def sums_of(place_ref, factors_ref, level_ref, paired_ref, base_ref, slot, other):
    def third(at):
        rows = jnp.concatenate([level_ref[at], paired_ref[at]], axis=0)
        return matmul(factor_of(factors_ref, place_ref, 2, at), rows).astype(jnp.bfloat16)

    columns = level_ref.shape[2]
    rows = jnp.concatenate([third(slot), third(other)], axis=0)
    bases = jnp.concatenate([base_ref[slot, :, :columns], base_ref[other, :, :columns]], axis=0)
    return lax.dot_general(
        rows, bases, (((1,), (1,)), ((), ())), preferred_element_type=jnp.float32
    )


PAIRS = tuple((slot, slot ^ 2) for slot in range(SLOTS) if slot < slot ^ 2)


def early_kernel(place_ref, factors_ref, level_ref, paired_ref, base_ref, out_ref):
    for at, (slot, other) in enumerate(PAIRS):
        out_ref[at] = sums_of(
            place_ref, factors_ref, level_ref, paired_ref, base_ref, slot, other
        )


def cross_kernel(place_ref, factors_ref, level_ref, paired_ref, base_ref, early_ref, out_ref):
    for at, (slot, other) in enumerate(PAIRS):
        sums = early_ref[at] + sums_of(
            place_ref, factors_ref, level_ref, paired_ref, base_ref, slot, other
        )
        parts = []
        for _ in range(3):
            part = sums.astype(jnp.bfloat16)
            parts.append(part)
            sums = sums - part.astype(jnp.float32)
        factor = (
            factor_of(factors_ref, place_ref, 3, slot),
            factor_of(factors_ref, place_ref, 3, other, True),
        )
        for side, block in enumerate((slot, other)):
            side_of = slice(side * RANK, (side + 1) * RANK)
            cross = sum(matmul(factor[side], part[:, side_of]) for part in parts[::-1])
            for x in range(4):
                for zl in range(4):
                    start = 8 * (4 * x + zl)
                    out_ref[x, block, zl] = cross[start : start + 8]


def sums_call(kernel, shape, place, *arrays):
    vmem = pl.BlockSpec(memory_space=pltpu.VMEM)
    return pl.pallas_call(
        kernel,
        out_shape=jax.ShapeDtypeStruct(shape, jnp.float32),
        in_specs=[pl.BlockSpec(memory_space=pltpu.SMEM)] + [vmem] * len(arrays),
        out_specs=vmem,
        compiler_params=pltpu.CompilerParams(vmem_limit_bytes=32 * 2**20),
    )(place, *arrays)


def nothing_kernel(*refs):
    del refs


def once_done(value, *others):
    return pl.pallas_call(
        nothing_kernel,
        out_shape=jax.ShapeDtypeStruct(value.shape, value.dtype),
        in_specs=[pl.BlockSpec(memory_space=pl.ANY)] * (1 + len(others)),
        out_specs=pl.BlockSpec(memory_space=pl.ANY),
        input_output_aliases={0: 0},
    )(value, *others)


def exchange(blocks, axes):
    return lax.all_to_all(blocks, axes, 0, 0, tiled=True)


def gather(block, axes):
    count = lax.axis_size(axes)
    return exchange(jnp.broadcast_to(block[None], (count,) + block.shape), axes)


def swap(block, axis, bit):
    return lax.ppermute(block, axis, [(i, i ^ bit) for i in range(lax.axis_size(axis))])


def along_x(block, *after):
    count = lax.axis_size("x")
    shift = lambda d: lax.ppermute(block, "x", [(i, (i - d) % count) for i in range(count)])
    own = once_done(block, *after) if after else block
    return jnp.stack([own] + [shift(d) for d in range(1, count)])


def part(blocks, at, count):
    return lax.dynamic_slice_in_dim(blocks, at * count, count, 0)


def grams(panels):
    x_at = lax.axis_index("x")
    packed = local_grams(panels)
    high, low = x_at // 2, x_at % 2
    packed = part(packed, high, 2) + swap(part(packed, 1 - high, 2), "x", 2)
    packed = part(packed, low, 1) + swap(part(packed, 1 - low, 1), "x", 1)
    return packed + swap(packed, "zl", 1) + (swap(packed, "zl", 2) + swap(packed, "zl", 3))


def to_every_x(inverse):
    x_at = lax.axis_index("x")
    every = along_x(inverse)
    order = [lax.dynamic_index_in_dim(every, (x + 4 - x_at) % 4, 0, False) for x in range(4)]
    return jnp.concatenate(order, axis=0)


def gather_halved(solved):
    top = jnp.max(jnp.abs(solved), axis=2)
    power = jnp.clip(jnp.floor(jnp.log2(jnp.maximum(top, 1e-36))), -120.0, 120.0)
    values = (solved * jnp.exp2(-power)[:, :, None]).astype(jnp.float16)
    powers = jnp.pad(power.astype(jnp.float16), ((0, 0), (0, RANK - power.shape[1])))
    sent = gather(jnp.concatenate([values, powers[None]], axis=0), COL)
    blocks = solved.shape[0]
    power = sent[:, blocks, :, : solved.shape[1]].astype(jnp.float32)
    values = sent[:, :blocks].astype(jnp.float32) * jnp.exp2(power)[:, :, :, None]
    return values.transpose(1, 0, 2, 3).reshape(-1, RANK)


def first_kernel(place_ref, mask_ref, panels_ref, own_ref, paired_ref, out_ref):
    columns = panels_ref.shape[1]
    for slot in range(SLOTS):
        rows = slice(slot * RANK, (slot + 1) * RANK)
        mask = mask_ref[place_ref[0], slot].astype(jnp.float32)
        out_ref[slot, :, :columns] = panels_ref[rows]
        out_ref[slot, :, columns : columns + RANK] = own_ref[0, rows]
        paired = paired_ref[0, rows].astype(jnp.float32) * mask
        out_ref[slot, :, columns + RANK :] = paired.astype(jnp.bfloat16)


def first_part(place, panels, self_factors, partner_factors, link_mask, columns):
    rows = panels.shape[0]
    level = pl.BlockSpec((1, rows, RANK), lambda i, place: (place[0], 0, 0))
    shape = SLOTS, RANK, columns + 2 * RANK
    return pl.pallas_call(
        first_kernel,
        out_shape=jax.ShapeDtypeStruct(shape, panels.dtype),
        grid_spec=pltpu.PrefetchScalarGridSpec(
            num_scalar_prefetch=1,
            grid=(1,),
            in_specs=[
                pl.BlockSpec(memory_space=pltpu.SMEM),
                pl.BlockSpec((rows, columns), lambda i, place: (0, 0)),
                level,
                level,
            ],
            out_specs=pl.BlockSpec(shape, lambda i, place: (0, 0, 0)),
        ),
        compiler_params=pltpu.CompilerParams(vmem_limit_bytes=60 * 2**20),
    )(place, link_mask, panels, self_factors, partner_factors)


def body(panels, self_factors, partner_factors, link_mask, block_ranks):
    columns = panels.shape[1]
    early = columns // 2
    late = columns - early
    own = panels.reshape(SLOTS, RANK, columns)
    place = lax.axis_index("x").astype(jnp.int32).reshape(1)

    first = first_part(place, panels, self_factors, partner_factors, link_mask, early)
    first = exchange(first, PEERS)
    gram = grams(panels)
    second = exchange(once_done(own[:, :, early:], first, gram), PEERS)
    inverse = invert(place, block_ranks, gram)
    factors = along_x(first[:, :, early:], inverse)
    inverse = to_every_x(inverse)

    level = near_levels(place, first, factors, early)
    paired = swap(level, "core", 1)
    sums = sums_call(
        early_kernel, (len(PAIRS), 2 * RANK, 2 * RANK), place, factors, level, paired, first
    )
    level = near_levels(place, second, factors, late, inverse, sums)
    paired = swap(level, "core", 1)
    cross = sums_call(
        cross_kernel, (4, SLOTS, 4, 8, RANK), place, factors, level, paired, second, sums
    )

    cross = exchange(cross.reshape(4, 4 * SLOTS, 8, RANK), "x").sum(0)
    cross = exchange(cross, PEERS + ("zl",)).reshape(SLOTS, 4, 8, RANK).sum(1)
    solved = jnp.einsum("jrk,jkm->jrm", cross, inverse, precision=HIGHEST)
    return gather_halved(solved)


def solution(mesh):
    split = Mesh(mesh.devices.reshape(2, 2, 4, 2, 4, 4), ROW + COL)
    return jax.shard_map(
        body,
        mesh=split,
        in_specs=(P(ROW, COL), P(None, ROW, None), P(None, ROW, None), P(None, ROW), P(ROW)),
        out_specs=P(ROW, None),
        check_vma=False,
    )
```

time: 305 us -> 233 us (0.76)
  waiting for transfers between devices: 91.9 us -> 64.7 us
  blocking collectives: 72.8 us -> 54.5 us
  matrix products: 15.9 us -> 0.6 us
  between operations: 13.7 us -> 0.46 us
  Pallas kernels: 11.1 us -> 22.4 us
  starting transfers between devices: 78.8 us -> 72.1 us
  local copies, waits for them, and re-layouts: 16.5 us -> 11.2 us
    all_gather x3 -> x0, blocking collectives: 53.7 us -> none  [the longest x1 22.9 us: body(): gram = lax.all_gather(gram, 'zl', axis=0).sum(0)]
    all_to_all x1 -> x3, blocking collectives: 19.1 us -> 54.5 us  [exchange(): return lax.all_to_all(blocks, axes, 0, 0, tiled=True)]
    all_to_all x4 -> x2, starting transfers between devices: 47.9 us -> 31.5 us  [exchange(): return lax.all_to_all(blocks, axes, 0, 0, tiled=True)]
    dot_general x7 -> x0, matrix products: 15.3 us -> none  [the longest x3 8.37 us: body(): jnp.einsum('hnf,hfe->hne', factors[depth], jnp.concatenate([level, paired...]
    all_to_all x4 -> x2, waiting for transfers between devices: 14.2 us -> 0.01 us  [exchange(): return lax.all_to_all(blocks, axes, 0, 0, tiled=True)]
    ppermute x8 -> x13, waiting for transfers between devices: 77.8 us -> 64.7 us  [the longest x7 50.8 us: swap(): lax.ppermute(block, axis, [(i, i ^ bit) for i in range(lax.axis_size(axis...]
    pallas_call x1 -> x9, Pallas kernels: 11.1 us -> 22.4 us  [the longest x1 11.7 us: invert(): pl.pallas_call(invert_kernel, out_shape=jax.ShapeDtypeStruct((2, RANK, RA...]
    ppermute x8 -> x13, starting transfers between devices: 30.9 us -> 40.6 us  [the longest x7 22.5 us: swap(): lax.ppermute(block, axis, [(i, i ^ bit) for i in range(lax.axis_size(axis...]
  transfers between devices with their start and end apart: 13 -> 15, of which waited for: 6 -> 9; matrix products, arithmetic and copies ran while one was open for 6% -> 3% of each run, Pallas kernels for 4% -> 7%
where the time goes in v2:
time: 233 us; the launch traced here: 231 us
  starting transfers between devices  72.1 us (31%)
  waiting for transfers between devices  64.7 us (28%)
  blocking collectives  54.5 us (23%)
  Pallas kernels  22.4 us (10%)
  local copies, waits for them, and re-layouts  11.2 us (5%)
  other arithmetic  5.53 us (2%)
    all_to_all x3, blocking collectives, exchange(): return lax.all_to_all(blocks, axes, 0, 0, tiled=True)  54.5 us
    ppermute x7, waiting for transfers between devices, swap(): lax.ppermute(block, axis, [(i, i ^ bit) for i in range(lax.axis_size(axis...  50.8 us
    all_to_all x2, starting transfers between devices, exchange(): return lax.all_to_all(blocks, axes, 0, 0, tiled=True)  31.5 us
    ppermute x7, starting transfers between devices, swap(): lax.ppermute(block, axis, [(i, i ^ bit) for i in range(lax.axis_size(axis...  22.5 us
    ppermute x6, starting transfers between devices, along_x(): lax.ppermute(block, 'x', [(i, (i - d) % count) for i in range(count)])  18.1 us
    ppermute x6, waiting for transfers between devices, along_x(): lax.ppermute(block, 'x', [(i, (i - d) % count) for i in range(count)])  13.9 us
    pallas_call x1, Pallas kernels, invert(): pl.pallas_call(invert_kernel, out_shape=jax.ShapeDtypeStruct((2, RANK, RA...  11.7 us
    unnamed x34, local copies, waits for them, and re-layouts  7.66 us
  transfers between devices with their start and end apart: 15, of which 9 were waited for; matrix products, arithmetic and copies ran while one was open for 3% of the time, Pallas kernels for 7%

profile of v2, /device:TPU:24, one launch (start us, length us, event | category | flops | bytes accessed | tf_op | source)
XLA Modules:
  0.0 231.5 jit_solution(10058285346111785048)
XLA Ops:
  0.0 2.7 %shard_map.55 = bf16[8,128,768]{2,1,0:T(8,128)(2,1)} custom-call(s32[1]{0:T(128)} %bitcast.place_ref, s32[4,8]{1,0:T(4,128)} %mask_ref.1, bf16[1024,1024]{1,0:T(8,128)(2,1)} %panels_ref.3, bf16[4,1024,128]{2,1,0:T(8,128)(2,1)} %own_ref.1, bf16[4,1024,128]{2,1,0:T(8,128)(2,1)} %paired_ref.1), custom_call_target="tpu_custom_call" | custom-call | tf_op jit(solution)/shard_map/pallas_call | solution.py:290
  2.7 16.5 %all-to-all-start = ((bf16[8,128,768]{2,1,0:T(8,128)(2,1)}), bf16[8,128,768]{2,1,0:T(8,128)(2,1)S(1)}, u32[]{:S(2)}, u32[]{:S(2)}) async-start(bf16[8,128,768]{2,1,0:T(8,128)(2,1)} %shard_map.55), calls=%async_computation | async-start | bytes 3145728 | tf_op jit(solution)/shard_map/all_to_all | solution.py:224
  21.6 4.9 %collective-permute-start = (f32[2,136,128]{2,1,0:T(8,128)S(1)}, f32[2,136,128]{2,1,0:T(8,128)S(1)}, u32[]{:S(2)}, u32[]{:S(2)}) collective-permute-start(f32[2,136,128]{2,1,0:T(8,128)S(1)} %constant_dynamic-slice_fusion.1), channel_id=1, source_target_pairs={{0,8},{4,12},{8,0},{12,4},{1,9},{5,13},{9,1},{13,5},{2,10},{6,14},... | collective-permute-start | bytes 417800 | tf_op jit(solution)/shard_map/ppermute | solution.py:233
  26.5 3.5 %collective-permute-done = f32[2,136,128]{2,1,0:T(8,128)S(1)} collective-permute-done((f32[2,136,128]{2,1,0:T(8,128)S(1)}, f32[2,136,128]{2,1,0:T(8,128)S(1)}, u32[]{:S(2)}, u32[]{:S(2)}) %collective-permute-start) | collective-permute-done | bytes 139296 | tf_op jit(solution)/shard_map/ppermute | solution.py:233
  30.1 3.4 %collective-permute-start.1 = (f32[1,136,128]{2,1,0:T(8,128)S(1)}, f32[1,136,128]{2,1,0:T(8,128)S(1)}, u32[]{:S(2)}, u32[]{:S(2)}) collective-permute-start(f32[1,136,128]{2,1,0:T(8,128)S(1)} %constant_dynamic-slice_fusion), channel_id=1, source_target_pairs={{0,4},{4,0},{8,12},{12,8},{1,5},{5,1},{9,13},{13,9},{2,6},{6,2},{1... | collective-permute-start | bytes 208904 | tf_op jit(solution)/shard_map/ppermute | solution.py:233
  33.5 2.8 %collective-permute-done.1 = f32[1,136,128]{2,1,0:T(8,128)S(1)} collective-permute-done((f32[1,136,128]{2,1,0:T(8,128)S(1)}, f32[1,136,128]{2,1,0:T(8,128)S(1)}, u32[]{:S(2)}, u32[]{:S(2)}) %collective-permute-start.1) | collective-permute-done | bytes 69664 | tf_op jit(solution)/shard_map/ppermute | solution.py:233
  36.3 2.9 %collective-permute-start.2 = (f32[1,136,128]{2,1,0:T(8,128)S(1)}, f32[1,136,128]{2,1,0:T(8,128)S(1)}, u32[]{:S(2)}, u32[]{:S(2)}) collective-permute-start(f32[1,136,128]{2,1,0:T(8,128)S(1)} %dynamic-slice_add_fusion.1), channel_id=1, source_target_pairs={{0,1},{1,0},{2,3},{3,2},{4,5},{5,4},{6,7},{7,6},{8,9},{9,8},{10,11... | collective-permute-start | bytes 208904 | tf_op jit(solution)/shard_map/ppermute | solution.py:233
  39.2 3.4 %collective-permute-start.3 = (f32[1,136,128]{2,1,0:T(8,128)S(1)}, f32[1,136,128]{2,1,0:T(8,128)S(1)}, u32[]{:S(2)}, u32[]{:S(2)}) collective-permute-start(f32[1,136,128]{2,1,0:T(8,128)S(1)} %dynamic-slice_add_fusion.1), channel_id=1, source_target_pairs={{0,2},{1,3},{2,0},{3,1},{4,6},{5,7},{6,4},{7,5},{8,10},{9,11},{10,... | collective-permute-start | bytes 208904 | tf_op jit(solution)/shard_map/ppermute | solution.py:233
  42.6 3.8 %collective-permute-start.4 = (f32[1,136,128]{2,1,0:T(8,128)S(1)}, f32[1,136,128]{2,1,0:T(8,128)S(1)}, u32[]{:S(2)}, u32[]{:S(2)}) collective-permute-start(f32[1,136,128]{2,1,0:T(8,128)S(1)} %dynamic-slice_add_fusion.1), channel_id=1, source_target_pairs={{0,3},{1,2},{2,1},{3,0},{4,7},{5,6},{6,5},{7,4},{8,11},{9,10},{10,... | collective-permute-start | bytes 208904 | tf_op jit(solution)/shard_map/ppermute | solution.py:233
  48.7 42.1 %collective-permute-done.2 = f32[1,136,128]{2,1,0:T(8,128)S(1)} collective-permute-done((f32[1,136,128]{2,1,0:T(8,128)S(1)}, f32[1,136,128]{2,1,0:T(8,128)S(1)}, u32[]{:S(2)}, u32[]{:S(2)}) %collective-permute-start.2) | collective-permute-done | bytes 69664 | tf_op jit(solution)/shard_map/ppermute | solution.py:233
  92.6 15.0 %all-to-all-start.1 = ((bf16[8,128,512]{2,1,0:T(8,128)(2,1)}), bf16[8,128,512]{2,1,0:T(8,128)(2,1)S(1)}, u32[]{:S(2)}, u32[]{:S(2)}) async-start(bf16[8,128,512]{2,1,0:T(8,128)(2,1)} %shard_map.59), calls=%async_computation.1 | async-start | bytes 2097152 | tf_op jit(solution)/shard_map/all_to_all | solution.py:224
  108.7 4.7 %collective-permute-start.5 = (bf16[8,128,256]{2,1,0:T(8,128)(2,1)S(1)}, bf16[8,128,256]{2,1,0:T(8,128)(2,1)S(1)}, u32[]{:S(2)}, u32[]{:S(2)}) collective-permute-start(bf16[8,128,256]{2,1,0:T(8,128)(2,1)S(1)} %slice.16.refs_0_), channel_id=1, source_target_pairs={{0,12},{4,0},{8,4},{12,8},{1,13},{5,1},{9,5},{13,9},{2,14},{6,2},{... | collective-permute-start | bytes 1572872 | tf_op jit(solution)/shard_map/ppermute | solution.py:238
  113.3 2.7 %collective-permute-start.6 = (bf16[8,128,256]{2,1,0:T(8,128)(2,1)S(1)}, bf16[8,128,256]{2,1,0:T(8,128)(2,1)S(1)}, u32[]{:S(2)}, u32[]{:S(2)}) collective-permute-start(bf16[8,128,256]{2,1,0:T(8,128)(2,1)S(1)} %slice.16.refs_0_), channel_id=1, source_target_pairs={{0,8},{4,12},{8,0},{12,4},{1,9},{5,13},{9,1},{13,5},{2,10},{6,14},... | collective-permute-start | bytes 1572872 | tf_op jit(solution)/shard_map/ppermute | solution.py:238
  116.1 2.8 %collective-permute-start.7 = (bf16[8,128,256]{2,1,0:T(8,128)(2,1)S(1)}, bf16[8,128,256]{2,1,0:T(8,128)(2,1)S(1)}, u32[]{:S(2)}, u32[]{:S(2)}) collective-permute-start(bf16[8,128,256]{2,1,0:T(8,128)(2,1)S(1)} %slice.16.refs_0_), channel_id=1, source_target_pairs={{0,4},{4,8},{8,12},{12,0},{1,5},{5,9},{9,13},{13,1},{2,6},{6,10},{... | collective-permute-start | bytes 1572872 | tf_op jit(solution)/shard_map/ppermute | solution.py:238
  118.9 11.7 %shard_map.57.refs_1_ = f32[2,128,128]{2,1,0:T(8,128)S(1)} custom-call(s32[1]{0:T(128)} %bitcast.place_ref, s32[8]{0:T(128)S(1)} %copy-done.10, f32[1,136,128]{2,1,0:T(8,128)S(1)} %copy-done.9), custom_call_target="tpu_custom_call" | custom-call | tf_op jit(solution)/shard_map/pallas_call | solution.py:94
  133.3 5.6 %collective-permute-done.7 = bf16[8,128,256]{2,1,0:T(8,128)(2,1)S(1)} collective-permute-done((bf16[8,128,256]{2,1,0:T(8,128)(2,1)S(1)}, bf16[8,128,256]{2,1,0:T(8,128)(2,1)S(1)}, u32[]{:S(2)}, u32[]{:S(2)}) %collective-permute-start.7) | collective-permute-done | bytes 524320 | tf_op jit(solution)/shard_map/ppermute | solution.py:238
  145.3 2.5 %collective-permute-start.8 = (f32[2,128,128]{2,1,0:T(8,128)S(1)}, f32[2,128,128]{2,1,0:T(8,128)S(1)}, u32[]{:S(2)}, u32[]{:S(2)}) collective-permute-start(f32[2,128,128]{2,1,0:T(8,128)S(1)} %copy-done.8), channel_id=1, source_target_pairs={{0,12},{4,0},{8,4},{12,8},{1,13},{5,1},{9,5},{13,9},{2,14},{6,2},{... | collective-permute-start | bytes 393224 | tf_op jit(solution)/shard_map/ppermute | solution.py:238
  147.9 2.7 %collective-permute-start.9 = (f32[2,128,128]{2,1,0:T(8,128)S(1)}, f32[2,128,128]{2,1,0:T(8,128)S(1)}, u32[]{:S(2)}, u32[]{:S(2)}) collective-permute-start(f32[2,128,128]{2,1,0:T(8,128)S(1)} %copy-done.8), channel_id=1, source_target_pairs={{0,8},{4,12},{8,0},{12,4},{1,9},{5,13},{9,1},{13,5},{2,10},{6,14},... | collective-permute-start | bytes 393224 | tf_op jit(solution)/shard_map/ppermute | solution.py:238
  150.6 2.7 %collective-permute-start.10 = (f32[2,128,128]{2,1,0:T(8,128)S(1)}, f32[2,128,128]{2,1,0:T(8,128)}, u32[]{:S(2)}, u32[]{:S(2)}) collective-permute-start(f32[2,128,128]{2,1,0:T(8,128)S(1)} %copy-done.8), channel_id=1, source_target_pairs={{0,4},{4,8},{8,12},{12,0},{1,5},{5,9},{9,13},{13,1},{2,6},{6,10},{... | collective-permute-start | bytes 393224 | tf_op jit(solution)/shard_map/ppermute | solution.py:238
  153.5 3.4 %collective-permute-done.9 = f32[2,128,128]{2,1,0:T(8,128)S(1)} collective-permute-done((f32[2,128,128]{2,1,0:T(8,128)S(1)}, f32[2,128,128]{2,1,0:T(8,128)S(1)}, u32[]{:S(2)}, u32[]{:S(2)}) %collective-permute-start.9) | collective-permute-done | bytes 131104 | tf_op jit(solution)/shard_map/ppermute | solution.py:238
  156.9 2.9 %collective-permute-done.10 = f32[2,128,128]{2,1,0:T(8,128)} collective-permute-done((f32[2,128,128]{2,1,0:T(8,128)S(1)}, f32[2,128,128]{2,1,0:T(8,128)}, u32[]{:S(2)}, u32[]{:S(2)}) %collective-permute-start.10) | collective-permute-done | bytes 131104 | tf_op jit(solution)/shard_map/ppermute | solution.py:238
  175.1 12.6 %all_to_all.25 = f32[4,32,8,128]{3,2,1,0:T(8,128)S(1)} all-to-all(f32[4,32,8,128]{3,2,1,0:T(8,128)S(1)} %bitcast.30), channel_id=1, replica_groups=mesh['yh'=2,'yl'=2,'zh'=4,'core'=2,'x'=4,'zl'=4] {'x'}, dimensions={0} | all-to-all | bytes 1048576 | tf_op jit(solution)/shard_map/all_to_all | solution.py:224
  187.7 29.4 %all_to_all.26 = f32[32,8,128]{2,1,0:T(8,128)S(1)} all-to-all(f32[32,8,128]{2,1,0:T(8,128)S(1)} %reduce_sum.18), channel_id=1, replica_groups=mesh['yh'=2,'yl'=2,'zh'=4,'core'=2,'x'=4,'zl'=4] {'yl','zh','zl'}, dimensions={0} | all-to-all | bytes 262144 | tf_op jit(solution)/shard_map/all_to_all | solution.py:224
  217.9 12.5 %all_to_all.27 = f16[16,9,8,128]{3,2,1,0:T(8,128)(2,1)S(1)} all-to-all(f16[16,9,8,128]{3,2,1,0:T(8,128)(2,1)S(1)} %broadcast_in_dim.5), channel_id=1, replica_groups=mesh['yh'=2,'yl'=2,'zh'=4,'core'=2,'x'=4,'zl'=4] {'x','zl'}, dimensions={0} | all-to-all | bytes 589824 | tf_op jit(solution)/shard_map/all_to_all | solution.py:224
  (74 shorter events, 33.9 us)
Async XLA Ops:
  2.7 88.7 %all-to-all-start = ((bf16[8,128,768]{2,1,0:T(8,128)(2,1)}), bf16[8,128,768]{2,1,0:T(8,128)(2,1)S(1)}, u32[]{:S(2)}, u32[]{:S(2)}) async-start(bf16[8,128,768]{2,1,0:T(8,128)(2,1)} %shard_map.55), calls=%async_computation | async-start | bytes 3145728 | tf_op jit(solution)/shard_map/all_to_all | solution.py:224
  21.6 8.5 %collective-permute-start = (f32[2,136,128]{2,1,0:T(8,128)S(1)}, f32[2,136,128]{2,1,0:T(8,128)S(1)}, u32[]{:S(2)}, u32[]{:S(2)}) collective-permute-start(f32[2,136,128]{2,1,0:T(8,128)S(1)} %constant_dynamic-slice_fusion.1), channel_id=1, source_target_pairs={{0,8},{4,12},{8,0},{12,4},{1,9},{5,13},{9,1},{13,5},{2,10},{6,14},... | collective-permute-start | bytes 417800 | tf_op jit(solution)/shard_map/ppermute | solution.py:233
  30.1 6.2 %collective-permute-start.1 = (f32[1,136,128]{2,1,0:T(8,128)S(1)}, f32[1,136,128]{2,1,0:T(8,128)S(1)}, u32[]{:S(2)}, u32[]{:S(2)}) collective-permute-start(f32[1,136,128]{2,1,0:T(8,128)S(1)} %constant_dynamic-slice_fusion), channel_id=1, source_target_pairs={{0,4},{4,0},{8,12},{12,8},{1,5},{5,1},{9,13},{13,9},{2,6},{6,2},{1... | collective-permute-start | bytes 208904 | tf_op jit(solution)/shard_map/ppermute | solution.py:233
  36.3 54.5 %collective-permute-start.2 = (f32[1,136,128]{2,1,0:T(8,128)S(1)}, f32[1,136,128]{2,1,0:T(8,128)S(1)}, u32[]{:S(2)}, u32[]{:S(2)}) collective-permute-start(f32[1,136,128]{2,1,0:T(8,128)S(1)} %dynamic-slice_add_fusion.1), channel_id=1, source_target_pairs={{0,1},{1,0},{2,3},{3,2},{4,5},{5,4},{6,7},{7,6},{8,9},{9,8},{10,11... | collective-permute-start | bytes 208904 | tf_op jit(solution)/shard_map/ppermute | solution.py:233
  39.2 51.5 %collective-permute-start.3 = (f32[1,136,128]{2,1,0:T(8,128)S(1)}, f32[1,136,128]{2,1,0:T(8,128)S(1)}, u32[]{:S(2)}, u32[]{:S(2)}) collective-permute-start(f32[1,136,128]{2,1,0:T(8,128)S(1)} %dynamic-slice_add_fusion.1), channel_id=1, source_target_pairs={{0,2},{1,3},{2,0},{3,1},{4,6},{5,7},{6,4},{7,5},{8,10},{9,11},{10,... | collective-permute-start | bytes 208904 | tf_op jit(solution)/shard_map/ppermute | solution.py:233
  42.6 48.1 %collective-permute-start.4 = (f32[1,136,128]{2,1,0:T(8,128)S(1)}, f32[1,136,128]{2,1,0:T(8,128)S(1)}, u32[]{:S(2)}, u32[]{:S(2)}) collective-permute-start(f32[1,136,128]{2,1,0:T(8,128)S(1)} %dynamic-slice_add_fusion.1), channel_id=1, source_target_pairs={{0,3},{1,2},{2,1},{3,0},{4,7},{5,6},{6,5},{7,4},{8,11},{9,10},{10,... | collective-permute-start | bytes 208904 | tf_op jit(solution)/shard_map/ppermute | solution.py:233
  92.6 26.3 %copy-start.9 = (f32[1,136,128]{2,1,0:T(8,128)S(1)}, f32[1,136,128]{2,1,0:T(8,128)}, u32[]{:S(2)}) copy-start(f32[1,136,128]{2,1,0:T(8,128)} %add_add_fusion.packed_ref.refs_2_) | copy-start | bytes 208900
  92.6 26.3 %copy-start.10 = (s32[8]{0:T(128)S(1)}, s32[8]{0:T(128)}, u32[]{:S(2)}) copy-start(s32[8]{0:T(128)} %ranks_ref.1) | copy-start | bytes 100
  92.6 72.6 %all-to-all-start.1 = ((bf16[8,128,512]{2,1,0:T(8,128)(2,1)}), bf16[8,128,512]{2,1,0:T(8,128)(2,1)S(1)}, u32[]{:S(2)}, u32[]{:S(2)}) async-start(bf16[8,128,512]{2,1,0:T(8,128)(2,1)} %shard_map.59), calls=%async_computation.1 | async-start | bytes 2097152 | tf_op jit(solution)/shard_map/all_to_all | solution.py:224
  108.7 30.2 %copy-start.11 = (bf16[8,128,256]{2,1,0:T(8,128)(2,1)}, bf16[8,128,256]{2,1,0:T(8,128)(2,1)S(1)}, u32[]{:S(2)}) copy-start(bf16[8,128,256]{2,1,0:T(8,128)(2,1)S(1)} %slice.16.refs_0_) | copy-start | bytes 1572868
  108.7 24.6 %collective-permute-start.5 = (bf16[8,128,256]{2,1,0:T(8,128)(2,1)S(1)}, bf16[8,128,256]{2,1,0:T(8,128)(2,1)S(1)}, u32[]{:S(2)}, u32[]{:S(2)}) collective-permute-start(bf16[8,128,256]{2,1,0:T(8,128)(2,1)S(1)} %slice.16.refs_0_), channel_id=1, source_target_pairs={{0,12},{4,0},{8,4},{12,8},{1,13},{5,1},{9,5},{13,9},{2,14},{6,2},{... | collective-permute-start | bytes 1572872 | tf_op jit(solution)/shard_map/ppermute | solution.py:238
  113.3 19.9 %collective-permute-start.6 = (bf16[8,128,256]{2,1,0:T(8,128)(2,1)S(1)}, bf16[8,128,256]{2,1,0:T(8,128)(2,1)S(1)}, u32[]{:S(2)}, u32[]{:S(2)}) collective-permute-start(bf16[8,128,256]{2,1,0:T(8,128)(2,1)S(1)} %slice.16.refs_0_), channel_id=1, source_target_pairs={{0,8},{4,12},{8,0},{12,4},{1,9},{5,13},{9,1},{13,5},{2,10},{6,14},... | collective-permute-start | bytes 1572872 | tf_op jit(solution)/shard_map/ppermute | solution.py:238
  116.1 22.8 %collective-permute-start.7 = (bf16[8,128,256]{2,1,0:T(8,128)(2,1)S(1)}, bf16[8,128,256]{2,1,0:T(8,128)(2,1)S(1)}, u32[]{:S(2)}, u32[]{:S(2)}) collective-permute-start(bf16[8,128,256]{2,1,0:T(8,128)(2,1)S(1)} %slice.16.refs_0_), channel_id=1, source_target_pairs={{0,4},{4,8},{8,12},{12,0},{1,5},{5,9},{9,13},{13,1},{2,6},{6,10},{... | collective-permute-start | bytes 1572872 | tf_op jit(solution)/shard_map/ppermute | solution.py:238
  133.3 5.6 %copy-start.12 = (bf16[8,128,256]{2,1,0:T(8,128)(2,1)}, bf16[8,128,256]{2,1,0:T(8,128)(2,1)S(1)}, u32[]{:S(2)}) copy-start(bf16[8,128,256]{2,1,0:T(8,128)(2,1)S(1)} %collective-permute-done.5) | copy-start | bytes 1572868
  133.3 5.6 %copy-start.13 = (bf16[8,128,256]{2,1,0:T(8,128)(2,1)}, bf16[8,128,256]{2,1,0:T(8,128)(2,1)S(1)}, u32[]{:S(2)}) copy-start(bf16[8,128,256]{2,1,0:T(8,128)(2,1)S(1)} %collective-permute-done.6) | copy-start | bytes 1572868
  139.6 2.0 copy-start.1
  141.7 3.7 %copy-start.8 = (f32[2,128,128]{2,1,0:T(8,128)S(1)}, f32[2,128,128]{2,1,0:T(8,128)}, u32[]{:S(2)}) copy-start(f32[2,128,128]{2,1,0:T(8,128)} %copy-done.7) | copy-start | bytes 393220
  143.4 18.3 %collective-permute-start.11 = (bf16[8,128,512]{2,1,0:T(8,128)(2,1)}, bf16[8,128,512]{2,1,0:T(8,128)(2,1)}, u32[]{:S(2)}, u32[]{:S(2)}) collective-permute-start(bf16[8,128,512]{2,1,0:T(8,128)(2,1)} %shard_map.60.level_ref), channel_id=1, source_target_pairs={{0,16},{16,0},{1,17},{17,1},{2,18},{18,2},{3,19},{19,3},{4,20},{20... | collective-permute-start | bytes 3145736 | tf_op jit(solution)/shard_map/ppermute | solution.py:233
  145.3 8.2 %collective-permute-start.8 = (f32[2,128,128]{2,1,0:T(8,128)S(1)}, f32[2,128,128]{2,1,0:T(8,128)S(1)}, u32[]{:S(2)}, u32[]{:S(2)}) collective-permute-start(f32[2,128,128]{2,1,0:T(8,128)S(1)} %copy-done.8), channel_id=1, source_target_pairs={{0,12},{4,0},{8,4},{12,8},{1,13},{5,1},{9,5},{13,9},{2,14},{6,2},{... | collective-permute-start | bytes 393224 | tf_op jit(solution)/shard_map/ppermute | solution.py:238
  147.9 9.1 %collective-permute-start.9 = (f32[2,128,128]{2,1,0:T(8,128)S(1)}, f32[2,128,128]{2,1,0:T(8,128)S(1)}, u32[]{:S(2)}, u32[]{:S(2)}) collective-permute-start(f32[2,128,128]{2,1,0:T(8,128)S(1)} %copy-done.8), channel_id=1, source_target_pairs={{0,8},{4,12},{8,0},{12,4},{1,9},{5,13},{9,1},{13,5},{2,10},{6,14},... | collective-permute-start | bytes 393224 | tf_op jit(solution)/shard_map/ppermute | solution.py:238
  150.6 9.2 %collective-permute-start.10 = (f32[2,128,128]{2,1,0:T(8,128)S(1)}, f32[2,128,128]{2,1,0:T(8,128)}, u32[]{:S(2)}, u32[]{:S(2)}) collective-permute-start(f32[2,128,128]{2,1,0:T(8,128)S(1)} %copy-done.8), channel_id=1, source_target_pairs={{0,4},{4,8},{8,12},{12,0},{1,5},{5,9},{9,13},{13,1},{2,6},{6,10},{... | collective-permute-start | bytes 393224 | tf_op jit(solution)/shard_map/ppermute | solution.py:238
  153.4 8.3 %copy-start.2 = (bf16[8,128,768]{2,1,0:T(8,128)(2,1)S(1)}, bf16[8,128,768]{2,1,0:T(8,128)(2,1)}, u32[]{:S(2)}) copy-start(bf16[8,128,768]{2,1,0:T(8,128)(2,1)} %copy-done) | copy-start | bytes 4718596
  168.2 4.6 %collective-permute-start.12 = (bf16[8,128,512]{2,1,0:T(8,128)(2,1)S(1)}, bf16[8,128,512]{2,1,0:T(8,128)(2,1)S(1)}, u32[]{:S(2)}, u32[]{:S(2)}) collective-permute-start(bf16[8,128,512]{2,1,0:T(8,128)(2,1)S(1)} %shard_map.62.level_ref), channel_id=1, source_target_pairs={{0,16},{16,0},{1,17},{17,1},{2,18},{18,2},{3,19},{19,3},{4,20},{20... | collective-permute-start | bytes 3145736 | tf_op jit(solution)/shard_map/ppermute | solution.py:233
  175.1 42.0 %copy-start.16 = (f32[2,128,128]{2,1,0:T(8,128)S(1)}, f32[2,128,128]{2,1,0:T(8,128)}, u32[]{:S(2)}) copy-start(f32[2,128,128]{2,1,0:T(8,128)} %copy-done.15) | copy-start | bytes 393220
  (8 other events, 8.4 us)

commit v3 on v2

--- a/solution.py
+++ b/solution.py
@@ -39,7 +39,7 @@
         out_shape=jax.ShapeDtypeStruct((SLOTS // 2, RANK + 8, RANK), jnp.float32),
         in_specs=[pl.BlockSpec(memory_space=pltpu.VMEM)],
         out_specs=pl.BlockSpec(memory_space=pltpu.VMEM),
-        compiler_params=pltpu.CompilerParams(vmem_limit_bytes=32 * 2**20),
+        compiler_params=pltpu.CompilerParams(vmem_limit_bytes=16 * 2**20),
     )(panels)
 
 
@@ -96,22 +96,22 @@
         out_shape=jax.ShapeDtypeStruct((2, RANK, RANK), jnp.float32),
         in_specs=[smem, smem, pl.BlockSpec(memory_space=pltpu.VMEM)],
         out_specs=pl.BlockSpec(memory_space=pltpu.VMEM),
-        compiler_params=pltpu.CompilerParams(vmem_limit_bytes=32 * 2**20),
+        compiler_params=pltpu.CompilerParams(vmem_limit_bytes=16 * 2**20),
     )(place, block_ranks, packed)
 
 
-def factor_of(factors_ref, place_ref, level, slot, flipped=False):
-    factor = factors_ref[(level + 4 - place_ref[0]) % 4, slot]
+def factor_of(factors_ref, level, slot, flipped=False):
+    factor = factors_ref[level % 2, slot]
     if flipped:
         factor = jnp.concatenate([factor[:, RANK:], factor[:, :RANK]], axis=1)
     return factor
 
 
-def joint(factors_ref, place_ref, level, slot, other):
+def joint(factors_ref, level, slot, other):
     return jnp.concatenate(
         [
-            factor_of(factors_ref, place_ref, level, slot),
-            factor_of(factors_ref, place_ref, level, other, True),
+            factor_of(factors_ref, level, slot),
+            factor_of(factors_ref, level, other, True),
         ],
         axis=0,
     )
@@ -121,7 +121,7 @@
     return jnp.dot(left, right, preferred_element_type=jnp.float32)
 
 
-def near_levels_kernel(place_ref, base_ref, factors_ref, *rest):
+def near_levels_kernel(base_ref, factors_ref, *rest):
     out_ref, mid_ref = rest[-2:]
     columns = out_ref.shape[2]
     for source, target, level, bit in ((base_ref, mid_ref, 0, 1), (mid_ref, out_ref, 1, 4)):
@@ -129,30 +129,29 @@
             other = slot ^ bit
             if slot < other:
                 rows = jnp.concatenate([source[slot, :, :columns], source[other, :, :columns]], axis=0)
-                mixed = matmul(joint(factors_ref, place_ref, level, slot, other), rows)
+                mixed = matmul(joint(factors_ref, level, slot, other), rows)
                 mixed = mixed.astype(jnp.bfloat16)
                 target[slot] = mixed[:RANK]
                 target[other] = mixed[RANK:]
 
 
-def near_levels(place, base, factors, columns, *after):
+def near_levels(base, factors, columns, *after):
     vmem = pl.BlockSpec(memory_space=pltpu.VMEM)
-    smem = pl.BlockSpec(memory_space=pltpu.SMEM)
     shape = SLOTS, RANK, columns
     return pl.pallas_call(
         near_levels_kernel,
         out_shape=jax.ShapeDtypeStruct(shape, base.dtype),
-        in_specs=[smem, vmem, vmem] + [pl.BlockSpec(memory_space=pl.ANY)] * len(after),
+        in_specs=[vmem, vmem] + [pl.BlockSpec(memory_space=pl.ANY)] * len(after),
         out_specs=vmem,
         scratch_shapes=[pltpu.VMEM(shape, base.dtype)],
-        compiler_params=pltpu.CompilerParams(vmem_limit_bytes=32 * 2**20),
-    )(place, base, factors, *after)
-
-
-def sums_of(place_ref, factors_ref, level_ref, paired_ref, base_ref, slot, other):
+        compiler_params=pltpu.CompilerParams(vmem_limit_bytes=16 * 2**20),
+    )(base, factors, *[corner(other) for other in after])
+
+
+def sums_of(factors_ref, level_ref, paired_ref, base_ref, slot, other):
     def third(at):
         rows = jnp.concatenate([level_ref[at], paired_ref[at]], axis=0)
-        return matmul(factor_of(factors_ref, place_ref, 2, at), rows).astype(jnp.bfloat16)
+        return matmul(factor_of(factors_ref, 2, at), rows).astype(jnp.bfloat16)
 
     columns = level_ref.shape[2]
     rows = jnp.concatenate([third(slot), third(other)], axis=0)
@@ -165,17 +164,17 @@
 PAIRS = tuple((slot, slot ^ 2) for slot in range(SLOTS) if slot < slot ^ 2)
 
 
-def early_kernel(place_ref, factors_ref, level_ref, paired_ref, base_ref, out_ref):
+def early_kernel(factors_ref, level_ref, paired_ref, base_ref, out_ref):
     for at, (slot, other) in enumerate(PAIRS):
         out_ref[at] = sums_of(
-            place_ref, factors_ref, level_ref, paired_ref, base_ref, slot, other
-        )
-
-
-def cross_kernel(place_ref, factors_ref, level_ref, paired_ref, base_ref, early_ref, out_ref):
+            factors_ref, level_ref, paired_ref, base_ref, slot, other
+        )
+
+
+def cross_kernel(factors_ref, level_ref, paired_ref, base_ref, early_ref, out_ref):
     for at, (slot, other) in enumerate(PAIRS):
         sums = early_ref[at] + sums_of(
-            place_ref, factors_ref, level_ref, paired_ref, base_ref, slot, other
+            factors_ref, level_ref, paired_ref, base_ref, slot, other
         )
         parts = []
         for _ in range(3):
@@ -183,8 +182,8 @@
             parts.append(part)
             sums = sums - part.astype(jnp.float32)
         factor = (
-            factor_of(factors_ref, place_ref, 3, slot),
-            factor_of(factors_ref, place_ref, 3, other, True),
+            factor_of(factors_ref, 3, slot),
+            factor_of(factors_ref, 3, other, True),
         )
         for side, block in enumerate((slot, other)):
             side_of = slice(side * RANK, (side + 1) * RANK)
@@ -192,25 +191,31 @@
             for x in range(4):
                 for zl in range(4):
                     start = 8 * (4 * x + zl)
-                    out_ref[x, block, zl] = cross[start : start + 8]
-
-
-def sums_call(kernel, shape, place, *arrays):
+                    out_ref[block // 4, x, block % 4, zl] = cross[start : start + 8]
+
+
+def sums_call(kernel, shape, *arrays):
     vmem = pl.BlockSpec(memory_space=pltpu.VMEM)
     return pl.pallas_call(
         kernel,
         out_shape=jax.ShapeDtypeStruct(shape, jnp.float32),
-        in_specs=[pl.BlockSpec(memory_space=pltpu.SMEM)] + [vmem] * len(arrays),
+        in_specs=[vmem] * len(arrays),
         out_specs=vmem,
-        compiler_params=pltpu.CompilerParams(vmem_limit_bytes=32 * 2**20),
-    )(place, *arrays)
+        compiler_params=pltpu.CompilerParams(vmem_limit_bytes=16 * 2**20),
+    )(*arrays)
 
 
 def nothing_kernel(*refs):
     del refs
 
 
+def corner(value):
+    value = value.reshape(-1, *value.shape[-2:])
+    return value[0, :16, :RANK]
+
+
 def once_done(value, *others):
+    others = [corner(other) for other in others]
     return pl.pallas_call(
         nothing_kernel,
         out_shape=jax.ShapeDtypeStruct(value.shape, value.dtype),
@@ -253,11 +258,9 @@
     return packed + swap(packed, "zl", 1) + (swap(packed, "zl", 2) + swap(packed, "zl", 3))
 
 
-def to_every_x(inverse):
+def by_place(every):
     x_at = lax.axis_index("x")
-    every = along_x(inverse)
-    order = [lax.dynamic_index_in_dim(every, (x + 4 - x_at) % 4, 0, False) for x in range(4)]
-    return jnp.concatenate(order, axis=0)
+    return [lax.dynamic_index_in_dim(every, (x + 4 - x_at) % 4, 0, False) for x in range(4)]
 
 
 def gather_halved(solved):
@@ -307,7 +310,7 @@
 
 def body(panels, self_factors, partner_factors, link_mask, block_ranks):
     columns = panels.shape[1]
-    early = columns // 2
+    early = columns * 3 // 8
     late = columns - early
     own = panels.reshape(SLOTS, RANK, columns)
     place = lax.axis_index("x").astype(jnp.int32).reshape(1)
@@ -318,21 +321,25 @@
     second = exchange(once_done(own[:, :, early:], first, gram), PEERS)
     inverse = invert(place, block_ranks, gram)
     factors = along_x(first[:, :, early:], inverse)
-    inverse = to_every_x(inverse)
-
-    level = near_levels(place, first, factors, early)
+    inverse = along_x(once_done(inverse, factors))
+    factors = by_place(factors)
+    lower, upper = jnp.stack(factors[:2]), jnp.stack(factors[2:])
+
+    level = near_levels(first, lower, early)
     paired = swap(level, "core", 1)
-    sums = sums_call(
-        early_kernel, (len(PAIRS), 2 * RANK, 2 * RANK), place, factors, level, paired, first
-    )
-    level = near_levels(place, second, factors, late, inverse, sums)
+    shape = len(PAIRS), 2 * RANK, 2 * RANK
+    sums = sums_call(early_kernel, shape, upper, level, paired, first)
+    level = near_levels(second, lower, late, sums, inverse)
     paired = swap(level, "core", 1)
-    cross = sums_call(
-        cross_kernel, (4, SLOTS, 4, 8, RANK), place, factors, level, paired, second, sums
-    )
-
-    cross = exchange(cross.reshape(4, 4 * SLOTS, 8, RANK), "x").sum(0)
-    cross = exchange(cross, PEERS + ("zl",)).reshape(SLOTS, 4, 8, RANK).sum(1)
+    shape = 2, 4, 4, 4, 8, RANK
+    cross = sums_call(cross_kernel, shape, upper, level, paired, second, sums)
+
+    cross = exchange(cross.reshape(2 * 4, 16, 8, RANK), ("yl", "x"))
+    cross = cross.reshape(2, 4, 16, 8, RANK).sum(1)
+    cross = exchange(cross.transpose(1, 0, 2, 3), ("zh", "zl"))
+    cross = cross.reshape(4, 4, 2, 8, RANK).sum(1)
+    cross = cross.transpose(1, 0, 2, 3).reshape(SLOTS, 8, RANK)
+    inverse = jnp.concatenate(by_place(inverse), axis=0)
     solved = jnp.einsum("jrk,jkm->jrm", cross, inverse, precision=HIGHEST)
     return gather_halved(solved)
 

time: 233 us -> 221 us (0.948)
  blocking collectives: 54.5 us -> 28.2 us
  starting transfers between devices: 72.1 us -> 83.4 us
    all_to_all x3 -> x2, blocking collectives: 54.5 us -> 28.2 us  [exchange(): return lax.all_to_all(blocks, axes, 0, 0, tiled=True)]
    all_to_all x2 -> x3, waiting for transfers between devices: 0.01 us -> 17.7 us  [exchange(): return lax.all_to_all(blocks, axes, 0, 0, tiled=True)]
    ppermute x7, waiting for transfers between devices: 50.8 us -> 40.5 us  [swap(): lax.ppermute(block, axis, [(i, i ^ bit) for i in range(lax.axis_size(axis...]
    all_to_all x2 -> x3, starting transfers between devices: 31.5 us -> 38.1 us  [exchange(): return lax.all_to_all(blocks, axes, 0, 0, tiled=True)]
    ppermute x6, waiting for transfers between devices: 13.9 us -> 8.54 us  [along_x(): lax.ppermute(block, 'x', [(i, (i - d) % count) for i in range(count)])]
    ppermute x6, starting transfers between devices: 18.1 us -> 22.9 us  [along_x(): lax.ppermute(block, 'x', [(i, (i - d) % count) for i in range(count)])]
    unnamed x34 -> x28, local copies, waits for them, and re-layouts: 7.66 us -> 4.72 us
    squeeze x1 -> x7, local copies, waits for them, and re-layouts: 0.05 us -> 2.46 us  [the longest x6 2.42 us: corner(): return value[0, :16, :RANK]]
  transfers between devices with their start and end apart: 15 -> 16, of which waited for: 9 -> 11; matrix products, arithmetic and copies ran while one was open for 3% -> 5% of each run, Pallas kernels for 7% -> 7%
where the time goes in v3:
time: 221 us; the launch traced here: 219 us
  starting transfers between devices  83.4 us (38%)
  waiting for transfers between devices  66.7 us (30%)
  blocking collectives  28.2 us (13%)
  Pallas kernels  21.6 us (10%)
  local copies, waits for them, and re-layouts  11.9 us (5%)
  other arithmetic  6.26 us (3%)
    ppermute x7, waiting for transfers between devices, swap(): lax.ppermute(block, axis, [(i, i ^ bit) for i in range(lax.axis_size(axis...  40.5 us
    all_to_all x3, starting transfers between devices, exchange(): return lax.all_to_all(blocks, axes, 0, 0, tiled=True)  38.1 us
    all_to_all x2, blocking collectives, exchange(): return lax.all_to_all(blocks, axes, 0, 0, tiled=True)  28.2 us
    ppermute x6, starting transfers between devices, along_x(): lax.ppermute(block, 'x', [(i, (i - d) % count) for i in range(count)])  22.9 us
    ppermute x7, starting transfers between devices, swap(): lax.ppermute(block, axis, [(i, i ^ bit) for i in range(lax.axis_size(axis...  22.4 us
    all_to_all x3, waiting for transfers between devices, exchange(): return lax.all_to_all(blocks, axes, 0, 0, tiled=True)  17.7 us
    pallas_call x1, Pallas kernels, invert(): pl.pallas_call(invert_kernel, out_shape=jax.ShapeDtypeStruct((2, RANK, RA...  11.7 us
    ppermute x6, waiting for transfers between devices, along_x(): lax.ppermute(block, 'x', [(i, (i - d) % count) for i in range(count)])  8.54 us
  transfers between devices with their start and end apart: 16, of which 11 were waited for; matrix products, arithmetic and copies ran while one was open for 5% of the time, Pallas kernels for 7%

profile of v3, /device:TPU:24, one launch (start us, length us, event | category | flops | bytes accessed | tf_op | source)
XLA Modules:
  0.0 219.2 jit_solution(7718956277409687312)
XLA Ops:
  2.5 16.7 %all-to-all-start = ((bf16[8,128,640]{2,1,0:T(8,128)(2,1)}), bf16[8,128,640]{2,1,0:T(8,128)(2,1)S(1)}, u32[]{:S(2)}, u32[]{:S(2)}) async-start(bf16[8,128,640]{2,1,0:T(8,128)(2,1)} %shard_map.55), calls=%async_computation | async-start | bytes 2621440 | tf_op jit(solution)/shard_map/all_to_all | solution.py:229
  21.5 4.9 %collective-permute-start = (f32[2,136,128]{2,1,0:T(8,128)S(1)}, f32[2,136,128]{2,1,0:T(8,128)}, u32[]{:S(2)}, u32[]{:S(2)}) collective-permute-start(f32[2,136,128]{2,1,0:T(8,128)S(1)} %constant_dynamic-slice_fusion.5), channel_id=1, source_target_pairs={{0,8},{4,12},{8,0},{12,4},{1,9},{5,13},{9,1},{13,5},{2,10},{6,14},... | collective-permute-start | bytes 417800 | tf_op jit(solution)/shard_map/ppermute | solution.py:238
  26.5 3.6 %collective-permute-done = f32[2,136,128]{2,1,0:T(8,128)} collective-permute-done((f32[2,136,128]{2,1,0:T(8,128)S(1)}, f32[2,136,128]{2,1,0:T(8,128)}, u32[]{:S(2)}, u32[]{:S(2)}) %collective-permute-start) | collective-permute-done | bytes 139296 | tf_op jit(solution)/shard_map/ppermute | solution.py:238
  31.7 3.4 %collective-permute-start.1 = (f32[1,136,128]{2,1,0:T(8,128)}, f32[1,136,128]{2,1,0:T(8,128)}, u32[]{:S(2)}, u32[]{:S(2)}) collective-permute-start(f32[1,136,128]{2,1,0:T(8,128)} %constant_dynamic-slice_fusion.4), channel_id=1, source_target_pairs={{0,4},{4,0},{8,12},{12,8},{1,5},{5,1},{9,13},{13,9},{2,6},{6,2},{1... | collective-permute-start | bytes 208904 | tf_op jit(solution)/shard_map/ppermute | solution.py:238
  35.1 3.1 %collective-permute-done.1 = f32[1,136,128]{2,1,0:T(8,128)} collective-permute-done((f32[1,136,128]{2,1,0:T(8,128)}, f32[1,136,128]{2,1,0:T(8,128)}, u32[]{:S(2)}, u32[]{:S(2)}) %collective-permute-start.1) | collective-permute-done | bytes 69664 | tf_op jit(solution)/shard_map/ppermute | solution.py:238
  39.1 3.8 %collective-permute-start.4 = (f32[1,136,128]{2,1,0:T(8,128)S(1)}, f32[1,136,128]{2,1,0:T(8,128)S(1)}, u32[]{:S(2)}, u32[]{:S(2)}) collective-permute-start(f32[1,136,128]{2,1,0:T(8,128)S(1)} %dynamic-slice_add_fusion.1), channel_id=1, source_target_pairs={{0,3},{1,2},{2,1},{3,0},{4,7},{5,6},{6,5},{7,4},{8,11},{9,10},{10,... | collective-permute-start | bytes 208904 | tf_op jit(solution)/shard_map/ppermute | solution.py:238
  45.5 3.8 %collective-permute-start.2 = (f32[1,136,128]{2,1,0:T(8,128)S(1)}, f32[1,136,128]{2,1,0:T(8,128)S(1)}, u32[]{:S(2)}, u32[]{:S(2)}) collective-permute-start(f32[1,136,128]{2,1,0:T(8,128)S(1)} %dynamic-slice_add_fusion.1), channel_id=1, source_target_pairs={{0,1},{1,0},{2,3},{3,2},{4,5},{5,4},{6,7},{7,6},{8,9},{9,8},{10,11... | collective-permute-start | bytes 208904 | tf_op jit(solution)/shard_map/ppermute | solution.py:238
  50.5 14.2 %collective-permute-done.4 = f32[1,136,128]{2,1,0:T(8,128)S(1)} collective-permute-done((f32[1,136,128]{2,1,0:T(8,128)S(1)}, f32[1,136,128]{2,1,0:T(8,128)S(1)}, u32[]{:S(2)}, u32[]{:S(2)}) %collective-permute-start.4) | collective-permute-done | bytes 69664 | tf_op jit(solution)/shard_map/ppermute | solution.py:238
  64.7 16.8 %collective-permute-done.3 = f32[1,136,128]{2,1,0:T(8,128)S(1)} collective-permute-done((f32[1,136,128]{2,1,0:T(8,128)S(1)}, f32[1,136,128]{2,1,0:T(8,128)S(1)}, u32[]{:S(2)}, u32[]{:S(2)}) %collective-permute-start.3) | collective-permute-done | bytes 69664 | tf_op jit(solution)/shard_map/ppermute | solution.py:238
  82.7 13.8 %all-to-all-start.1 = ((bf16[8,128,640]{2,1,0:T(8,128)(2,1)}), bf16[8,128,640]{2,1,0:T(8,128)(2,1)S(1)}, u32[]{:S(2)}, u32[]{:S(2)}) async-start(bf16[8,128,640]{2,1,0:T(8,128)(2,1)} %shard_map.59), calls=%async_computation.1 | async-start | bytes 2621440 | tf_op jit(solution)/shard_map/all_to_all | solution.py:229
  96.5 3.4 %collective-permute-start.7 = (bf16[8,128,256]{2,1,0:T(8,128)(2,1)S(1)}, bf16[8,128,256]{2,1,0:T(8,128)(2,1)}, u32[]{:S(2)}, u32[]{:S(2)}) collective-permute-start(bf16[8,128,256]{2,1,0:T(8,128)(2,1)S(1)} %slice.40.refs_0_), channel_id=1, source_target_pairs={{0,4},{4,8},{8,12},{12,0},{1,5},{5,9},{9,13},{13,1},{2,6},{6,10},{... | collective-permute-start | bytes 1572872 | tf_op jit(solution)/shard_map/ppermute | solution.py:243
  100.0 4.6 %collective-permute-start.6 = (bf16[8,128,256]{2,1,0:T(8,128)(2,1)S(1)}, bf16[8,128,256]{2,1,0:T(8,128)(2,1)}, u32[]{:S(2)}, u32[]{:S(2)}) collective-permute-start(bf16[8,128,256]{2,1,0:T(8,128)(2,1)S(1)} %slice.40.refs_0_), channel_id=1, source_target_pairs={{0,8},{4,12},{8,0},{12,4},{1,9},{5,13},{9,1},{13,5},{2,10},{6,14},... | collective-permute-start | bytes 1572872 | tf_op jit(solution)/shard_map/ppermute | solution.py:243
  104.6 3.3 %collective-permute-start.5 = (bf16[8,128,256]{2,1,0:T(8,128)(2,1)S(1)}, bf16[8,128,256]{2,1,0:T(8,128)(2,1)}, u32[]{:S(2)}, u32[]{:S(2)}) collective-permute-start(bf16[8,128,256]{2,1,0:T(8,128)(2,1)S(1)} %slice.40.refs_0_), channel_id=1, source_target_pairs={{0,12},{4,0},{8,4},{12,8},{1,13},{5,1},{9,5},{13,9},{2,14},{6,2},{... | collective-permute-start | bytes 1572872 | tf_op jit(solution)/shard_map/ppermute | solution.py:243
  108.0 11.7 %shard_map.57.refs_0_ = f32[2,128,128]{2,1,0:T(8,128)S(1)} custom-call(s32[1]{0:T(128)} %bitcast.place_ref, s32[8]{0:T(128)S(1)} %copy-done.10, f32[1,136,128]{2,1,0:T(8,128)S(1)} %add_add_fusion.packed_ref), custom_call_target="tpu_custom_call" | custom-call | tf_op jit(solution)/shard_map/pallas_call | solution.py:94
  120.4 4.3 %collective-permute-done.6 = bf16[8,128,256]{2,1,0:T(8,128)(2,1)} collective-permute-done((bf16[8,128,256]{2,1,0:T(8,128)(2,1)S(1)}, bf16[8,128,256]{2,1,0:T(8,128)(2,1)}, u32[]{:S(2)}, u32[]{:S(2)}) %collective-permute-start.6) | collective-permute-done | bytes 524320 | tf_op jit(solution)/shard_map/ppermute | solution.py:243
  133.6 4.4 %collective-permute-start.11 = (f32[2,128,128]{2,1,0:T(8,128)}, f32[2,128,128]{2,1,0:T(8,128)S(1)}, u32[]{:S(2)}, u32[]{:S(2)}) collective-permute-start(f32[2,128,128]{2,1,0:T(8,128)} %shard_map.62), channel_id=1, source_target_pairs={{0,4},{4,8},{8,12},{12,0},{1,5},{5,9},{9,13},{13,1},{2,6},{6,10},{... | collective-permute-start | bytes 393224 | tf_op jit(solution)/shard_map/ppermute | solution.py:243
  138.0 3.6 %collective-permute-start.10 = (f32[2,128,128]{2,1,0:T(8,128)}, f32[2,128,128]{2,1,0:T(8,128)S(1)}, u32[]{:S(2)}, u32[]{:S(2)}) collective-permute-start(f32[2,128,128]{2,1,0:T(8,128)} %shard_map.62), channel_id=1, source_target_pairs={{0,8},{4,12},{8,0},{12,4},{1,9},{5,13},{9,1},{13,5},{2,10},{6,14},... | collective-permute-start | bytes 393224 | tf_op jit(solution)/shard_map/ppermute | solution.py:243
  141.7 3.5 %collective-permute-start.9 = (f32[2,128,128]{2,1,0:T(8,128)}, f32[2,128,128]{2,1,0:T(8,128)S(1)}, u32[]{:S(2)}, u32[]{:S(2)}) collective-permute-start(f32[2,128,128]{2,1,0:T(8,128)} %shard_map.62), channel_id=1, source_target_pairs={{0,12},{4,0},{8,4},{12,8},{1,13},{5,1},{9,5},{13,9},{2,14},{6,2},{... | collective-permute-start | bytes 393224 | tf_op jit(solution)/shard_map/ppermute | solution.py:243
  153.0 3.7 %all-to-all-done.1.base_ref = bf16[8,128,640]{2,1,0:T(8,128)(2,1)S(1)} async-done(((bf16[8,128,640]{2,1,0:T(8,128)(2,1)}), bf16[8,128,640]{2,1,0:T(8,128)(2,1)S(1)}, u32[]{:S(2)}, u32[]{:S(2)}) %all-to-all-start.1) | async-done | bytes 1310752 | tf_op jit(solution)/shard_map/all_to_all | solution.py:229
  163.8 2.9 %shard_map.64 = f32[2,4,4,4,8,128]{5,4,3,2,1,0:T(8,128)S(1)} custom-call(bf16[2,8,128,256]{3,2,1,0:T(8,128)(2,1)S(1)} %copy-done.4, bf16[8,128,640]{2,1,0:T(8,128)(2,1)S(1)} %shard_map.63.level_ref, bf16[8,128,640]{2,1,0:T(8,128)(2,1)S(1)} %collective-permute-done.12.paired_ref, bf16[8,128,640]{2,1,0:T(8,128)(2,1)S(1)} %all-to-all-done.1.base_ref, ...), custom_call_target="tpu_custom_call" | custom-call | tf_op jit(solution)/shard_map/pallas_call | solution.py:199
  166.7 14.6 %all_to_all.25 = f32[8,16,8,128]{3,2,1,0:T(8,128)S(1)} all-to-all(f32[8,16,8,128]{3,2,1,0:T(8,128)S(1)} %bitcast.49), channel_id=1, replica_groups=mesh['yh'=2,'yl'=2,'zh'=4,'core'=2,'x'=4,'zl'=4] {'yl','x'}, dimensions={0} | all-to-all | bytes 1048576 | tf_op jit(solution)/shard_map/all_to_all | solution.py:229
  182.0 7.6 %all-to-all-start.3 = ((f32[16,2,8,128]{3,2,1,0:T(8,128)}), f32[16,2,8,128]{3,2,1,0:T(8,128)S(1)}, u32[]{:S(2)}, u32[]{:S(2)}) async-start(f32[16,2,8,128]{3,2,1,0:T(8,128)} %copy.15), calls=%async_computation.3 | async-start | bytes 262144 | tf_op jit(solution)/shard_map/all_to_all | solution.py:229
  189.7 14.0 %all-to-all-done.3 = f32[16,2,8,128]{3,2,1,0:T(8,128)S(1)} async-done(((f32[16,2,8,128]{3,2,1,0:T(8,128)}), f32[16,2,8,128]{3,2,1,0:T(8,128)S(1)}, u32[]{:S(2)}, u32[]{:S(2)}) %all-to-all-start.3) | async-done | bytes 131104 | tf_op jit(solution)/shard_map/all_to_all | solution.py:229
  204.6 13.6 %all_to_all.26 = f16[16,9,8,128]{3,2,1,0:T(8,128)(2,1)S(1)} all-to-all(f16[16,9,8,128]{3,2,1,0:T(8,128)(2,1)S(1)} %broadcast_in_dim.5), channel_id=1, replica_groups=mesh['yh'=2,'yl'=2,'zh'=4,'core'=2,'x'=4,'zl'=4] {'x','zl'}, dimensions={0} | all-to-all | bytes 589824 | tf_op jit(solution)/shard_map/all_to_all | solution.py:229
  (80 shorter events, 39.2 us)
Async XLA Ops:
  2.5 16.7 %copy-start = (bf16[1024,1024]{1,0:T(8,128)(2,1)S(1)}, bf16[1024,1024]{1,0:T(8,128)(2,1)}, u32[]{:S(2)}) copy-start(bf16[1024,1024]{1,0:T(8,128)(2,1)} %panels_ref.3) | copy-start | bytes 6291460
  2.5 79.6 %all-to-all-start = ((bf16[8,128,640]{2,1,0:T(8,128)(2,1)}), bf16[8,128,640]{2,1,0:T(8,128)(2,1)S(1)}, u32[]{:S(2)}, u32[]{:S(2)}) async-start(bf16[8,128,640]{2,1,0:T(8,128)(2,1)} %shard_map.55), calls=%async_computation | async-start | bytes 2621440 | tf_op jit(solution)/shard_map/all_to_all | solution.py:229
  21.5 8.6 %collective-permute-start = (f32[2,136,128]{2,1,0:T(8,128)S(1)}, f32[2,136,128]{2,1,0:T(8,128)}, u32[]{:S(2)}, u32[]{:S(2)}) collective-permute-start(f32[2,136,128]{2,1,0:T(8,128)S(1)} %constant_dynamic-slice_fusion.5), channel_id=1, source_target_pairs={{0,8},{4,12},{8,0},{12,4},{1,9},{5,13},{9,1},{13,5},{2,10},{6,14},... | collective-permute-start | bytes 417800 | tf_op jit(solution)/shard_map/ppermute | solution.py:238
  31.7 6.5 %collective-permute-start.1 = (f32[1,136,128]{2,1,0:T(8,128)}, f32[1,136,128]{2,1,0:T(8,128)}, u32[]{:S(2)}, u32[]{:S(2)}) collective-permute-start(f32[1,136,128]{2,1,0:T(8,128)} %constant_dynamic-slice_fusion.4), channel_id=1, source_target_pairs={{0,4},{4,0},{8,12},{12,8},{1,5},{5,1},{9,13},{13,9},{2,6},{6,2},{1... | collective-permute-start | bytes 208904 | tf_op jit(solution)/shard_map/ppermute | solution.py:238
  39.1 25.5 %collective-permute-start.4 = (f32[1,136,128]{2,1,0:T(8,128)S(1)}, f32[1,136,128]{2,1,0:T(8,128)S(1)}, u32[]{:S(2)}, u32[]{:S(2)}) collective-permute-start(f32[1,136,128]{2,1,0:T(8,128)S(1)} %dynamic-slice_add_fusion.1), channel_id=1, source_target_pairs={{0,3},{1,2},{2,1},{3,0},{4,7},{5,6},{6,5},{7,4},{8,11},{9,10},{10,... | collective-permute-start | bytes 208904 | tf_op jit(solution)/shard_map/ppermute | solution.py:238
  43.0 38.5 %collective-permute-start.3 = (f32[1,136,128]{2,1,0:T(8,128)S(1)}, f32[1,136,128]{2,1,0:T(8,128)S(1)}, u32[]{:S(2)}, u32[]{:S(2)}) collective-permute-start(f32[1,136,128]{2,1,0:T(8,128)S(1)} %dynamic-slice_add_fusion.1), channel_id=1, source_target_pairs={{0,2},{1,3},{2,0},{3,1},{4,6},{5,7},{6,4},{7,5},{8,10},{9,11},{10,... | collective-permute-start | bytes 208904 | tf_op jit(solution)/shard_map/ppermute | solution.py:238
  45.5 36.0 %collective-permute-start.2 = (f32[1,136,128]{2,1,0:T(8,128)S(1)}, f32[1,136,128]{2,1,0:T(8,128)S(1)}, u32[]{:S(2)}, u32[]{:S(2)}) collective-permute-start(f32[1,136,128]{2,1,0:T(8,128)S(1)} %dynamic-slice_add_fusion.1), channel_id=1, source_target_pairs={{0,1},{1,0},{2,3},{3,2},{4,5},{5,4},{6,7},{7,6},{8,9},{9,8},{10,11... | collective-permute-start | bytes 208904 | tf_op jit(solution)/shard_map/ppermute | solution.py:238
  82.7 25.3 %copy-start.10 = (s32[8]{0:T(128)S(1)}, s32[8]{0:T(128)}, u32[]{:S(2)}) copy-start(s32[8]{0:T(128)} %ranks_ref.1) | copy-start | bytes 100
  82.7 73.9 %all-to-all-start.1 = ((bf16[8,128,640]{2,1,0:T(8,128)(2,1)}), bf16[8,128,640]{2,1,0:T(8,128)(2,1)S(1)}, u32[]{:S(2)}, u32[]{:S(2)}) async-start(bf16[8,128,640]{2,1,0:T(8,128)(2,1)} %shard_map.59), calls=%async_computation.1 | async-start | bytes 2621440 | tf_op jit(solution)/shard_map/all_to_all | solution.py:229
  96.5 29.8 %copy-start.11 = (bf16[8,128,256]{2,1,0:T(8,128)(2,1)}, bf16[8,128,256]{2,1,0:T(8,128)(2,1)S(1)}, u32[]{:S(2)}) copy-start(bf16[8,128,256]{2,1,0:T(8,128)(2,1)S(1)} %slice.40.refs_0_) | copy-start | bytes 1572868
  96.5 23.9 %collective-permute-start.7 = (bf16[8,128,256]{2,1,0:T(8,128)(2,1)S(1)}, bf16[8,128,256]{2,1,0:T(8,128)(2,1)}, u32[]{:S(2)}, u32[]{:S(2)}) collective-permute-start(bf16[8,128,256]{2,1,0:T(8,128)(2,1)S(1)} %slice.40.refs_0_), channel_id=1, source_target_pairs={{0,4},{4,8},{8,12},{12,0},{1,5},{5,9},{9,13},{13,1},{2,6},{6,10},{... | collective-permute-start | bytes 1572872 | tf_op jit(solution)/shard_map/ppermute | solution.py:243
  100.0 24.8 %collective-permute-start.6 = (bf16[8,128,256]{2,1,0:T(8,128)(2,1)S(1)}, bf16[8,128,256]{2,1,0:T(8,128)(2,1)}, u32[]{:S(2)}, u32[]{:S(2)}) collective-permute-start(bf16[8,128,256]{2,1,0:T(8,128)(2,1)S(1)} %slice.40.refs_0_), channel_id=1, source_target_pairs={{0,8},{4,12},{8,0},{12,4},{1,9},{5,13},{9,1},{13,5},{2,10},{6,14},... | collective-permute-start | bytes 1572872 | tf_op jit(solution)/shard_map/ppermute | solution.py:243
  104.6 21.7 %collective-permute-start.5 = (bf16[8,128,256]{2,1,0:T(8,128)(2,1)S(1)}, bf16[8,128,256]{2,1,0:T(8,128)(2,1)}, u32[]{:S(2)}, u32[]{:S(2)}) collective-permute-start(bf16[8,128,256]{2,1,0:T(8,128)(2,1)S(1)} %slice.40.refs_0_), channel_id=1, source_target_pairs={{0,12},{4,0},{8,4},{12,8},{1,13},{5,1},{9,5},{13,9},{2,14},{6,2},{... | collective-permute-start | bytes 1572872 | tf_op jit(solution)/shard_map/ppermute | solution.py:243
  119.8 8.3 %copy-start.7 = (f32[2,128,128]{2,1,0:T(8,128)}, f32[2,128,128]{2,1,0:T(8,128)S(1)}, u32[]{:S(2)}) copy-start(f32[2,128,128]{2,1,0:T(8,128)S(1)} %shard_map.57.refs_0_) | copy-start | bytes 393220
  131.1 18.8 %collective-permute-start.8 = (bf16[8,128,384]{2,1,0:T(8,128)(2,1)S(1)}, bf16[8,128,384]{2,1,0:T(8,128)(2,1)}, u32[]{:S(2)}, u32[]{:S(2)}) collective-permute-start(bf16[8,128,384]{2,1,0:T(8,128)(2,1)S(1)} %shard_map.60.level_ref), channel_id=1, source_target_pairs={{0,16},{16,0},{1,17},{17,1},{2,18},{18,2},{3,19},{19,3},{4,20},{20... | collective-permute-start | bytes 2359304 | tf_op jit(solution)/shard_map/ppermute | solution.py:238
  133.6 15.5 %copy-start.8 = (f32[2,128,128]{2,1,0:T(8,128)S(1)}, f32[2,128,128]{2,1,0:T(8,128)}, u32[]{:S(2)}) copy-start(f32[2,128,128]{2,1,0:T(8,128)} %shard_map.62) | copy-start | bytes 393220
  133.6 12.8 %collective-permute-start.11 = (f32[2,128,128]{2,1,0:T(8,128)}, f32[2,128,128]{2,1,0:T(8,128)S(1)}, u32[]{:S(2)}, u32[]{:S(2)}) collective-permute-start(f32[2,128,128]{2,1,0:T(8,128)} %shard_map.62), channel_id=1, source_target_pairs={{0,4},{4,8},{8,12},{12,0},{1,5},{5,9},{9,13},{13,1},{2,6},{6,10},{... | collective-permute-start | bytes 393224 | tf_op jit(solution)/shard_map/ppermute | solution.py:243
  138.0 9.2 %collective-permute-start.10 = (f32[2,128,128]{2,1,0:T(8,128)}, f32[2,128,128]{2,1,0:T(8,128)S(1)}, u32[]{:S(2)}, u32[]{:S(2)}) collective-permute-start(f32[2,128,128]{2,1,0:T(8,128)} %shard_map.62), channel_id=1, source_target_pairs={{0,8},{4,12},{8,0},{12,4},{1,9},{5,13},{9,1},{13,5},{2,10},{6,14},... | collective-permute-start | bytes 393224 | tf_op jit(solution)/shard_map/ppermute | solution.py:243
  141.7 7.4 %collective-permute-start.9 = (f32[2,128,128]{2,1,0:T(8,128)}, f32[2,128,128]{2,1,0:T(8,128)S(1)}, u32[]{:S(2)}, u32[]{:S(2)}) collective-permute-start(f32[2,128,128]{2,1,0:T(8,128)} %shard_map.62), channel_id=1, source_target_pairs={{0,12},{4,0},{8,4},{12,8},{1,13},{5,1},{9,5},{13,9},{2,14},{6,2},{... | collective-permute-start | bytes 393224 | tf_op jit(solution)/shard_map/ppermute | solution.py:243
  157.9 5.9 %copy-start.4 = (bf16[2,8,128,256]{3,2,1,0:T(8,128)(2,1)S(1)}, bf16[2,8,128,256]{3,2,1,0:T(8,128)(2,1)}, u32[]{:S(2)}) copy-start(bf16[2,8,128,256]{3,2,1,0:T(8,128)(2,1)} %copy-done.3) | copy-start | bytes 3145732
  157.9 5.9 %copy-start.6 = (f32[4,256,256]{2,1,0:T(8,128)S(1)}, f32[4,256,256]{2,1,0:T(8,128)}, u32[]{:S(2)}) copy-start(f32[4,256,256]{2,1,0:T(8,128)} %copy-done.5) | copy-start | bytes 3145732
  158.9 4.9 %collective-permute-start.12 = (bf16[8,128,640]{2,1,0:T(8,128)(2,1)S(1)}, bf16[8,128,640]{2,1,0:T(8,128)(2,1)S(1)}, u32[]{:S(2)}, u32[]{:S(2)}) collective-permute-start(bf16[8,128,640]{2,1,0:T(8,128)(2,1)S(1)} %shard_map.63.level_ref), channel_id=1, source_target_pairs={{0,16},{16,0},{1,17},{17,1},{2,18},{18,2},{3,19},{19,3},{4,20},{20... | collective-permute-start | bytes 3932168 | tf_op jit(solution)/shard_map/ppermute | solution.py:238
  166.7 23.0 %copy-start.13 = (f32[4,2,128,128]{3,2,1,0:T(8,128)S(1)}, f32[4,2,128,128]{3,2,1,0:T(8,128)}, u32[]{:S(2)}) copy-start(f32[4,2,128,128]{3,2,1,0:T(8,128)} %copy-done.12) | copy-start | bytes 1572868
  182.0 21.7 %all-to-all-start.3 = ((f32[16,2,8,128]{3,2,1,0:T(8,128)}), f32[16,2,8,128]{3,2,1,0:T(8,128)S(1)}, u32[]{:S(2)}, u32[]{:S(2)}) async-start(f32[16,2,8,128]{3,2,1,0:T(8,128)} %copy.15), calls=%async_computation.3 | async-start | bytes 262144 | tf_op jit(solution)/shard_map/all_to_all | solution.py:229
  (6 other events, 10.3 us)

commit v4 on v3

--- a/solution.py
+++ b/solution.py
@@ -16,7 +16,7 @@
 HIGHEST = lax.Precision.HIGHEST
 
 
-def gram_kernel(panels_ref, out_ref):
+def gram_kernel(panels_ref, out_ref, copy_ref):
     rows = lax.broadcasted_iota(jnp.int32, (RANK, RANK), 0)
     cols = lax.broadcasted_iota(jnp.int32, (RANK, RANK), 1)
 
@@ -31,14 +31,18 @@
         out_ref[pair, :RANK] = jnp.where(rows >= cols, below, above)
         diagonal = jnp.sum(jnp.where(rows == cols, above, 0.0), axis=0, keepdims=True)
         out_ref[pair, RANK:] = jnp.broadcast_to(diagonal, (8, RANK))
+    copy_ref[...] = panels_ref[...]
 
 
 def local_grams(panels):
     return pl.pallas_call(
         gram_kernel,
-        out_shape=jax.ShapeDtypeStruct((SLOTS // 2, RANK + 8, RANK), jnp.float32),
+        out_shape=(
+            jax.ShapeDtypeStruct((SLOTS // 2, RANK + 8, RANK), jnp.float32),
+            jax.ShapeDtypeStruct(panels.shape, panels.dtype),
+        ),
         in_specs=[pl.BlockSpec(memory_space=pltpu.VMEM)],
-        out_specs=pl.BlockSpec(memory_space=pltpu.VMEM),
+        out_specs=[pl.BlockSpec(memory_space=pltpu.VMEM)] * 2,
         compiler_params=pltpu.CompilerParams(vmem_limit_bytes=16 * 2**20),
     )(panels)
 
@@ -164,18 +168,9 @@
 PAIRS = tuple((slot, slot ^ 2) for slot in range(SLOTS) if slot < slot ^ 2)
 
 
-def early_kernel(factors_ref, level_ref, paired_ref, base_ref, out_ref):
-    for at, (slot, other) in enumerate(PAIRS):
-        out_ref[at] = sums_of(
-            factors_ref, level_ref, paired_ref, base_ref, slot, other
-        )
-
-
-def cross_kernel(factors_ref, level_ref, paired_ref, base_ref, early_ref, out_ref):
-    for at, (slot, other) in enumerate(PAIRS):
-        sums = early_ref[at] + sums_of(
-            factors_ref, level_ref, paired_ref, base_ref, slot, other
-        )
+def cross_kernel(factors_ref, level_ref, paired_ref, base_ref, out_ref):
+    for slot, other in PAIRS:
+        sums = sums_of(factors_ref, level_ref, paired_ref, base_ref, slot, other)
         parts = []
         for _ in range(3):
             part = sums.astype(jnp.bfloat16)
@@ -189,9 +184,7 @@
             side_of = slice(side * RANK, (side + 1) * RANK)
             cross = sum(matmul(factor[side], part[:, side_of]) for part in parts[::-1])
             for x in range(4):
-                for zl in range(4):
-                    start = 8 * (4 * x + zl)
-                    out_ref[block // 4, x, block % 4, zl] = cross[start : start + 8]
+                out_ref[block // 4, x, block % 4] = cross[32 * x : 32 * x + 32]
 
 
 def sums_call(kernel, shape, *arrays):
@@ -250,12 +243,12 @@
 
 
 def grams(panels):
-    x_at = lax.axis_index("x")
-    packed = local_grams(panels)
-    high, low = x_at // 2, x_at % 2
-    packed = part(packed, high, 2) + swap(part(packed, 1 - high, 2), "x", 2)
-    packed = part(packed, low, 1) + swap(part(packed, 1 - low, 1), "x", 1)
-    return packed + swap(packed, "zl", 1) + (swap(packed, "zl", 2) + swap(packed, "zl", 3))
+    zl_at = lax.axis_index("zl")
+    packed, panels = local_grams(panels)
+    total = part(packed, zl_at, 1)
+    for other in range(1, 4):
+        total = total + swap(part(packed, zl_at ^ other, 1), "zl", other)
+    return total, panels
 
 
 def by_place(every):
@@ -264,82 +257,76 @@
 
 
 def gather_halved(solved):
+    blocks, rows, _ = solved.shape
     top = jnp.max(jnp.abs(solved), axis=2)
     power = jnp.clip(jnp.floor(jnp.log2(jnp.maximum(top, 1e-36))), -120.0, 120.0)
     values = (solved * jnp.exp2(-power)[:, :, None]).astype(jnp.float16)
-    powers = jnp.pad(power.astype(jnp.float16), ((0, 0), (0, RANK - power.shape[1])))
+    powers = jnp.pad(power.T.astype(jnp.float16), ((0, 0), (0, RANK - blocks)))
     sent = gather(jnp.concatenate([values, powers[None]], axis=0), COL)
-    blocks = solved.shape[0]
-    power = sent[:, blocks, :, : solved.shape[1]].astype(jnp.float32)
+    power = sent[:, blocks, :, :blocks].astype(jnp.float32).transpose(0, 2, 1)
     values = sent[:, :blocks].astype(jnp.float32) * jnp.exp2(power)[:, :, :, None]
-    return values.transpose(1, 0, 2, 3).reshape(-1, RANK)
-
-
-def first_kernel(place_ref, mask_ref, panels_ref, own_ref, paired_ref, out_ref):
-    columns = panels_ref.shape[1]
+    values = values.reshape(4, 2, 2, blocks, rows, RANK)
+    return values.transpose(1, 3, 0, 2, 4, 5).reshape(-1, RANK)
+
+
+def level_kernel(place_ref, mask_ref, own_ref, paired_ref, out_ref):
     for slot in range(SLOTS):
-        rows = slice(slot * RANK, (slot + 1) * RANK)
         mask = mask_ref[place_ref[0], slot].astype(jnp.float32)
-        out_ref[slot, :, :columns] = panels_ref[rows]
-        out_ref[slot, :, columns : columns + RANK] = own_ref[0, rows]
-        paired = paired_ref[0, rows].astype(jnp.float32) * mask
-        out_ref[slot, :, columns + RANK :] = paired.astype(jnp.bfloat16)
-
-
-def first_part(place, panels, self_factors, partner_factors, link_mask, columns):
-    rows = panels.shape[0]
-    level = pl.BlockSpec((1, rows, RANK), lambda i, place: (place[0], 0, 0))
-    shape = SLOTS, RANK, columns + 2 * RANK
-    return pl.pallas_call(
-        first_kernel,
-        out_shape=jax.ShapeDtypeStruct(shape, panels.dtype),
+        out_ref[slot, :, :RANK] = own_ref[0, slot, 0]
+        paired = paired_ref[0, slot, 0].astype(jnp.float32) * mask
+        out_ref[slot, :, RANK:] = paired.astype(jnp.bfloat16)
+
+
+def half_level(place, self_factors, partner_factors, link_mask):
+    half = RANK // 2
+    spec = pl.BlockSpec(
+        (1, SLOTS, 1, half, RANK), lambda i, place: (place[0], 0, place[1], 0, 0)
+    )
+    shape = SLOTS, half, 2 * RANK
+    split = LEVELS, SLOTS, 2, half, RANK
+    return pl.pallas_call(
+        level_kernel,
+        out_shape=jax.ShapeDtypeStruct(shape, self_factors.dtype),
         grid_spec=pltpu.PrefetchScalarGridSpec(
             num_scalar_prefetch=1,
             grid=(1,),
-            in_specs=[
-                pl.BlockSpec(memory_space=pltpu.SMEM),
-                pl.BlockSpec((rows, columns), lambda i, place: (0, 0)),
-                level,
-                level,
-            ],
+            in_specs=[pl.BlockSpec(memory_space=pltpu.SMEM), spec, spec],
             out_specs=pl.BlockSpec(shape, lambda i, place: (0, 0, 0)),
         ),
         compiler_params=pltpu.CompilerParams(vmem_limit_bytes=60 * 2**20),
-    )(place, link_mask, panels, self_factors, partner_factors)
+    )(place, link_mask, self_factors.reshape(split), partner_factors.reshape(split))
 
 
 def body(panels, self_factors, partner_factors, link_mask, block_ranks):
     columns = panels.shape[1]
-    early = columns * 3 // 8
-    late = columns - early
-    own = panels.reshape(SLOTS, RANK, columns)
-    place = lax.axis_index("x").astype(jnp.int32).reshape(1)
-
-    first = first_part(place, panels, self_factors, partner_factors, link_mask, early)
-    first = exchange(first, PEERS)
-    gram = grams(panels)
-    second = exchange(once_done(own[:, :, early:], first, gram), PEERS)
-    inverse = invert(place, block_ranks, gram)
-    factors = along_x(first[:, :, early:], inverse)
-    inverse = along_x(once_done(inverse, factors))
-    factors = by_place(factors)
+    zl_at = lax.axis_index("zl")
+    odd = zl_at % 2
+    place = jnp.stack([lax.axis_index("x"), odd]).astype(jnp.int32)
+
+    own_half = exchange(half_level(place, self_factors, partner_factors, link_mask), PEERS)
+    other_half = swap(own_half, "zl", 1)
+    gram, panels = grams(panels)
+    panels = once_done(panels, other_half, gram).reshape(SLOTS, RANK, columns)
+    base = exchange(panels, PEERS)
+
+    gram = gram + swap(gram, "x", 1)
+    gram = gram + swap(gram, "x", 2)
+    inverse = invert(zl_at.astype(jnp.int32).reshape(1), block_ranks, gram)
+    halves = [jnp.where(odd == at, own_half, other_half) for at in range(2)]
+    factors = by_place(along_x(jnp.concatenate(halves, axis=1), inverse))
     lower, upper = jnp.stack(factors[:2]), jnp.stack(factors[2:])
 
-    level = near_levels(first, lower, early)
+    level = near_levels(base, lower, columns)
     paired = swap(level, "core", 1)
-    shape = len(PAIRS), 2 * RANK, 2 * RANK
-    sums = sums_call(early_kernel, shape, upper, level, paired, first)
-    level = near_levels(second, lower, late, sums, inverse)
-    paired = swap(level, "core", 1)
-    shape = 2, 4, 4, 4, 8, RANK
-    cross = sums_call(cross_kernel, shape, upper, level, paired, second, sums)
-
-    cross = exchange(cross.reshape(2 * 4, 16, 8, RANK), ("yl", "x"))
-    cross = cross.reshape(2, 4, 16, 8, RANK).sum(1)
-    cross = exchange(cross.transpose(1, 0, 2, 3), ("zh", "zl"))
-    cross = cross.reshape(4, 4, 2, 8, RANK).sum(1)
-    cross = cross.transpose(1, 0, 2, 3).reshape(SLOTS, 8, RANK)
-    inverse = jnp.concatenate(by_place(inverse), axis=0)
+    cross = sums_call(cross_kernel, (2, 4, 4, 32, RANK), upper, level, paired, base)
+
+    cross = exchange(cross.reshape(2 * 4, 4, 32, RANK), ("yl", "x"))
+    cross = cross.reshape(2, 4, 4, 2, 16, RANK).sum(1)
+    cross = cross.transpose(1, 0, 2, 3, 4).reshape(16, 16, RANK)
+    cross = exchange(cross, ("zh", "zl")).reshape(4, 4, 16, RANK).sum(1)
+    pairs = jnp.stack([inverse, swap(inverse, "zl", 1)])
+    pairs = [lax.dynamic_index_in_dim(pairs, zl_at % 2 ^ p, 0, False) for p in range(2)]
+    inverse = jnp.concatenate(pairs, axis=0)
     solved = jnp.einsum("jrk,jkm->jrm", cross, inverse, precision=HIGHEST)
     return gather_halved(solved)
 

time: 221 us -> 216 us (0.977)
  starting transfers between devices: 83.4 us -> 105 us
  waiting for transfers between devices: 66.7 us -> 52.7 us
  local copies, waits for them, and re-layouts: 11.9 us -> 6.09 us
  other arithmetic: 6.26 us -> 3 us
    all_to_all x3, starting transfers between devices: 38.1 us -> 61.2 us  [exchange(): return lax.all_to_all(blocks, axes, 0, 0, tiled=True)]
    ppermute x6 -> x3, starting transfers between devices: 22.9 us -> 11.4 us  [along_x(): lax.ppermute(block, 'x', [(i, (i - d) % count) for i in range(count)])]
    ppermute x7 -> x8, starting transfers between devices: 22.4 us -> 32.2 us  [swap(): lax.ppermute(block, axis, [(i, i ^ bit) for i in range(lax.axis_size(axis...]
    ppermute x6 -> x3, waiting for transfers between devices: 8.54 us -> 0.01 us  [along_x(): lax.ppermute(block, 'x', [(i, (i - d) % count) for i in range(count)])]
    ppermute x7 -> x8, waiting for transfers between devices: 40.5 us -> 33.1 us  [swap(): lax.ppermute(block, axis, [(i, i ^ bit) for i in range(lax.axis_size(axis...]
    unnamed x28 -> x12, local copies, waits for them, and re-layouts: 4.72 us -> 1.35 us
    pallas_call x2 -> x1, Pallas kernels: 4.9 us -> 3.39 us  [sums_call(): pl.pallas_call(kernel, out_shape=jax.ShapeDtypeStruct(shape, jnp.float32)...]
  transfers between devices with their start and end apart: 16 -> 14, of which waited for: 11 -> 8; matrix products, arithmetic and copies ran while one was open for 5% -> 2% of each run, Pallas kernels for 7% -> 6%
where the time goes in v4:
time: 216 us; the launch traced here: 215 us
  starting transfers between devices  105 us (49%)
  waiting for transfers between devices  52.7 us (24%)
  blocking collectives  27.9 us (13%)
  Pallas kernels  19.7 us (9%)
  local copies, waits for them, and re-layouts  6.09 us (3%)
  other arithmetic  3 us (1%)
    all_to_all x3, starting transfers between devices, exchange(): return lax.all_to_all(blocks, axes, 0, 0, tiled=True)  61.2 us
    ppermute x8, waiting for transfers between devices, swap(): lax.ppermute(block, axis, [(i, i ^ bit) for i in range(lax.axis_size(axis...  33.1 us
    ppermute x8, starting transfers between devices, swap(): lax.ppermute(block, axis, [(i, i ^ bit) for i in range(lax.axis_size(axis...  32.2 us
    all_to_all x2, blocking collectives, exchange(): return lax.all_to_all(blocks, axes, 0, 0, tiled=True)  27.9 us
    all_to_all x3, waiting for transfers between devices, exchange(): return lax.all_to_all(blocks, axes, 0, 0, tiled=True)  19.5 us
    pallas_call x1, Pallas kernels, invert(): pl.pallas_call(invert_kernel, out_shape=jax.ShapeDtypeStruct((2, RANK, RA...  11.7 us
    ppermute x3, starting transfers between devices, along_x(): lax.ppermute(block, 'x', [(i, (i - d) % count) for i in range(count)])  11.4 us
  transfers between devices with their start and end apart: 14, of which 8 were waited for; matrix products, arithmetic and copies ran while one was open for 2% of the time, Pallas kernels for 6%

profile of v4, /device:TPU:24, one launch (start us, length us, event | category | flops | bytes accessed | tf_op | source)
XLA Modules:
  0.0 215.0 jit_solution(6928169011467206351)
XLA Ops:
  0.6 2.5 %shard_map.55 = bf16[8,64,256]{2,1,0:T(8,128)(2,1)} custom-call(s32[2]{0:T(128)} %pad_add_fusion.place_ref, s32[4,8]{1,0:T(4,128)} %mask_ref.1, bf16[4,8,2,64,128]{4,3,2,1,0:T(8,128)(2,1)} %bitcast.47, bf16[4,8,2,64,128]{4,3,2,1,0:T(8,128)(2,1)} %bitcast.48), custom_call_target="tpu_custom_call" | custom-call | tf_op jit(solution)/shard_map/pallas_call | solution.py:287
  3.1 16.5 %all-to-all-start = ((bf16[8,64,256]{2,1,0:T(8,128)(2,1)}), bf16[8,64,256]{2,1,0:T(8,128)(2,1)S(1)}, u32[]{:S(2)}, u32[]{:S(2)}) async-start(bf16[8,64,256]{2,1,0:T(8,128)(2,1)} %shard_map.55), calls=%async_computation | async-start | bytes 524288 | tf_op jit(solution)/shard_map/all_to_all | solution.py:222
  21.8 3.8 %collective-permute-start.3 = (f32[1,136,128]{2,1,0:T(8,128)S(1)}, f32[1,136,128]{2,1,0:T(8,128)S(1)}, u32[]{:S(2)}, u32[]{:S(2)}) collective-permute-start(f32[1,136,128]{2,1,0:T(8,128)S(1)} %get-tuple-element.16), channel_id=1, source_target_pairs={{0,3},{1,2},{2,1},{3,0},{4,7},{5,6},{6,5},{7,4},{8,11},{9,10},{10,... | collective-permute-start | bytes 208904 | tf_op jit(solution)/shard_map/ppermute | solution.py:231
  28.1 3.8 %collective-permute-start.1 = (f32[1,136,128]{2,1,0:T(8,128)S(1)}, f32[1,136,128]{2,1,0:T(8,128)S(1)}, u32[]{:S(2)}, u32[]{:S(2)}) collective-permute-start(f32[1,136,128]{2,1,0:T(8,128)S(1)} %get-tuple-element.15), channel_id=1, source_target_pairs={{0,1},{1,0},{2,3},{3,2},{4,5},{5,4},{6,7},{7,6},{8,9},{9,8},{10,11... | collective-permute-start | bytes 208904 | tf_op jit(solution)/shard_map/ppermute | solution.py:231
  31.9 5.0 %all-to-all-done = bf16[8,64,256]{2,1,0:T(8,128)(2,1)S(1)} async-done(((bf16[8,64,256]{2,1,0:T(8,128)(2,1)}), bf16[8,64,256]{2,1,0:T(8,128)(2,1)S(1)}, u32[]{:S(2)}, u32[]{:S(2)}) %all-to-all-start) | async-done | bytes 262176 | tf_op jit(solution)/shard_map/all_to_all | solution.py:222
  36.9 8.7 %collective-permute-start = (bf16[8,64,256]{2,1,0:T(8,128)(2,1)S(1)}, bf16[8,64,256]{2,1,0:T(8,128)(2,1)S(1)}, u32[]{:S(2)}, u32[]{:S(2)}) collective-permute-start(bf16[8,64,256]{2,1,0:T(8,128)(2,1)S(1)} %all-to-all-done), channel_id=1, source_target_pairs={{0,1},{1,0},{2,3},{3,2},{4,5},{5,4},{6,7},{7,6},{8,9},{9,8},{10,11... | collective-permute-start | bytes 786440 | tf_op jit(solution)/shard_map/ppermute | solution.py:231
  46.3 3.7 %collective-permute-done = bf16[8,64,256]{2,1,0:T(8,128)(2,1)S(1)} collective-permute-done((bf16[8,64,256]{2,1,0:T(8,128)(2,1)S(1)}, bf16[8,64,256]{2,1,0:T(8,128)(2,1)S(1)}, u32[]{:S(2)}, u32[]{:S(2)}) %collective-permute-start) | collective-permute-done | bytes 262176 | tf_op jit(solution)/shard_map/ppermute | solution.py:231
  50.6 4.9 %all-to-all-start.1 = ((bf16[8,128,1024]{2,1,0:T(8,128)(2,1)}), bf16[8,128,1024]{2,1,0:T(8,128)(2,1)S(1)}, u32[]{:S(2)}, u32[]{:S(2)}) async-start(bf16[8,128,1024]{2,1,0:T(8,128)(2,1)} %bitcast.41), calls=%async_computation.1 | async-start | bytes 4194304 | tf_op jit(solution)/shard_map/all_to_all | solution.py:222
  55.6 3.4 %collective-permute-start.8 = (bf16[8,128,256]{2,1,0:T(8,128)(2,1)S(1)}, bf16[8,128,256]{2,1,0:T(8,128)(2,1)S(1)}, u32[]{:S(2)}, u32[]{:S(2)}) collective-permute-start(bf16[8,128,256]{2,1,0:T(8,128)(2,1)S(1)} %pad_maximum_fusion.3.refs_0_), channel_id=1, source_target_pairs={{0,4},{4,8},{8,12},{12,0},{1,5},{5,9},{9,13},{13,1},{2,6},{6,10},{... | collective-permute-start | bytes 1572872 | tf_op jit(solution)/shard_map/ppermute | solution.py:236
  59.0 4.6 %collective-permute-start.7 = (bf16[8,128,256]{2,1,0:T(8,128)(2,1)S(1)}, bf16[8,128,256]{2,1,0:T(8,128)(2,1)}, u32[]{:S(2)}, u32[]{:S(2)}) collective-permute-start(bf16[8,128,256]{2,1,0:T(8,128)(2,1)S(1)} %pad_maximum_fusion.3.refs_0_), channel_id=1, source_target_pairs={{0,8},{4,12},{8,0},{12,4},{1,9},{5,13},{9,1},{13,5},{2,10},{6,14},... | collective-permute-start | bytes 1572872 | tf_op jit(solution)/shard_map/ppermute | solution.py:236
  63.6 3.3 %collective-permute-start.6 = (bf16[8,128,256]{2,1,0:T(8,128)(2,1)S(1)}, bf16[8,128,256]{2,1,0:T(8,128)(2,1)}, u32[]{:S(2)}, u32[]{:S(2)}) collective-permute-start(bf16[8,128,256]{2,1,0:T(8,128)(2,1)S(1)} %pad_maximum_fusion.3.refs_0_), channel_id=1, source_target_pairs={{0,12},{4,0},{8,4},{12,8},{1,13},{5,1},{9,5},{13,9},{2,14},{6,2},{... | collective-permute-start | bytes 1572872 | tf_op jit(solution)/shard_map/ppermute | solution.py:236
  69.5 16.2 %collective-permute-done.4 = f32[1,136,128]{2,1,0:T(8,128)S(1)} collective-permute-done((f32[1,136,128]{2,1,0:T(8,128)S(1)}, f32[1,136,128]{2,1,0:T(8,128)S(1)}, u32[]{:S(2)}, u32[]{:S(2)}) %collective-permute-start.4) | collective-permute-done | bytes 69664 | tf_op jit(solution)/shard_map/ppermute | solution.py:231
  85.7 5.0 %collective-permute-start.5 = (f32[1,136,128]{2,1,0:T(8,128)S(1)}, f32[1,136,128]{2,1,0:T(8,128)S(1)}, u32[]{:S(2)}, u32[]{:S(2)}) collective-permute-start(f32[1,136,128]{2,1,0:T(8,128)S(1)} %add.75), channel_id=1, source_target_pairs={{0,8},{4,12},{8,0},{12,4},{1,9},{5,13},{9,1},{13,5},{2,10},{6,14},... | collective-permute-start | bytes 208904 | tf_op jit(solution)/shard_map/ppermute | solution.py:231
  90.8 2.7 %collective-permute-done.5 = f32[1,136,128]{2,1,0:T(8,128)S(1)} collective-permute-done((f32[1,136,128]{2,1,0:T(8,128)S(1)}, f32[1,136,128]{2,1,0:T(8,128)S(1)}, u32[]{:S(2)}, u32[]{:S(2)}) %collective-permute-start.5) | collective-permute-done | bytes 69664 | tf_op jit(solution)/shard_map/ppermute | solution.py:231
  93.5 11.7 %shard_map.57 = f32[2,128,128]{2,1,0:T(8,128)S(1)} custom-call(s32[1]{0:T(128)} %bitcast.4.place_ref, s32[8]{0:T(128)S(1)} %copy-done.2, f32[1,136,128]{2,1,0:T(8,128)S(1)} %add.76.packed_ref), custom_call_target="tpu_custom_call" | custom-call | tf_op jit(solution)/shard_map/pallas_call | solution.py:98
  108.7 10.5 %all-to-all-done.1.base_ref = bf16[8,128,1024]{2,1,0:T(8,128)(2,1)S(1)} async-done(((bf16[8,128,1024]{2,1,0:T(8,128)(2,1)}), bf16[8,128,1024]{2,1,0:T(8,128)(2,1)S(1)}, u32[]{:S(2)}, u32[]{:S(2)}) %all-to-all-start.1) | async-done | bytes 2097184 | tf_op jit(solution)/shard_map/all_to_all | solution.py:222
  122.8 3.8 %collective-permute-done.9.paired_ref = bf16[8,128,1024]{2,1,0:T(8,128)(2,1)S(1)} collective-permute-done((bf16[8,128,1024]{2,1,0:T(8,128)(2,1)S(1)}, bf16[8,128,1024]{2,1,0:T(8,128)(2,1)S(1)}, u32[]{:S(2)}, u32[]{:S(2)}) %collective-permute-start.9) | collective-permute-done | bytes 2097184 | tf_op jit(solution)/shard_map/ppermute | solution.py:231
  126.6 3.4 %shard_map.61 = f32[2,4,4,32,128]{4,3,2,1,0:T(8,128)S(1)} custom-call(bf16[2,8,128,256]{3,2,1,0:T(8,128)(2,1)S(1)} %pad_maximum_fusion.1.factors_ref, bf16[8,128,1024]{2,1,0:T(8,128)(2,1)S(1)} %shard_map.60.level_ref, bf16[8,128,1024]{2,1,0:T(8,128)(2,1)S(1)} %collective-permute-done.9.paired_ref, bf16[8,128,1024]{2,1,0:T(8,128)(2,1)S(1)} %all-to-all-done.1.base_ref), custom_call_target="tpu_custom_call" | custom-call | tf_op jit(solution)/shard_map/pallas_call | solution.py:192
  130.0 14.5 %all_to_all.25 = f32[8,4,32,128]{3,2,1,0:T(8,128)S(1)} all-to-all(f32[8,4,32,128]{3,2,1,0:T(8,128)S(1)} %bitcast.42), channel_id=1, replica_groups=mesh['yh'=2,'yl'=2,'zh'=4,'core'=2,'x'=4,'zl'=4] {'yl','x'}, dimensions={0} | all-to-all | bytes 1048576 | tf_op jit(solution)/shard_map/all_to_all | solution.py:222
  145.2 39.8 %all-to-all-start.3 = ((f32[16,16,128]{2,1,0:T(8,128)}), f32[16,16,128]{2,1,0:T(8,128)S(1)}, u32[]{:S(2)}, u32[]{:S(2)}) async-start(f32[16,16,128]{2,1,0:T(8,128)} %bitcast.16), calls=%async_computation.3 | async-start | bytes 262144 | tf_op jit(solution)/shard_map/all_to_all | solution.py:222
  185.0 3.8 %collective-permute-start.10 = (f32[2,128,128]{2,1,0:T(8,128)S(1)}, f32[2,128,128]{2,1,0:T(8,128)S(1)}, u32[]{:S(2)}, u32[]{:S(2)}) collective-permute-start(f32[2,128,128]{2,1,0:T(8,128)S(1)} %shard_map.57), channel_id=1, source_target_pairs={{0,1},{1,0},{2,3},{3,2},{4,5},{5,4},{6,7},{7,6},{8,9},{9,8},{10,11... | collective-permute-start | bytes 393224 | tf_op jit(solution)/shard_map/ppermute | solution.py:231
  188.8 6.7 %collective-permute-done.10 = f32[2,128,128]{2,1,0:T(8,128)S(1)} collective-permute-done((f32[2,128,128]{2,1,0:T(8,128)S(1)}, f32[2,128,128]{2,1,0:T(8,128)S(1)}, u32[]{:S(2)}, u32[]{:S(2)}) %collective-permute-start.10) | collective-permute-done | bytes 131104 | tf_op jit(solution)/shard_map/ppermute | solution.py:231
  195.6 4.0 %all-to-all-done.3 = f32[16,16,128]{2,1,0:T(8,128)S(1)} async-done(((f32[16,16,128]{2,1,0:T(8,128)}), f32[16,16,128]{2,1,0:T(8,128)S(1)}, u32[]{:S(2)}, u32[]{:S(2)}) %all-to-all-start.3) | async-done | bytes 131104 | tf_op jit(solution)/shard_map/all_to_all | solution.py:222
  200.3 13.4 %all_to_all.26 = f16[16,5,16,128]{3,2,1,0:T(8,128)(2,1)S(1)} all-to-all(f16[16,5,16,128]{3,2,1,0:T(8,128)(2,1)S(1)} %broadcast_in_dim.5), channel_id=1, replica_groups=mesh['yh'=2,'yl'=2,'zh'=4,'core'=2,'x'=4,'zl'=4] {'x','zl'}, dimensions={0} | all-to-all | bytes 655360 | tf_op jit(solution)/shard_map/all_to_all | solution.py:222
  (54 shorter events, 18.6 us)
Async XLA Ops:
  0.0 19.7 %copy-start.1 = (bf16[1024,1024]{1,0:T(8,128)(2,1)S(1)}, bf16[1024,1024]{1,0:T(8,128)(2,1)}, u32[]{:S(2)}) copy-start(bf16[1024,1024]{1,0:T(8,128)(2,1)} %panels_ref.1) | copy-start | bytes 6291460
  3.1 33.8 %all-to-all-start = ((bf16[8,64,256]{2,1,0:T(8,128)(2,1)}), bf16[8,64,256]{2,1,0:T(8,128)(2,1)S(1)}, u32[]{:S(2)}, u32[]{:S(2)}) async-start(bf16[8,64,256]{2,1,0:T(8,128)(2,1)} %shard_map.55), calls=%async_computation | async-start | bytes 524288 | tf_op jit(solution)/shard_map/all_to_all | solution.py:222
  20.4 1.3 copy-start
  21.8 23.9 %collective-permute-start.3 = (f32[1,136,128]{2,1,0:T(8,128)S(1)}, f32[1,136,128]{2,1,0:T(8,128)S(1)}, u32[]{:S(2)}, u32[]{:S(2)}) collective-permute-start(f32[1,136,128]{2,1,0:T(8,128)S(1)} %get-tuple-element.16), channel_id=1, source_target_pairs={{0,3},{1,2},{2,1},{3,0},{4,7},{5,6},{6,5},{7,4},{8,11},{9,10},{10,... | collective-permute-start | bytes 208904 | tf_op jit(solution)/shard_map/ppermute | solution.py:231
  25.6 20.0 %collective-permute-start.2 = (f32[1,136,128]{2,1,0:T(8,128)S(1)}, f32[1,136,128]{2,1,0:T(8,128)S(1)}, u32[]{:S(2)}, u32[]{:S(2)}) collective-permute-start(f32[1,136,128]{2,1,0:T(8,128)S(1)} %get-tuple-element.17), channel_id=1, source_target_pairs={{0,2},{1,3},{2,0},{3,1},{4,6},{5,7},{6,4},{7,5},{8,10},{9,11},{10,... | collective-permute-start | bytes 208904 | tf_op jit(solution)/shard_map/ppermute | solution.py:231
  28.1 17.6 %collective-permute-start.1 = (f32[1,136,128]{2,1,0:T(8,128)S(1)}, f32[1,136,128]{2,1,0:T(8,128)S(1)}, u32[]{:S(2)}, u32[]{:S(2)}) collective-permute-start(f32[1,136,128]{2,1,0:T(8,128)S(1)} %get-tuple-element.15), channel_id=1, source_target_pairs={{0,1},{1,0},{2,3},{3,2},{4,5},{5,4},{6,7},{7,6},{8,9},{9,8},{10,11... | collective-permute-start | bytes 208904 | tf_op jit(solution)/shard_map/ppermute | solution.py:231
  36.9 13.1 %collective-permute-start = (bf16[8,64,256]{2,1,0:T(8,128)(2,1)S(1)}, bf16[8,64,256]{2,1,0:T(8,128)(2,1)S(1)}, u32[]{:S(2)}, u32[]{:S(2)}) collective-permute-start(bf16[8,64,256]{2,1,0:T(8,128)(2,1)S(1)} %all-to-all-done), channel_id=1, source_target_pairs={{0,1},{1,0},{2,3},{3,2},{4,5},{5,4},{6,7},{7,6},{8,9},{9,8},{10,11... | collective-permute-start | bytes 786440 | tf_op jit(solution)/shard_map/ppermute | solution.py:231
  50.6 68.7 %all-to-all-start.1 = ((bf16[8,128,1024]{2,1,0:T(8,128)(2,1)}), bf16[8,128,1024]{2,1,0:T(8,128)(2,1)S(1)}, u32[]{:S(2)}, u32[]{:S(2)}) async-start(bf16[8,128,1024]{2,1,0:T(8,128)(2,1)} %bitcast.41), calls=%async_computation.1 | async-start | bytes 4194304 | tf_op jit(solution)/shard_map/all_to_all | solution.py:222
  55.5 38.0 %copy-start.2 = (s32[8]{0:T(128)S(1)}, s32[8]{0:T(128)}, u32[]{:S(2)}) copy-start(s32[8]{0:T(128)} %ranks_ref.1) | copy-start | bytes 100
  55.6 50.3 %copy-start.3 = (bf16[8,128,256]{2,1,0:T(8,128)(2,1)}, bf16[8,128,256]{2,1,0:T(8,128)(2,1)S(1)}, u32[]{:S(2)}) copy-start(bf16[8,128,256]{2,1,0:T(8,128)(2,1)S(1)} %pad_maximum_fusion.3.refs_0_) | copy-start | bytes 1572868
  55.6 50.3 %collective-permute-start.8 = (bf16[8,128,256]{2,1,0:T(8,128)(2,1)S(1)}, bf16[8,128,256]{2,1,0:T(8,128)(2,1)S(1)}, u32[]{:S(2)}, u32[]{:S(2)}) collective-permute-start(bf16[8,128,256]{2,1,0:T(8,128)(2,1)S(1)} %pad_maximum_fusion.3.refs_0_), channel_id=1, source_target_pairs={{0,4},{4,8},{8,12},{12,0},{1,5},{5,9},{9,13},{13,1},{2,6},{6,10},{... | collective-permute-start | bytes 1572872 | tf_op jit(solution)/shard_map/ppermute | solution.py:236
  59.0 46.9 %collective-permute-start.7 = (bf16[8,128,256]{2,1,0:T(8,128)(2,1)S(1)}, bf16[8,128,256]{2,1,0:T(8,128)(2,1)}, u32[]{:S(2)}, u32[]{:S(2)}) collective-permute-start(bf16[8,128,256]{2,1,0:T(8,128)(2,1)S(1)} %pad_maximum_fusion.3.refs_0_), channel_id=1, source_target_pairs={{0,8},{4,12},{8,0},{12,4},{1,9},{5,13},{9,1},{13,5},{2,10},{6,14},... | collective-permute-start | bytes 1572872 | tf_op jit(solution)/shard_map/ppermute | solution.py:236
  63.6 42.2 %collective-permute-start.6 = (bf16[8,128,256]{2,1,0:T(8,128)(2,1)S(1)}, bf16[8,128,256]{2,1,0:T(8,128)(2,1)}, u32[]{:S(2)}, u32[]{:S(2)}) collective-permute-start(bf16[8,128,256]{2,1,0:T(8,128)(2,1)S(1)} %pad_maximum_fusion.3.refs_0_), channel_id=1, source_target_pairs={{0,12},{4,0},{8,4},{12,8},{1,13},{5,1},{9,5},{13,9},{2,14},{6,2},{... | collective-permute-start | bytes 1572872 | tf_op jit(solution)/shard_map/ppermute | solution.py:236
  67.0 18.8 %collective-permute-start.4 = (f32[1,136,128]{2,1,0:T(8,128)S(1)}, f32[1,136,128]{2,1,0:T(8,128)S(1)}, u32[]{:S(2)}, u32[]{:S(2)}) collective-permute-start(f32[1,136,128]{2,1,0:T(8,128)S(1)} %add_add_fusion), channel_id=1, source_target_pairs={{0,4},{4,0},{8,12},{12,8},{1,5},{5,1},{9,13},{13,9},{2,6},{6,2},{1... | collective-permute-start | bytes 208904 | tf_op jit(solution)/shard_map/ppermute | solution.py:231
  85.7 7.7 %collective-permute-start.5 = (f32[1,136,128]{2,1,0:T(8,128)S(1)}, f32[1,136,128]{2,1,0:T(8,128)S(1)}, u32[]{:S(2)}, u32[]{:S(2)}) collective-permute-start(f32[1,136,128]{2,1,0:T(8,128)S(1)} %add.75), channel_id=1, source_target_pairs={{0,8},{4,12},{8,0},{12,4},{1,9},{5,13},{9,1},{13,5},{2,10},{6,14},... | collective-permute-start | bytes 208904 | tf_op jit(solution)/shard_map/ppermute | solution.py:231
  119.3 3.4 %copy-start.4 = (bf16[1,8,128,256]{3,2,1,0:T(8,128)(2,1)S(1)}, bf16[1,8,128,256]{3,2,1,0:T(8,128)(2,1)}, u32[]{:S(2)}) copy-start(bf16[1,8,128,256]{3,2,1,0:T(8,128)(2,1)} %get-tuple-element.11) | copy-start | bytes 1572868
  119.3 3.4 %copy-start.5 = (bf16[1,8,128,256]{3,2,1,0:T(8,128)(2,1)S(1)}, bf16[1,8,128,256]{3,2,1,0:T(8,128)(2,1)}, u32[]{:S(2)}) copy-start(bf16[1,8,128,256]{3,2,1,0:T(8,128)(2,1)} %get-tuple-element.12) | copy-start | bytes 1572868
  120.5 6.1 %collective-permute-start.9 = (bf16[8,128,1024]{2,1,0:T(8,128)(2,1)S(1)}, bf16[8,128,1024]{2,1,0:T(8,128)(2,1)S(1)}, u32[]{:S(2)}, u32[]{:S(2)}) collective-permute-start(bf16[8,128,1024]{2,1,0:T(8,128)(2,1)S(1)} %shard_map.60.level_ref), channel_id=1, source_target_pairs={{0,16},{16,0},{1,17},{17,1},{2,18},{18,2},{3,19},{19,3},{4,20},{20... | collective-permute-start | bytes 6291464 | tf_op jit(solution)/shard_map/ppermute | solution.py:231
  145.2 54.4 %all-to-all-start.3 = ((f32[16,16,128]{2,1,0:T(8,128)}), f32[16,16,128]{2,1,0:T(8,128)S(1)}, u32[]{:S(2)}, u32[]{:S(2)}) async-start(f32[16,16,128]{2,1,0:T(8,128)} %bitcast.16), calls=%async_computation.3 | async-start | bytes 262144 | tf_op jit(solution)/shard_map/all_to_all | solution.py:222
  185.0 10.6 %collective-permute-start.10 = (f32[2,128,128]{2,1,0:T(8,128)S(1)}, f32[2,128,128]{2,1,0:T(8,128)S(1)}, u32[]{:S(2)}, u32[]{:S(2)}) collective-permute-start(f32[2,128,128]{2,1,0:T(8,128)S(1)} %shard_map.57), channel_id=1, source_target_pairs={{0,1},{1,0},{2,3},{3,2},{4,5},{5,4},{6,7},{7,6},{8,9},{9,8},{10,11... | collective-permute-start | bytes 393224 | tf_op jit(solution)/shard_map/ppermute | solution.py:231

commit v5 on v4

--- a/solution.py
+++ b/solution.py
@@ -31,15 +31,15 @@
         out_ref[pair, :RANK] = jnp.where(rows >= cols, below, above)
         diagonal = jnp.sum(jnp.where(rows == cols, above, 0.0), axis=0, keepdims=True)
         out_ref[pair, RANK:] = jnp.broadcast_to(diagonal, (8, RANK))
-    copy_ref[...] = panels_ref[...]
-
-
-def local_grams(panels):
+    copy_ref[...] = panels_ref[:, panels_ref.shape[1] - copy_ref.shape[1] :]
+
+
+def local_grams(panels, late):
     return pl.pallas_call(
         gram_kernel,
         out_shape=(
             jax.ShapeDtypeStruct((SLOTS // 2, RANK + 8, RANK), jnp.float32),
-            jax.ShapeDtypeStruct(panels.shape, panels.dtype),
+            jax.ShapeDtypeStruct((panels.shape[0], late), panels.dtype),
         ),
         in_specs=[pl.BlockSpec(memory_space=pltpu.VMEM)],
         out_specs=[pl.BlockSpec(memory_space=pltpu.VMEM)] * 2,
@@ -168,9 +168,16 @@
 PAIRS = tuple((slot, slot ^ 2) for slot in range(SLOTS) if slot < slot ^ 2)
 
 
-def cross_kernel(factors_ref, level_ref, paired_ref, base_ref, out_ref):
-    for slot, other in PAIRS:
-        sums = sums_of(factors_ref, level_ref, paired_ref, base_ref, slot, other)
+def early_kernel(factors_ref, level_ref, paired_ref, base_ref, out_ref):
+    for at, (slot, other) in enumerate(PAIRS):
+        out_ref[at] = sums_of(factors_ref, level_ref, paired_ref, base_ref, slot, other)
+
+
+def cross_kernel(factors_ref, level_ref, paired_ref, base_ref, early_ref, out_ref):
+    for at, (slot, other) in enumerate(PAIRS):
+        sums = early_ref[at] + sums_of(
+            factors_ref, level_ref, paired_ref, base_ref, slot, other
+        )
         parts = []
         for _ in range(3):
             part = sums.astype(jnp.bfloat16)
@@ -242,9 +249,9 @@
     return lax.dynamic_slice_in_dim(blocks, at * count, count, 0)
 
 
-def grams(panels):
+def grams(panels, late):
     zl_at = lax.axis_index("zl")
-    packed, panels = local_grams(panels)
+    packed, panels = local_grams(panels, late)
     total = part(packed, zl_at, 1)
     for other in range(1, 4):
         total = total + swap(part(packed, zl_at ^ other, 1), "zl", other)
@@ -269,56 +276,75 @@
     return values.transpose(1, 3, 0, 2, 4, 5).reshape(-1, RANK)
 
 
-def level_kernel(place_ref, mask_ref, own_ref, paired_ref, out_ref):
+def first_kernel(place_ref, mask_ref, panels_ref, own_ref, paired_ref, out_ref):
+    columns = panels_ref.shape[1]
+    half = RANK // 2
     for slot in range(SLOTS):
-        mask = mask_ref[place_ref[0], slot].astype(jnp.float32)
-        out_ref[slot, :, :RANK] = own_ref[0, slot, 0]
+        mask = mask_ref[lax.shift_right_logical(place_ref[0], 1), slot].astype(jnp.float32)
+        out_ref[slot, :, :columns] = panels_ref[slot * RANK : (slot + 1) * RANK]
+        out_ref[slot, :half, columns:] = own_ref[0, slot, 0]
         paired = paired_ref[0, slot, 0].astype(jnp.float32) * mask
-        out_ref[slot, :, RANK:] = paired.astype(jnp.bfloat16)
-
-
-def half_level(place, self_factors, partner_factors, link_mask):
+        out_ref[slot, half:, columns:] = paired.astype(jnp.bfloat16)
+
+
+def first_part(place, panels, self_factors, partner_factors, link_mask, columns):
     half = RANK // 2
     spec = pl.BlockSpec(
-        (1, SLOTS, 1, half, RANK), lambda i, place: (place[0], 0, place[1], 0, 0)
-    )
-    shape = SLOTS, half, 2 * RANK
+        (1, SLOTS, 1, half, RANK),
+        lambda i, place: (lax.shift_right_logical(place[0], 1), 0, place[0] & 1, 0, 0),
+    )
+    shape = SLOTS, RANK, columns + RANK
     split = LEVELS, SLOTS, 2, half, RANK
     return pl.pallas_call(
-        level_kernel,
-        out_shape=jax.ShapeDtypeStruct(shape, self_factors.dtype),
+        first_kernel,
+        out_shape=jax.ShapeDtypeStruct(shape, panels.dtype),
         grid_spec=pltpu.PrefetchScalarGridSpec(
             num_scalar_prefetch=1,
             grid=(1,),
-            in_specs=[pl.BlockSpec(memory_space=pltpu.SMEM), spec, spec],
+            in_specs=[
+                pl.BlockSpec(memory_space=pltpu.SMEM),
+                pl.BlockSpec((panels.shape[0], columns), lambda i, place: (0, 0)),
+                spec,
+                spec,
+            ],
             out_specs=pl.BlockSpec(shape, lambda i, place: (0, 0, 0)),
         ),
         compiler_params=pltpu.CompilerParams(vmem_limit_bytes=60 * 2**20),
-    )(place, link_mask, self_factors.reshape(split), partner_factors.reshape(split))
+    )(place, link_mask, panels, self_factors.reshape(split), partner_factors.reshape(split))
 
 
 def body(panels, self_factors, partner_factors, link_mask, block_ranks):
     columns = panels.shape[1]
+    early = columns // 8
+    late = columns - early
+    half = RANK // 2
     zl_at = lax.axis_index("zl")
     odd = zl_at % 2
-    place = jnp.stack([lax.axis_index("x"), odd]).astype(jnp.int32)
-
-    own_half = exchange(half_level(place, self_factors, partner_factors, link_mask), PEERS)
+    place = (lax.axis_index("x") * 2 + odd).astype(jnp.int32).reshape(1)
+
+    first = first_part(place, panels, self_factors, partner_factors, link_mask, early)
+    first = exchange(first, PEERS)
+    own_half = first[:, :, early:]
     other_half = swap(own_half, "zl", 1)
-    gram, panels = grams(panels)
-    panels = once_done(panels, other_half, gram).reshape(SLOTS, RANK, columns)
-    base = exchange(panels, PEERS)
+    gram, panels = grams(panels, late)
+    second = once_done(panels, other_half, gram).reshape(SLOTS, RANK, late)
+    second = exchange(second, PEERS)
 
     gram = gram + swap(gram, "x", 1)
     gram = gram + swap(gram, "x", 2)
     inverse = invert(zl_at.astype(jnp.int32).reshape(1), block_ranks, gram)
-    halves = [jnp.where(odd == at, own_half, other_half) for at in range(2)]
-    factors = by_place(along_x(jnp.concatenate(halves, axis=1), inverse))
+    low, high = (jnp.where(odd == at, own_half, other_half) for at in range(2))
+    factors = [jnp.concatenate([low[:, i], high[:, i]], axis=1) for i in (slice(half), slice(half, RANK))]
+    factors = by_place(along_x(jnp.concatenate(factors, axis=2), inverse))
     lower, upper = jnp.stack(factors[:2]), jnp.stack(factors[2:])
 
-    level = near_levels(base, lower, columns)
+    level = near_levels(first, lower, early)
     paired = swap(level, "core", 1)
-    cross = sums_call(cross_kernel, (2, 4, 4, 32, RANK), upper, level, paired, base)
+    shape = len(PAIRS), 2 * RANK, 2 * RANK
+    sums = sums_call(early_kernel, shape, upper, level, paired, first)
+    level = near_levels(second, lower, late, sums)
+    paired = swap(level, "core", 1)
+    cross = sums_call(cross_kernel, (2, 4, 4, 32, RANK), upper, level, paired, second, sums)
 
     cross = exchange(cross.reshape(2 * 4, 4, 32, RANK), ("yl", "x"))
     cross = cross.reshape(2, 4, 4, 2, 16, RANK).sum(1)

time: 216 us -> 212 us (0.981)
  waiting for transfers between devices: 52.7 us -> 48.6 us
    ppermute x8 -> x9, starting transfers between devices: 32.2 us -> 41.8 us  [swap(): lax.ppermute(block, axis, [(i, i ^ bit) for i in range(lax.axis_size(axis...]
    all_to_all x3, starting transfers between devices: 61.2 us -> 51.9 us  [exchange(): return lax.all_to_all(blocks, axes, 0, 0, tiled=True)]
    all_to_all x3, waiting for transfers between devices: 19.5 us -> 16.6 us  [exchange(): return lax.all_to_all(blocks, axes, 0, 0, tiled=True)]
    ppermute x8 -> x9, waiting for transfers between devices: 33.1 us -> 32 us  [swap(): lax.ppermute(block, axis, [(i, i ^ bit) for i in range(lax.axis_size(axis...]
  transfers between devices with their start and end apart: 14 -> 15, of which waited for: 8 -> 9; matrix products, arithmetic and copies ran while one was open for 2% -> 2% of each run, Pallas kernels for 6% -> 7%
where the time goes in v5:
time: 212 us; the launch traced here: 210 us
  starting transfers between devices  104 us (49%)
  waiting for transfers between devices  48.6 us (23%)
  blocking collectives  27.9 us (13%)
  Pallas kernels  20.4 us (10%)
  local copies, waits for them, and re-layouts  6.19 us (3%)
  other arithmetic  2.45 us (1%)
    all_to_all x3, starting transfers between devices, exchange(): return lax.all_to_all(blocks, axes, 0, 0, tiled=True)  51.9 us
    ppermute x9, starting transfers between devices, swap(): lax.ppermute(block, axis, [(i, i ^ bit) for i in range(lax.axis_size(axis...  41.8 us
    ppermute x9, waiting for transfers between devices, swap(): lax.ppermute(block, axis, [(i, i ^ bit) for i in range(lax.axis_size(axis...  32 us
    all_to_all x2, blocking collectives, exchange(): return lax.all_to_all(blocks, axes, 0, 0, tiled=True)  27.9 us
    all_to_all x3, waiting for transfers between devices, exchange(): return lax.all_to_all(blocks, axes, 0, 0, tiled=True)  16.6 us
    pallas_call x1, Pallas kernels, invert(): pl.pallas_call(invert_kernel, out_shape=jax.ShapeDtypeStruct((2, RANK, RA...  11.7 us
    ppermute x3, starting transfers between devices, along_x(): lax.ppermute(block, 'x', [(i, (i - d) % count) for i in range(count)])  10.2 us
  transfers between devices with their start and end apart: 15, of which 9 were waited for; matrix products, arithmetic and copies ran while one was open for 2% of the time, Pallas kernels for 7%

profile of v5, /device:TPU:24, one launch (start us, length us, event | category | flops | bytes accessed | tf_op | source)
XLA Modules:
  0.0 210.3 jit_solution(11420940656543164178)
XLA Ops:
  2.1 16.5 %all-to-all-start = ((bf16[8,128,256]{2,1,0:T(8,128)(2,1)}), bf16[8,128,256]{2,1,0:T(8,128)(2,1)S(1)}, u32[]{:S(2)}, u32[]{:S(2)}) async-start(bf16[8,128,256]{2,1,0:T(8,128)(2,1)} %shard_map.55), calls=%async_computation | async-start | bytes 1048576 | tf_op jit(solution)/shard_map/all_to_all | solution.py:229
  20.7 2.9 %collective-permute-start.1 = (f32[1,136,128]{2,1,0:T(8,128)S(1)}, f32[1,136,128]{2,1,0:T(8,128)S(1)}, u32[]{:S(2)}, u32[]{:S(2)}) collective-permute-start(f32[1,136,128]{2,1,0:T(8,128)S(1)} %get-tuple-element.15), channel_id=1, source_target_pairs={{0,1},{1,0},{2,3},{3,2},{4,5},{5,4},{6,7},{7,6},{8,9},{9,8},{10,11... | collective-permute-start | bytes 208904 | tf_op jit(solution)/shard_map/ppermute | solution.py:238
  23.6 3.4 %collective-permute-start.2 = (f32[1,136,128]{2,1,0:T(8,128)S(1)}, f32[1,136,128]{2,1,0:T(8,128)S(1)}, u32[]{:S(2)}, u32[]{:S(2)}) collective-permute-start(f32[1,136,128]{2,1,0:T(8,128)S(1)} %get-tuple-element.17), channel_id=1, source_target_pairs={{0,2},{1,3},{2,0},{3,1},{4,6},{5,7},{6,4},{7,5},{8,10},{9,11},{10,... | collective-permute-start | bytes 208904 | tf_op jit(solution)/shard_map/ppermute | solution.py:238
  27.0 3.8 %collective-permute-start.3 = (f32[1,136,128]{2,1,0:T(8,128)S(1)}, f32[1,136,128]{2,1,0:T(8,128)S(1)}, u32[]{:S(2)}, u32[]{:S(2)}) collective-permute-start(f32[1,136,128]{2,1,0:T(8,128)S(1)} %get-tuple-element.16), channel_id=1, source_target_pairs={{0,3},{1,2},{2,1},{3,0},{4,7},{5,6},{6,5},{7,4},{8,11},{9,10},{10,... | collective-permute-start | bytes 208904 | tf_op jit(solution)/shard_map/ppermute | solution.py:238
  30.8 9.7 %all-to-all-done.base_ref = bf16[8,128,256]{2,1,0:T(8,128)(2,1)S(1)} async-done(((bf16[8,128,256]{2,1,0:T(8,128)(2,1)}), bf16[8,128,256]{2,1,0:T(8,128)(2,1)S(1)}, u32[]{:S(2)}, u32[]{:S(2)}) %all-to-all-start) | async-done | bytes 524320 | tf_op jit(solution)/shard_map/all_to_all | solution.py:229
  40.5 14.8 %collective-permute-start = (bf16[8,128,128]{2,1,0:T(8,128)(2,1)S(1)}, bf16[8,128,128]{2,1,0:T(8,128)(2,1)S(1)}, u32[]{:S(2)}, u32[]{:S(2)}) collective-permute-start(bf16[8,128,128]{2,1,0:T(8,128)(2,1)S(1)} %slice.44), channel_id=1, source_target_pairs={{0,1},{1,0},{2,3},{3,2},{4,5},{5,4},{6,7},{7,6},{8,9},{9,8},{10,11... | collective-permute-start | bytes 786440 | tf_op jit(solution)/shard_map/ppermute | solution.py:238
  56.0 3.7 %collective-permute-done = bf16[8,128,128]{2,1,0:T(8,128)(2,1)S(1)} collective-permute-done((bf16[8,128,128]{2,1,0:T(8,128)(2,1)S(1)}, bf16[8,128,128]{2,1,0:T(8,128)(2,1)S(1)}, u32[]{:S(2)}, u32[]{:S(2)}) %collective-permute-start) | collective-permute-done | bytes 262176 | tf_op jit(solution)/shard_map/ppermute | solution.py:238
  60.2 5.5 %all-to-all-start.1 = ((bf16[8,128,896]{2,1,0:T(8,128)(2,1)}), bf16[8,128,896]{2,1,0:T(8,128)(2,1)S(1)}, u32[]{:S(2)}, u32[]{:S(2)}) async-start(bf16[8,128,896]{2,1,0:T(8,128)(2,1)} %bitcast.42), calls=%async_computation.1 | async-start | bytes 3670016 | tf_op jit(solution)/shard_map/all_to_all | solution.py:229
  65.9 4.7 %collective-permute-start.6 = (bf16[8,128,256]{2,1,0:T(8,128)(2,1)S(1)}, bf16[8,128,256]{2,1,0:T(8,128)(2,1)S(1)}, u32[]{:S(2)}, u32[]{:S(2)}) collective-permute-start(bf16[8,128,256]{2,1,0:T(8,128)(2,1)S(1)} %maximum_maximum_fusion.refs_0_), channel_id=1, source_target_pairs={{0,12},{4,0},{8,4},{12,8},{1,13},{5,1},{9,5},{13,9},{2,14},{6,2},{... | collective-permute-start | bytes 1572872 | tf_op jit(solution)/shard_map/ppermute | solution.py:243
  70.5 2.7 %collective-permute-start.7 = (bf16[8,128,256]{2,1,0:T(8,128)(2,1)S(1)}, bf16[8,128,256]{2,1,0:T(8,128)(2,1)}, u32[]{:S(2)}, u32[]{:S(2)}) collective-permute-start(bf16[8,128,256]{2,1,0:T(8,128)(2,1)S(1)} %maximum_maximum_fusion.refs_0_), channel_id=1, source_target_pairs={{0,8},{4,12},{8,0},{12,4},{1,9},{5,13},{9,1},{13,5},{2,10},{6,14},... | collective-permute-start | bytes 1572872 | tf_op jit(solution)/shard_map/ppermute | solution.py:243
  73.3 2.8 %collective-permute-start.8 = (bf16[8,128,256]{2,1,0:T(8,128)(2,1)S(1)}, bf16[8,128,256]{2,1,0:T(8,128)(2,1)}, u32[]{:S(2)}, u32[]{:S(2)}) collective-permute-start(bf16[8,128,256]{2,1,0:T(8,128)(2,1)S(1)} %maximum_maximum_fusion.refs_0_), channel_id=1, source_target_pairs={{0,4},{4,8},{8,12},{12,0},{1,5},{5,9},{9,13},{13,1},{2,6},{6,10},{... | collective-permute-start | bytes 1572872 | tf_op jit(solution)/shard_map/ppermute | solution.py:243
  76.1 3.7 %collective-permute-start.4 = (f32[1,136,128]{2,1,0:T(8,128)S(1)}, f32[1,136,128]{2,1,0:T(8,128)S(1)}, u32[]{:S(2)}, u32[]{:S(2)}) collective-permute-start(f32[1,136,128]{2,1,0:T(8,128)S(1)} %add_add_fusion), channel_id=1, source_target_pairs={{0,4},{4,0},{8,12},{12,8},{1,5},{5,1},{9,13},{13,9},{2,6},{6,2},{1... | collective-permute-start | bytes 208904 | tf_op jit(solution)/shard_map/ppermute | solution.py:238
  79.8 14.4 %collective-permute-done.4 = f32[1,136,128]{2,1,0:T(8,128)S(1)} collective-permute-done((f32[1,136,128]{2,1,0:T(8,128)S(1)}, f32[1,136,128]{2,1,0:T(8,128)S(1)}, u32[]{:S(2)}, u32[]{:S(2)}) %collective-permute-start.4) | collective-permute-done | bytes 69664 | tf_op jit(solution)/shard_map/ppermute | solution.py:238
  94.2 5.4 %collective-permute-start.5 = (f32[1,136,128]{2,1,0:T(8,128)S(1)}, f32[1,136,128]{2,1,0:T(8,128)S(1)}, u32[]{:S(2)}, u32[]{:S(2)}) collective-permute-start(f32[1,136,128]{2,1,0:T(8,128)S(1)} %add.79), channel_id=1, source_target_pairs={{0,8},{4,12},{8,0},{12,4},{1,9},{5,13},{9,1},{13,5},{2,10},{6,14},... | collective-permute-start | bytes 208904 | tf_op jit(solution)/shard_map/ppermute | solution.py:238
  102.0 11.7 %shard_map.57 = f32[2,128,128]{2,1,0:T(8,128)S(1)} custom-call(s32[1]{0:T(128)} %bitcast.3.place_ref, s32[8]{0:T(128)S(1)} %copy-done.6, f32[1,136,128]{2,1,0:T(8,128)S(1)} %add.80.packed_ref), custom_call_target="tpu_custom_call" | custom-call | tf_op jit(solution)/shard_map/pallas_call | solution.py:98
  121.9 2.9 %all-to-all-done.1.base_ref = bf16[8,128,896]{2,1,0:T(8,128)(2,1)S(1)} async-done(((bf16[8,128,896]{2,1,0:T(8,128)(2,1)}), bf16[8,128,896]{2,1,0:T(8,128)(2,1)S(1)}, u32[]{:S(2)}, u32[]{:S(2)}) %all-to-all-start.1) | async-done | bytes 1835040 | tf_op jit(solution)/shard_map/all_to_all | solution.py:229
  128.2 3.6 %collective-permute-done.10.paired_ref = bf16[8,128,896]{2,1,0:T(8,128)(2,1)S(1)} collective-permute-done((bf16[8,128,896]{2,1,0:T(8,128)(2,1)S(1)}, bf16[8,128,896]{2,1,0:T(8,128)(2,1)S(1)}, u32[]{:S(2)}, u32[]{:S(2)}) %collective-permute-start.10) | collective-permute-done | bytes 1835040 | tf_op jit(solution)/shard_map/ppermute | solution.py:238
  131.8 3.4 %shard_map.63 = f32[2,4,4,32,128]{4,3,2,1,0:T(8,128)S(1)} custom-call(bf16[2,8,128,256]{3,2,1,0:T(8,128)(2,1)S(1)} %copy-done.1, bf16[8,128,896]{2,1,0:T(8,128)(2,1)S(1)} %shard_map.62.level_ref, bf16[8,128,896]{2,1,0:T(8,128)(2,1)S(1)} %collective-permute-done.10.paired_ref, bf16[8,128,896]{2,1,0:T(8,128)(2,1)S(1)} %all-to-all-done.1.base_ref, ...), custom_call_target="tpu_custom_call" | custom-call | tf_op jit(solution)/shard_map/pallas_call | solution.py:199
  135.2 14.5 %all_to_all.25 = f32[8,4,32,128]{3,2,1,0:T(8,128)S(1)} all-to-all(f32[8,4,32,128]{3,2,1,0:T(8,128)S(1)} %bitcast.43), channel_id=1, replica_groups=mesh['yh'=2,'yl'=2,'zh'=4,'core'=2,'x'=4,'zl'=4] {'yl','x'}, dimensions={0} | all-to-all | bytes 1048576 | tf_op jit(solution)/shard_map/all_to_all | solution.py:229
  150.4 29.9 %all-to-all-start.3 = ((f32[16,16,128]{2,1,0:T(8,128)}), f32[16,16,128]{2,1,0:T(8,128)S(1)}, u32[]{:S(2)}, u32[]{:S(2)}) async-start(f32[16,16,128]{2,1,0:T(8,128)} %bitcast.16), calls=%async_computation.3 | async-start | bytes 262144 | tf_op jit(solution)/shard_map/all_to_all | solution.py:229
  180.3 3.8 %collective-permute-start.11 = (f32[2,128,128]{2,1,0:T(8,128)S(1)}, f32[2,128,128]{2,1,0:T(8,128)S(1)}, u32[]{:S(2)}, u32[]{:S(2)}) collective-permute-start(f32[2,128,128]{2,1,0:T(8,128)S(1)} %shard_map.57), channel_id=1, source_target_pairs={{0,1},{1,0},{2,3},{3,2},{4,5},{5,4},{6,7},{7,6},{8,9},{9,8},{10,11... | collective-permute-start | bytes 393224 | tf_op jit(solution)/shard_map/ppermute | solution.py:238
  184.2 6.7 %collective-permute-done.11 = f32[2,128,128]{2,1,0:T(8,128)S(1)} collective-permute-done((f32[2,128,128]{2,1,0:T(8,128)S(1)}, f32[2,128,128]{2,1,0:T(8,128)S(1)}, u32[]{:S(2)}, u32[]{:S(2)}) %collective-permute-start.11) | collective-permute-done | bytes 131104 | tf_op jit(solution)/shard_map/ppermute | solution.py:238
  190.9 4.0 %all-to-all-done.3 = f32[16,16,128]{2,1,0:T(8,128)S(1)} async-done(((f32[16,16,128]{2,1,0:T(8,128)}), f32[16,16,128]{2,1,0:T(8,128)S(1)}, u32[]{:S(2)}, u32[]{:S(2)}) %all-to-all-start.3) | async-done | bytes 131104 | tf_op jit(solution)/shard_map/all_to_all | solution.py:229
  195.6 13.4 %all_to_all.26 = f16[16,5,16,128]{3,2,1,0:T(8,128)(2,1)S(1)} all-to-all(f16[16,5,16,128]{3,2,1,0:T(8,128)(2,1)S(1)} %broadcast_in_dim.5), channel_id=1, replica_groups=mesh['yh'=2,'yl'=2,'zh'=4,'core'=2,'x'=4,'zl'=4] {'x','zl'}, dimensions={0} | all-to-all | bytes 655360 | tf_op jit(solution)/shard_map/all_to_all | solution.py:229
  (64 shorter events, 22.0 us)
Async XLA Ops:
  0.0 18.6 %copy-start.2 = (bf16[1024,1024]{1,0:T(8,128)(2,1)S(1)}, bf16[1024,1024]{1,0:T(8,128)(2,1)}, u32[]{:S(2)}) copy-start(bf16[1024,1024]{1,0:T(8,128)(2,1)} %panels_ref.3) | copy-start | bytes 6291460
  2.1 38.4 %all-to-all-start = ((bf16[8,128,256]{2,1,0:T(8,128)(2,1)}), bf16[8,128,256]{2,1,0:T(8,128)(2,1)S(1)}, u32[]{:S(2)}, u32[]{:S(2)}) async-start(bf16[8,128,256]{2,1,0:T(8,128)(2,1)} %shard_map.55), calls=%async_computation | async-start | bytes 1048576 | tf_op jit(solution)/shard_map/all_to_all | solution.py:229
  19.4 1.3 copy-start.3
  20.7 34.6 %collective-permute-start.1 = (f32[1,136,128]{2,1,0:T(8,128)S(1)}, f32[1,136,128]{2,1,0:T(8,128)S(1)}, u32[]{:S(2)}, u32[]{:S(2)}) collective-permute-start(f32[1,136,128]{2,1,0:T(8,128)S(1)} %get-tuple-element.15), channel_id=1, source_target_pairs={{0,1},{1,0},{2,3},{3,2},{4,5},{5,4},{6,7},{7,6},{8,9},{9,8},{10,11... | collective-permute-start | bytes 208904 | tf_op jit(solution)/shard_map/ppermute | solution.py:238
  23.6 31.7 %collective-permute-start.2 = (f32[1,136,128]{2,1,0:T(8,128)S(1)}, f32[1,136,128]{2,1,0:T(8,128)S(1)}, u32[]{:S(2)}, u32[]{:S(2)}) collective-permute-start(f32[1,136,128]{2,1,0:T(8,128)S(1)} %get-tuple-element.17), channel_id=1, source_target_pairs={{0,2},{1,3},{2,0},{3,1},{4,6},{5,7},{6,4},{7,5},{8,10},{9,11},{10,... | collective-permute-start | bytes 208904 | tf_op jit(solution)/shard_map/ppermute | solution.py:238
  27.0 28.3 %collective-permute-start.3 = (f32[1,136,128]{2,1,0:T(8,128)S(1)}, f32[1,136,128]{2,1,0:T(8,128)S(1)}, u32[]{:S(2)}, u32[]{:S(2)}) collective-permute-start(f32[1,136,128]{2,1,0:T(8,128)S(1)} %get-tuple-element.16), channel_id=1, source_target_pairs={{0,3},{1,2},{2,1},{3,0},{4,7},{5,6},{6,5},{7,4},{8,11},{9,10},{10,... | collective-permute-start | bytes 208904 | tf_op jit(solution)/shard_map/ppermute | solution.py:238
  40.5 19.1 %collective-permute-start = (bf16[8,128,128]{2,1,0:T(8,128)(2,1)S(1)}, bf16[8,128,128]{2,1,0:T(8,128)(2,1)S(1)}, u32[]{:S(2)}, u32[]{:S(2)}) collective-permute-start(bf16[8,128,128]{2,1,0:T(8,128)(2,1)S(1)} %slice.44), channel_id=1, source_target_pairs={{0,1},{1,0},{2,3},{3,2},{4,5},{5,4},{6,7},{7,6},{8,9},{9,8},{10,11... | collective-permute-start | bytes 786440 | tf_op jit(solution)/shard_map/ppermute | solution.py:238
  60.2 64.6 %all-to-all-start.1 = ((bf16[8,128,896]{2,1,0:T(8,128)(2,1)}), bf16[8,128,896]{2,1,0:T(8,128)(2,1)S(1)}, u32[]{:S(2)}, u32[]{:S(2)}) async-start(bf16[8,128,896]{2,1,0:T(8,128)(2,1)} %bitcast.42), calls=%async_computation.1 | async-start | bytes 3670016 | tf_op jit(solution)/shard_map/all_to_all | solution.py:229
  65.7 36.3 %copy-start.6 = (s32[8]{0:T(128)S(1)}, s32[8]{0:T(128)}, u32[]{:S(2)}) copy-start(s32[8]{0:T(128)} %ranks_ref.1) | copy-start | bytes 100
  65.9 48.5 %copy-start.7 = (bf16[8,128,256]{2,1,0:T(8,128)(2,1)}, bf16[8,128,256]{2,1,0:T(8,128)(2,1)S(1)}, u32[]{:S(2)}) copy-start(bf16[8,128,256]{2,1,0:T(8,128)(2,1)S(1)} %maximum_maximum_fusion.refs_0_) | copy-start | bytes 1572868
  65.9 48.4 %collective-permute-start.6 = (bf16[8,128,256]{2,1,0:T(8,128)(2,1)S(1)}, bf16[8,128,256]{2,1,0:T(8,128)(2,1)S(1)}, u32[]{:S(2)}, u32[]{:S(2)}) collective-permute-start(bf16[8,128,256]{2,1,0:T(8,128)(2,1)S(1)} %maximum_maximum_fusion.refs_0_), channel_id=1, source_target_pairs={{0,12},{4,0},{8,4},{12,8},{1,13},{5,1},{9,5},{13,9},{2,14},{6,2},{... | collective-permute-start | bytes 1572872 | tf_op jit(solution)/shard_map/ppermute | solution.py:243
  70.5 43.8 %collective-permute-start.7 = (bf16[8,128,256]{2,1,0:T(8,128)(2,1)S(1)}, bf16[8,128,256]{2,1,0:T(8,128)(2,1)}, u32[]{:S(2)}, u32[]{:S(2)}) collective-permute-start(bf16[8,128,256]{2,1,0:T(8,128)(2,1)S(1)} %maximum_maximum_fusion.refs_0_), channel_id=1, source_target_pairs={{0,8},{4,12},{8,0},{12,4},{1,9},{5,13},{9,1},{13,5},{2,10},{6,14},... | collective-permute-start | bytes 1572872 | tf_op jit(solution)/shard_map/ppermute | solution.py:243
  73.3 41.0 %collective-permute-start.8 = (bf16[8,128,256]{2,1,0:T(8,128)(2,1)S(1)}, bf16[8,128,256]{2,1,0:T(8,128)(2,1)}, u32[]{:S(2)}, u32[]{:S(2)}) collective-permute-start(bf16[8,128,256]{2,1,0:T(8,128)(2,1)S(1)} %maximum_maximum_fusion.refs_0_), channel_id=1, source_target_pairs={{0,4},{4,8},{8,12},{12,0},{1,5},{5,9},{9,13},{13,1},{2,6},{6,10},{... | collective-permute-start | bytes 1572872 | tf_op jit(solution)/shard_map/ppermute | solution.py:243
  76.1 18.1 %collective-permute-start.4 = (f32[1,136,128]{2,1,0:T(8,128)S(1)}, f32[1,136,128]{2,1,0:T(8,128)S(1)}, u32[]{:S(2)}, u32[]{:S(2)}) collective-permute-start(f32[1,136,128]{2,1,0:T(8,128)S(1)} %add_add_fusion), channel_id=1, source_target_pairs={{0,4},{4,0},{8,12},{12,8},{1,5},{5,1},{9,13},{13,9},{2,6},{6,2},{1... | collective-permute-start | bytes 208904 | tf_op jit(solution)/shard_map/ppermute | solution.py:238
  94.2 7.7 %collective-permute-start.5 = (f32[1,136,128]{2,1,0:T(8,128)S(1)}, f32[1,136,128]{2,1,0:T(8,128)S(1)}, u32[]{:S(2)}, u32[]{:S(2)}) collective-permute-start(f32[1,136,128]{2,1,0:T(8,128)S(1)} %add.79), channel_id=1, source_target_pairs={{0,8},{4,12},{8,0},{12,4},{1,9},{5,13},{9,1},{13,5},{2,10},{6,14},... | collective-permute-start | bytes 208904 | tf_op jit(solution)/shard_map/ppermute | solution.py:238
  116.9 3.4 %collective-permute-start.9 = (bf16[8,128,128]{2,1,0:T(8,128)(2,1)S(1)}, bf16[8,128,128]{2,1,0:T(8,128)(2,1)S(1)}, u32[]{:S(2)}, u32[]{:S(2)}) collective-permute-start(bf16[8,128,128]{2,1,0:T(8,128)(2,1)S(1)} %shard_map.60.level_ref), channel_id=1, source_target_pairs={{0,16},{16,0},{1,17},{17,1},{2,18},{18,2},{3,19},{19,3},{4,20},{20... | collective-permute-start | bytes 786440 | tf_op jit(solution)/shard_map/ppermute | solution.py:238
  118.9 2.0 copy-start
  120.9 1.0 copy-start.4
  124.8 6.9 %copy-start.1 = (bf16[2,8,128,256]{3,2,1,0:T(8,128)(2,1)S(1)}, bf16[2,8,128,256]{3,2,1,0:T(8,128)(2,1)}, u32[]{:S(2)}) copy-start(bf16[2,8,128,256]{3,2,1,0:T(8,128)(2,1)} %copy-done) | copy-start | bytes 3145732
  124.8 6.9 %copy-start.5 = (f32[4,256,256]{2,1,0:T(8,128)S(1)}, f32[4,256,256]{2,1,0:T(8,128)}, u32[]{:S(2)}) copy-start(f32[4,256,256]{2,1,0:T(8,128)} %copy-done.4) | copy-start | bytes 3145732
  126.1 5.7 %collective-permute-start.10 = (bf16[8,128,896]{2,1,0:T(8,128)(2,1)S(1)}, bf16[8,128,896]{2,1,0:T(8,128)(2,1)S(1)}, u32[]{:S(2)}, u32[]{:S(2)}) collective-permute-start(bf16[8,128,896]{2,1,0:T(8,128)(2,1)S(1)} %shard_map.62.level_ref), channel_id=1, source_target_pairs={{0,16},{16,0},{1,17},{17,1},{2,18},{18,2},{3,19},{19,3},{4,20},{20... | collective-permute-start | bytes 5505032 | tf_op jit(solution)/shard_map/ppermute | solution.py:238
  150.4 44.5 %all-to-all-start.3 = ((f32[16,16,128]{2,1,0:T(8,128)}), f32[16,16,128]{2,1,0:T(8,128)S(1)}, u32[]{:S(2)}, u32[]{:S(2)}) async-start(f32[16,16,128]{2,1,0:T(8,128)} %bitcast.16), calls=%async_computation.3 | async-start | bytes 262144 | tf_op jit(solution)/shard_map/all_to_all | solution.py:229
  180.3 10.6 %collective-permute-start.11 = (f32[2,128,128]{2,1,0:T(8,128)S(1)}, f32[2,128,128]{2,1,0:T(8,128)S(1)}, u32[]{:S(2)}, u32[]{:S(2)}) collective-permute-start(f32[2,128,128]{2,1,0:T(8,128)S(1)} %shard_map.57), channel_id=1, source_target_pairs={{0,1},{1,0},{2,3},{3,2},{4,5},{5,4},{6,7},{7,6},{8,9},{9,8},{10,11... | collective-permute-start | bytes 393224 | tf_op jit(solution)/shard_map/ppermute | solution.py:238

commit v6 on v5

--- a/solution.py
+++ b/solution.py
@@ -189,7 +189,8 @@
         )
         for side, block in enumerate((slot, other)):
             side_of = slice(side * RANK, (side + 1) * RANK)
-            cross = sum(matmul(factor[side], part[:, side_of]) for part in parts[::-1])
+            cross = matmul(factor[side], jnp.concatenate([part[:, side_of] for part in parts], axis=1))
+            cross = cross[:, 2 * RANK :] + cross[:, RANK : 2 * RANK] + cross[:, :RANK]
             for x in range(4):
                 out_ref[block // 4, x, block % 4] = cross[32 * x : 32 * x + 32]
 
@@ -267,11 +268,13 @@
     blocks, rows, _ = solved.shape
     top = jnp.max(jnp.abs(solved), axis=2)
     power = jnp.clip(jnp.floor(jnp.log2(jnp.maximum(top, 1e-36))), -120.0, 120.0)
-    values = (solved * jnp.exp2(-power)[:, :, None]).astype(jnp.float16)
-    powers = jnp.pad(power.T.astype(jnp.float16), ((0, 0), (0, RANK - blocks)))
-    sent = gather(jnp.concatenate([values, powers[None]], axis=0), COL)
-    power = sent[:, blocks, :, :blocks].astype(jnp.float32).transpose(0, 2, 1)
-    values = sent[:, :blocks].astype(jnp.float32) * jnp.exp2(power)[:, :, :, None]
+    values = (solved * jnp.exp2(-power)[:, :, None]).astype(jnp.float16).reshape(-1, 8, RANK)
+    powers = power.astype(jnp.float16).reshape(1, 1, blocks * rows)
+    powers = jnp.pad(powers, ((0, 0), (0, 7), (0, RANK - blocks * rows)))
+    sent = gather(jnp.concatenate([values, powers], axis=0), COL)
+    power = sent[:, -1, 0, : blocks * rows].astype(jnp.float32).reshape(-1, blocks, rows)
+    values = sent[:, :-1].astype(jnp.float32).reshape(-1, blocks, rows, RANK)
+    values = values * jnp.exp2(power)[:, :, :, None]
     values = values.reshape(4, 2, 2, blocks, rows, RANK)
     return values.transpose(1, 3, 0, 2, 4, 5).reshape(-1, RANK)
 

time: 212 us -> 211 us (level)
  no operation moved by 1% of the time
where the time goes in v6:
time: 211 us; the launch traced here: 210 us
  starting transfers between devices  104 us (49%)
  waiting for transfers between devices  48.6 us (23%)
  blocking collectives  27.6 us (13%)
  Pallas kernels  20.2 us (10%)
  local copies, waits for them, and re-layouts  6.18 us (3%)
  other arithmetic  2.43 us (1%)
    all_to_all x3, starting transfers between devices, exchange(): return lax.all_to_all(blocks, axes, 0, 0, tiled=True)  51.9 us
    ppermute x9, starting transfers between devices, swap(): lax.ppermute(block, axis, [(i, i ^ bit) for i in range(lax.axis_size(axis...  41.8 us
    ppermute x9, waiting for transfers between devices, swap(): lax.ppermute(block, axis, [(i, i ^ bit) for i in range(lax.axis_size(axis...  32 us
    all_to_all x2, blocking collectives, exchange(): return lax.all_to_all(blocks, axes, 0, 0, tiled=True)  27.6 us
    all_to_all x3, waiting for transfers between devices, exchange(): return lax.all_to_all(blocks, axes, 0, 0, tiled=True)  16.6 us
    pallas_call x1, Pallas kernels, invert(): pl.pallas_call(invert_kernel, out_shape=jax.ShapeDtypeStruct((2, RANK, RA...  11.7 us
    ppermute x3, starting transfers between devices, along_x(): lax.ppermute(block, 'x', [(i, (i - d) % count) for i in range(count)])  10.2 us
  transfers between devices with their start and end apart: 15, of which 9 were waited for; matrix products, arithmetic and copies ran while one was open for 2% of the time, Pallas kernels for 7%

profile of v6, /device:TPU:24, one launch (start us, length us, event | category | flops | bytes accessed | tf_op | source)
XLA Modules:
  0.0 209.7 jit_solution(1214758254275544646)
XLA Ops:
  2.1 16.5 %all-to-all-start = ((bf16[8,128,256]{2,1,0:T(8,128)(2,1)}), bf16[8,128,256]{2,1,0:T(8,128)(2,1)S(1)}, u32[]{:S(2)}, u32[]{:S(2)}) async-start(bf16[8,128,256]{2,1,0:T(8,128)(2,1)} %shard_map.55), calls=%async_computation | async-start | bytes 1048576 | tf_op jit(solution)/shard_map/all_to_all | solution.py:230
  20.7 2.9 %collective-permute-start.1 = (f32[1,136,128]{2,1,0:T(8,128)S(1)}, f32[1,136,128]{2,1,0:T(8,128)S(1)}, u32[]{:S(2)}, u32[]{:S(2)}) collective-permute-start(f32[1,136,128]{2,1,0:T(8,128)S(1)} %get-tuple-element.15), channel_id=1, source_target_pairs={{0,1},{1,0},{2,3},{3,2},{4,5},{5,4},{6,7},{7,6},{8,9},{9,8},{10,11... | collective-permute-start | bytes 208904 | tf_op jit(solution)/shard_map/ppermute | solution.py:239
  23.6 3.4 %collective-permute-start.2 = (f32[1,136,128]{2,1,0:T(8,128)S(1)}, f32[1,136,128]{2,1,0:T(8,128)S(1)}, u32[]{:S(2)}, u32[]{:S(2)}) collective-permute-start(f32[1,136,128]{2,1,0:T(8,128)S(1)} %get-tuple-element.17), channel_id=1, source_target_pairs={{0,2},{1,3},{2,0},{3,1},{4,6},{5,7},{6,4},{7,5},{8,10},{9,11},{10,... | collective-permute-start | bytes 208904 | tf_op jit(solution)/shard_map/ppermute | solution.py:239
  27.0 3.8 %collective-permute-start.3 = (f32[1,136,128]{2,1,0:T(8,128)S(1)}, f32[1,136,128]{2,1,0:T(8,128)S(1)}, u32[]{:S(2)}, u32[]{:S(2)}) collective-permute-start(f32[1,136,128]{2,1,0:T(8,128)S(1)} %get-tuple-element.16), channel_id=1, source_target_pairs={{0,3},{1,2},{2,1},{3,0},{4,7},{5,6},{6,5},{7,4},{8,11},{9,10},{10,... | collective-permute-start | bytes 208904 | tf_op jit(solution)/shard_map/ppermute | solution.py:239
  30.8 9.6 %all-to-all-done.base_ref = bf16[8,128,256]{2,1,0:T(8,128)(2,1)S(1)} async-done(((bf16[8,128,256]{2,1,0:T(8,128)(2,1)}), bf16[8,128,256]{2,1,0:T(8,128)(2,1)S(1)}, u32[]{:S(2)}, u32[]{:S(2)}) %all-to-all-start) | async-done | bytes 524320 | tf_op jit(solution)/shard_map/all_to_all | solution.py:230
  40.5 14.8 %collective-permute-start = (bf16[8,128,128]{2,1,0:T(8,128)(2,1)S(1)}, bf16[8,128,128]{2,1,0:T(8,128)(2,1)S(1)}, u32[]{:S(2)}, u32[]{:S(2)}) collective-permute-start(bf16[8,128,128]{2,1,0:T(8,128)(2,1)S(1)} %slice.44), channel_id=1, source_target_pairs={{0,1},{1,0},{2,3},{3,2},{4,5},{5,4},{6,7},{7,6},{8,9},{9,8},{10,11... | collective-permute-start | bytes 786440 | tf_op jit(solution)/shard_map/ppermute | solution.py:239
  56.0 3.7 %collective-permute-done = bf16[8,128,128]{2,1,0:T(8,128)(2,1)S(1)} collective-permute-done((bf16[8,128,128]{2,1,0:T(8,128)(2,1)S(1)}, bf16[8,128,128]{2,1,0:T(8,128)(2,1)S(1)}, u32[]{:S(2)}, u32[]{:S(2)}) %collective-permute-start) | collective-permute-done | bytes 262176 | tf_op jit(solution)/shard_map/ppermute | solution.py:239
  60.2 5.5 %all-to-all-start.1 = ((bf16[8,128,896]{2,1,0:T(8,128)(2,1)}), bf16[8,128,896]{2,1,0:T(8,128)(2,1)S(1)}, u32[]{:S(2)}, u32[]{:S(2)}) async-start(bf16[8,128,896]{2,1,0:T(8,128)(2,1)} %bitcast.36), calls=%async_computation.1 | async-start | bytes 3670016 | tf_op jit(solution)/shard_map/all_to_all | solution.py:230
  65.9 4.7 %collective-permute-start.6 = (bf16[8,128,256]{2,1,0:T(8,128)(2,1)S(1)}, bf16[8,128,256]{2,1,0:T(8,128)(2,1)S(1)}, u32[]{:S(2)}, u32[]{:S(2)}) collective-permute-start(bf16[8,128,256]{2,1,0:T(8,128)(2,1)S(1)} %maximum_maximum_fusion.refs_0_), channel_id=1, source_target_pairs={{0,12},{4,0},{8,4},{12,8},{1,13},{5,1},{9,5},{13,9},{2,14},{6,2},{... | collective-permute-start | bytes 1572872 | tf_op jit(solution)/shard_map/ppermute | solution.py:244
  70.5 2.7 %collective-permute-start.7 = (bf16[8,128,256]{2,1,0:T(8,128)(2,1)S(1)}, bf16[8,128,256]{2,1,0:T(8,128)(2,1)}, u32[]{:S(2)}, u32[]{:S(2)}) collective-permute-start(bf16[8,128,256]{2,1,0:T(8,128)(2,1)S(1)} %maximum_maximum_fusion.refs_0_), channel_id=1, source_target_pairs={{0,8},{4,12},{8,0},{12,4},{1,9},{5,13},{9,1},{13,5},{2,10},{6,14},... | collective-permute-start | bytes 1572872 | tf_op jit(solution)/shard_map/ppermute | solution.py:244
  73.2 2.8 %collective-permute-start.8 = (bf16[8,128,256]{2,1,0:T(8,128)(2,1)S(1)}, bf16[8,128,256]{2,1,0:T(8,128)(2,1)}, u32[]{:S(2)}, u32[]{:S(2)}) collective-permute-start(bf16[8,128,256]{2,1,0:T(8,128)(2,1)S(1)} %maximum_maximum_fusion.refs_0_), channel_id=1, source_target_pairs={{0,4},{4,8},{8,12},{12,0},{1,5},{5,9},{9,13},{13,1},{2,6},{6,10},{... | collective-permute-start | bytes 1572872 | tf_op jit(solution)/shard_map/ppermute | solution.py:244
  76.1 3.7 %collective-permute-start.4 = (f32[1,136,128]{2,1,0:T(8,128)S(1)}, f32[1,136,128]{2,1,0:T(8,128)S(1)}, u32[]{:S(2)}, u32[]{:S(2)}) collective-permute-start(f32[1,136,128]{2,1,0:T(8,128)S(1)} %add_add_fusion), channel_id=1, source_target_pairs={{0,4},{4,0},{8,12},{12,8},{1,5},{5,1},{9,13},{13,9},{2,6},{6,2},{1... | collective-permute-start | bytes 208904 | tf_op jit(solution)/shard_map/ppermute | solution.py:239
  79.8 14.4 %collective-permute-done.4 = f32[1,136,128]{2,1,0:T(8,128)S(1)} collective-permute-done((f32[1,136,128]{2,1,0:T(8,128)S(1)}, f32[1,136,128]{2,1,0:T(8,128)S(1)}, u32[]{:S(2)}, u32[]{:S(2)}) %collective-permute-start.4) | collective-permute-done | bytes 69664 | tf_op jit(solution)/shard_map/ppermute | solution.py:239
  94.2 5.4 %collective-permute-start.5 = (f32[1,136,128]{2,1,0:T(8,128)S(1)}, f32[1,136,128]{2,1,0:T(8,128)S(1)}, u32[]{:S(2)}, u32[]{:S(2)}) collective-permute-start(f32[1,136,128]{2,1,0:T(8,128)S(1)} %add.79), channel_id=1, source_target_pairs={{0,8},{4,12},{8,0},{12,4},{1,9},{5,13},{9,1},{13,5},{2,10},{6,14},... | collective-permute-start | bytes 208904 | tf_op jit(solution)/shard_map/ppermute | solution.py:239
  101.9 11.7 %shard_map.57 = f32[2,128,128]{2,1,0:T(8,128)S(1)} custom-call(s32[1]{0:T(128)} %bitcast.3.place_ref, s32[8]{0:T(128)S(1)} %copy-done.6, f32[1,136,128]{2,1,0:T(8,128)S(1)} %add.80.packed_ref), custom_call_target="tpu_custom_call" | custom-call | tf_op jit(solution)/shard_map/pallas_call | solution.py:98
  121.9 2.9 %all-to-all-done.1.base_ref = bf16[8,128,896]{2,1,0:T(8,128)(2,1)S(1)} async-done(((bf16[8,128,896]{2,1,0:T(8,128)(2,1)}), bf16[8,128,896]{2,1,0:T(8,128)(2,1)S(1)}, u32[]{:S(2)}, u32[]{:S(2)}) %all-to-all-start.1) | async-done | bytes 1835040 | tf_op jit(solution)/shard_map/all_to_all | solution.py:230
  128.2 3.6 %collective-permute-done.10.paired_ref = bf16[8,128,896]{2,1,0:T(8,128)(2,1)S(1)} collective-permute-done((bf16[8,128,896]{2,1,0:T(8,128)(2,1)S(1)}, bf16[8,128,896]{2,1,0:T(8,128)(2,1)S(1)}, u32[]{:S(2)}, u32[]{:S(2)}) %collective-permute-start.10) | collective-permute-done | bytes 1835040 | tf_op jit(solution)/shard_map/ppermute | solution.py:239
  131.8 3.1 %shard_map.63 = f32[2,4,4,32,128]{4,3,2,1,0:T(8,128)S(1)} custom-call(bf16[2,8,128,256]{3,2,1,0:T(8,128)(2,1)S(1)} %copy-done.1, bf16[8,128,896]{2,1,0:T(8,128)(2,1)S(1)} %shard_map.62.level_ref, bf16[8,128,896]{2,1,0:T(8,128)(2,1)S(1)} %collective-permute-done.10.paired_ref, bf16[8,128,896]{2,1,0:T(8,128)(2,1)S(1)} %all-to-all-done.1.base_ref, ...), custom_call_target="tpu_custom_call" | custom-call | tf_op jit(solution)/shard_map/pallas_call | solution.py:200
  134.9 14.5 %all_to_all.25 = f32[8,4,32,128]{3,2,1,0:T(8,128)S(1)} all-to-all(f32[8,4,32,128]{3,2,1,0:T(8,128)S(1)} %bitcast.37), channel_id=1, replica_groups=mesh['yh'=2,'yl'=2,'zh'=4,'core'=2,'x'=4,'zl'=4] {'yl','x'}, dimensions={0} | all-to-all | bytes 1048576 | tf_op jit(solution)/shard_map/all_to_all | solution.py:230
  150.1 29.9 %all-to-all-start.3 = ((f32[16,16,128]{2,1,0:T(8,128)}), f32[16,16,128]{2,1,0:T(8,128)S(1)}, u32[]{:S(2)}, u32[]{:S(2)}) async-start(f32[16,16,128]{2,1,0:T(8,128)} %bitcast.16), calls=%async_computation.3 | async-start | bytes 262144 | tf_op jit(solution)/shard_map/all_to_all | solution.py:230
  180.0 3.8 %collective-permute-start.11 = (f32[2,128,128]{2,1,0:T(8,128)S(1)}, f32[2,128,128]{2,1,0:T(8,128)S(1)}, u32[]{:S(2)}, u32[]{:S(2)}) collective-permute-start(f32[2,128,128]{2,1,0:T(8,128)S(1)} %shard_map.57), channel_id=1, source_target_pairs={{0,1},{1,0},{2,3},{3,2},{4,5},{5,4},{6,7},{7,6},{8,9},{9,8},{10,11... | collective-permute-start | bytes 393224 | tf_op jit(solution)/shard_map/ppermute | solution.py:239
  183.9 6.7 %collective-permute-done.11 = f32[2,128,128]{2,1,0:T(8,128)S(1)} collective-permute-done((f32[2,128,128]{2,1,0:T(8,128)S(1)}, f32[2,128,128]{2,1,0:T(8,128)S(1)}, u32[]{:S(2)}, u32[]{:S(2)}) %collective-permute-start.11) | collective-permute-done | bytes 131104 | tf_op jit(solution)/shard_map/ppermute | solution.py:239
  190.6 4.0 %all-to-all-done.3 = f32[16,16,128]{2,1,0:T(8,128)S(1)} async-done(((f32[16,16,128]{2,1,0:T(8,128)}), f32[16,16,128]{2,1,0:T(8,128)S(1)}, u32[]{:S(2)}, u32[]{:S(2)}) %all-to-all-start.3) | async-done | bytes 131104 | tf_op jit(solution)/shard_map/all_to_all | solution.py:230
  195.3 13.1 %all_to_all.26 = f16[16,9,8,128]{3,2,1,0:T(8,128)(2,1)S(1)} all-to-all(f16[16,9,8,128]{3,2,1,0:T(8,128)(2,1)S(1)} %broadcast_in_dim.2), channel_id=1, replica_groups=mesh['yh'=2,'yl'=2,'zh'=4,'core'=2,'x'=4,'zl'=4] {'x','zl'}, dimensions={0} | all-to-all | bytes 589824 | tf_op jit(solution)/shard_map/all_to_all | solution.py:230
  (64 shorter events, 22.0 us)
Async XLA Ops:
  0.0 18.6 %copy-start.2 = (bf16[1024,1024]{1,0:T(8,128)(2,1)S(1)}, bf16[1024,1024]{1,0:T(8,128)(2,1)}, u32[]{:S(2)}) copy-start(bf16[1024,1024]{1,0:T(8,128)(2,1)} %panels_ref.3) | copy-start | bytes 6291460
  2.1 38.4 %all-to-all-start = ((bf16[8,128,256]{2,1,0:T(8,128)(2,1)}), bf16[8,128,256]{2,1,0:T(8,128)(2,1)S(1)}, u32[]{:S(2)}, u32[]{:S(2)}) async-start(bf16[8,128,256]{2,1,0:T(8,128)(2,1)} %shard_map.55), calls=%async_computation | async-start | bytes 1048576 | tf_op jit(solution)/shard_map/all_to_all | solution.py:230
  19.4 1.3 copy-start.3
  20.7 34.6 %collective-permute-start.1 = (f32[1,136,128]{2,1,0:T(8,128)S(1)}, f32[1,136,128]{2,1,0:T(8,128)S(1)}, u32[]{:S(2)}, u32[]{:S(2)}) collective-permute-start(f32[1,136,128]{2,1,0:T(8,128)S(1)} %get-tuple-element.15), channel_id=1, source_target_pairs={{0,1},{1,0},{2,3},{3,2},{4,5},{5,4},{6,7},{7,6},{8,9},{9,8},{10,11... | collective-permute-start | bytes 208904 | tf_op jit(solution)/shard_map/ppermute | solution.py:239
  23.6 31.7 %collective-permute-start.2 = (f32[1,136,128]{2,1,0:T(8,128)S(1)}, f32[1,136,128]{2,1,0:T(8,128)S(1)}, u32[]{:S(2)}, u32[]{:S(2)}) collective-permute-start(f32[1,136,128]{2,1,0:T(8,128)S(1)} %get-tuple-element.17), channel_id=1, source_target_pairs={{0,2},{1,3},{2,0},{3,1},{4,6},{5,7},{6,4},{7,5},{8,10},{9,11},{10,... | collective-permute-start | bytes 208904 | tf_op jit(solution)/shard_map/ppermute | solution.py:239
  27.0 28.3 %collective-permute-start.3 = (f32[1,136,128]{2,1,0:T(8,128)S(1)}, f32[1,136,128]{2,1,0:T(8,128)S(1)}, u32[]{:S(2)}, u32[]{:S(2)}) collective-permute-start(f32[1,136,128]{2,1,0:T(8,128)S(1)} %get-tuple-element.16), channel_id=1, source_target_pairs={{0,3},{1,2},{2,1},{3,0},{4,7},{5,6},{6,5},{7,4},{8,11},{9,10},{10,... | collective-permute-start | bytes 208904 | tf_op jit(solution)/shard_map/ppermute | solution.py:239
  40.5 19.1 %collective-permute-start = (bf16[8,128,128]{2,1,0:T(8,128)(2,1)S(1)}, bf16[8,128,128]{2,1,0:T(8,128)(2,1)S(1)}, u32[]{:S(2)}, u32[]{:S(2)}) collective-permute-start(bf16[8,128,128]{2,1,0:T(8,128)(2,1)S(1)} %slice.44), channel_id=1, source_target_pairs={{0,1},{1,0},{2,3},{3,2},{4,5},{5,4},{6,7},{7,6},{8,9},{9,8},{10,11... | collective-permute-start | bytes 786440 | tf_op jit(solution)/shard_map/ppermute | solution.py:239
  60.2 64.6 %all-to-all-start.1 = ((bf16[8,128,896]{2,1,0:T(8,128)(2,1)}), bf16[8,128,896]{2,1,0:T(8,128)(2,1)S(1)}, u32[]{:S(2)}, u32[]{:S(2)}) async-start(bf16[8,128,896]{2,1,0:T(8,128)(2,1)} %bitcast.36), calls=%async_computation.1 | async-start | bytes 3670016 | tf_op jit(solution)/shard_map/all_to_all | solution.py:230
  65.7 36.3 %copy-start.6 = (s32[8]{0:T(128)S(1)}, s32[8]{0:T(128)}, u32[]{:S(2)}) copy-start(s32[8]{0:T(128)} %ranks_ref.1) | copy-start | bytes 100
  65.8 48.5 %copy-start.7 = (bf16[8,128,256]{2,1,0:T(8,128)(2,1)}, bf16[8,128,256]{2,1,0:T(8,128)(2,1)S(1)}, u32[]{:S(2)}) copy-start(bf16[8,128,256]{2,1,0:T(8,128)(2,1)S(1)} %maximum_maximum_fusion.refs_0_) | copy-start | bytes 1572868
  65.9 48.4 %collective-permute-start.6 = (bf16[8,128,256]{2,1,0:T(8,128)(2,1)S(1)}, bf16[8,128,256]{2,1,0:T(8,128)(2,1)S(1)}, u32[]{:S(2)}, u32[]{:S(2)}) collective-permute-start(bf16[8,128,256]{2,1,0:T(8,128)(2,1)S(1)} %maximum_maximum_fusion.refs_0_), channel_id=1, source_target_pairs={{0,12},{4,0},{8,4},{12,8},{1,13},{5,1},{9,5},{13,9},{2,14},{6,2},{... | collective-permute-start | bytes 1572872 | tf_op jit(solution)/shard_map/ppermute | solution.py:244
  70.5 43.8 %collective-permute-start.7 = (bf16[8,128,256]{2,1,0:T(8,128)(2,1)S(1)}, bf16[8,128,256]{2,1,0:T(8,128)(2,1)}, u32[]{:S(2)}, u32[]{:S(2)}) collective-permute-start(bf16[8,128,256]{2,1,0:T(8,128)(2,1)S(1)} %maximum_maximum_fusion.refs_0_), channel_id=1, source_target_pairs={{0,8},{4,12},{8,0},{12,4},{1,9},{5,13},{9,1},{13,5},{2,10},{6,14},... | collective-permute-start | bytes 1572872 | tf_op jit(solution)/shard_map/ppermute | solution.py:244
  73.2 41.0 %collective-permute-start.8 = (bf16[8,128,256]{2,1,0:T(8,128)(2,1)S(1)}, bf16[8,128,256]{2,1,0:T(8,128)(2,1)}, u32[]{:S(2)}, u32[]{:S(2)}) collective-permute-start(bf16[8,128,256]{2,1,0:T(8,128)(2,1)S(1)} %maximum_maximum_fusion.refs_0_), channel_id=1, source_target_pairs={{0,4},{4,8},{8,12},{12,0},{1,5},{5,9},{9,13},{13,1},{2,6},{6,10},{... | collective-permute-start | bytes 1572872 | tf_op jit(solution)/shard_map/ppermute | solution.py:244
  76.1 18.1 %collective-permute-start.4 = (f32[1,136,128]{2,1,0:T(8,128)S(1)}, f32[1,136,128]{2,1,0:T(8,128)S(1)}, u32[]{:S(2)}, u32[]{:S(2)}) collective-permute-start(f32[1,136,128]{2,1,0:T(8,128)S(1)} %add_add_fusion), channel_id=1, source_target_pairs={{0,4},{4,0},{8,12},{12,8},{1,5},{5,1},{9,13},{13,9},{2,6},{6,2},{1... | collective-permute-start | bytes 208904 | tf_op jit(solution)/shard_map/ppermute | solution.py:239
  94.2 7.7 %collective-permute-start.5 = (f32[1,136,128]{2,1,0:T(8,128)S(1)}, f32[1,136,128]{2,1,0:T(8,128)S(1)}, u32[]{:S(2)}, u32[]{:S(2)}) collective-permute-start(f32[1,136,128]{2,1,0:T(8,128)S(1)} %add.79), channel_id=1, source_target_pairs={{0,8},{4,12},{8,0},{12,4},{1,9},{5,13},{9,1},{13,5},{2,10},{6,14},... | collective-permute-start | bytes 208904 | tf_op jit(solution)/shard_map/ppermute | solution.py:239
  116.9 3.4 %collective-permute-start.9 = (bf16[8,128,128]{2,1,0:T(8,128)(2,1)S(1)}, bf16[8,128,128]{2,1,0:T(8,128)(2,1)S(1)}, u32[]{:S(2)}, u32[]{:S(2)}) collective-permute-start(bf16[8,128,128]{2,1,0:T(8,128)(2,1)S(1)} %shard_map.60.level_ref), channel_id=1, source_target_pairs={{0,16},{16,0},{1,17},{17,1},{2,18},{18,2},{3,19},{19,3},{4,20},{20... | collective-permute-start | bytes 786440 | tf_op jit(solution)/shard_map/ppermute | solution.py:239
  118.9 2.0 copy-start
  120.9 1.0 copy-start.4
  124.8 6.9 %copy-start.1 = (bf16[2,8,128,256]{3,2,1,0:T(8,128)(2,1)S(1)}, bf16[2,8,128,256]{3,2,1,0:T(8,128)(2,1)}, u32[]{:S(2)}) copy-start(bf16[2,8,128,256]{3,2,1,0:T(8,128)(2,1)} %copy-done) | copy-start | bytes 3145732
  124.8 6.9 %copy-start.5 = (f32[4,256,256]{2,1,0:T(8,128)S(1)}, f32[4,256,256]{2,1,0:T(8,128)}, u32[]{:S(2)}) copy-start(f32[4,256,256]{2,1,0:T(8,128)} %copy-done.4) | copy-start | bytes 3145732
  126.1 5.7 %collective-permute-start.10 = (bf16[8,128,896]{2,1,0:T(8,128)(2,1)S(1)}, bf16[8,128,896]{2,1,0:T(8,128)(2,1)S(1)}, u32[]{:S(2)}, u32[]{:S(2)}) collective-permute-start(bf16[8,128,896]{2,1,0:T(8,128)(2,1)S(1)} %shard_map.62.level_ref), channel_id=1, source_target_pairs={{0,16},{16,0},{1,17},{17,1},{2,18},{18,2},{3,19},{19,3},{4,20},{20... | collective-permute-start | bytes 5505032 | tf_op jit(solution)/shard_map/ppermute | solution.py:239
  150.1 44.5 %all-to-all-start.3 = ((f32[16,16,128]{2,1,0:T(8,128)}), f32[16,16,128]{2,1,0:T(8,128)S(1)}, u32[]{:S(2)}, u32[]{:S(2)}) async-start(f32[16,16,128]{2,1,0:T(8,128)} %bitcast.16), calls=%async_computation.3 | async-start | bytes 262144 | tf_op jit(solution)/shard_map/all_to_all | solution.py:230
  180.0 10.5 %collective-permute-start.11 = (f32[2,128,128]{2,1,0:T(8,128)S(1)}, f32[2,128,128]{2,1,0:T(8,128)S(1)}, u32[]{:S(2)}, u32[]{:S(2)}) collective-permute-start(f32[2,128,128]{2,1,0:T(8,128)S(1)} %shard_map.57), channel_id=1, source_target_pairs={{0,1},{1,0},{2,3},{3,2},{4,5},{5,4},{6,7},{7,6},{8,9},{9,8},{10,11... | collective-permute-start | bytes 393224 | tf_op jit(solution)/shard_map/ppermute | solution.py:239

commit v7 on v6

--- a/solution.py
+++ b/solution.py
@@ -318,7 +318,7 @@
 
 def body(panels, self_factors, partner_factors, link_mask, block_ranks):
     columns = panels.shape[1]
-    early = columns // 8
+    early = columns // 4
     late = columns - early
     half = RANK // 2
     zl_at = lax.axis_index("zl")

time: 211 us -> 212 us (level)
  starting transfers between devices: 104 us -> 96.7 us
  waiting for transfers between devices: 48.6 us -> 53 us
  local copies, waits for them, and re-layouts: 6.18 us -> 8.8 us
    all_to_all x3, starting transfers between devices: 51.9 us -> 42.1 us  [exchange(): return lax.all_to_all(blocks, axes, 0, 0, tiled=True)]
    all_to_all x3, waiting for transfers between devices: 16.6 us -> 20.8 us  [exchange(): return lax.all_to_all(blocks, axes, 0, 0, tiled=True)]
    unnamed x16, local copies, waits for them, and re-layouts: 2.28 us -> 4.95 us
    ppermute x9, starting transfers between devices: 41.8 us -> 44.4 us  [swap(): lax.ppermute(block, axis, [(i, i ^ bit) for i in range(lax.axis_size(axis...]
  transfers between devices with their start and end apart: 15 -> 15, of which waited for: 9 -> 8; matrix products, arithmetic and copies ran while one was open for 2% -> 2% of each run, Pallas kernels for 7% -> 6%
where the time goes in v7:
time: 212 us; the launch traced here: 210 us
  starting transfers between devices  96.7 us (46%)
  waiting for transfers between devices  53 us (25%)
  blocking collectives  29 us (14%)
  Pallas kernels  19.3 us (9%)
  local copies, waits for them, and re-layouts  8.8 us (4%)
  other arithmetic  2.43 us (1%)
    ppermute x9, starting transfers between devices, swap(): lax.ppermute(block, axis, [(i, i ^ bit) for i in range(lax.axis_size(axis...  44.4 us
    all_to_all x3, starting transfers between devices, exchange(): return lax.all_to_all(blocks, axes, 0, 0, tiled=True)  42.1 us
    ppermute x9, waiting for transfers between devices, swap(): lax.ppermute(block, axis, [(i, i ^ bit) for i in range(lax.axis_size(axis...  32.2 us
    all_to_all x2, blocking collectives, exchange(): return lax.all_to_all(blocks, axes, 0, 0, tiled=True)  29 us
    all_to_all x3, waiting for transfers between devices, exchange(): return lax.all_to_all(blocks, axes, 0, 0, tiled=True)  20.8 us
    pallas_call x1, Pallas kernels, invert(): pl.pallas_call(invert_kernel, out_shape=jax.ShapeDtypeStruct((2, RANK, RA...  11.7 us
    ppermute x3, starting transfers between devices, along_x(): lax.ppermute(block, 'x', [(i, (i - d) % count) for i in range(count)])  10.2 us
    unnamed x16, local copies, waits for them, and re-layouts  4.95 us
  transfers between devices with their start and end apart: 15, of which 8 were waited for; matrix products, arithmetic and copies ran while one was open for 2% of the time, Pallas kernels for 6%

profile of v7, /device:TPU:24, one launch (start us, length us, event | category | flops | bytes accessed | tf_op | source)
XLA Modules:
  0.0 210.2 jit_solution(16950108118911719642)
XLA Ops:
  2.1 16.5 %all-to-all-start = ((bf16[8,128,384]{2,1,0:T(8,128)(2,1)}), bf16[8,128,384]{2,1,0:T(8,128)(2,1)S(1)}, u32[]{:S(2)}, u32[]{:S(2)}) async-start(bf16[8,128,384]{2,1,0:T(8,128)(2,1)} %shard_map.55), calls=%async_computation | async-start | bytes 1572864 | tf_op jit(solution)/shard_map/all_to_all | solution.py:230
  22.1 2.9 %collective-permute-start.1 = (f32[1,136,128]{2,1,0:T(8,128)S(1)}, f32[1,136,128]{2,1,0:T(8,128)S(1)}, u32[]{:S(2)}, u32[]{:S(2)}) collective-permute-start(f32[1,136,128]{2,1,0:T(8,128)S(1)} %get-tuple-element.15), channel_id=1, source_target_pairs={{0,1},{1,0},{2,3},{3,2},{4,5},{5,4},{6,7},{7,6},{8,9},{9,8},{10,11... | collective-permute-start | bytes 208904 | tf_op jit(solution)/shard_map/ppermute | solution.py:239
  25.1 3.4 %collective-permute-start.2 = (f32[1,136,128]{2,1,0:T(8,128)S(1)}, f32[1,136,128]{2,1,0:T(8,128)S(1)}, u32[]{:S(2)}, u32[]{:S(2)}) collective-permute-start(f32[1,136,128]{2,1,0:T(8,128)S(1)} %get-tuple-element.17), channel_id=1, source_target_pairs={{0,2},{1,3},{2,0},{3,1},{4,6},{5,7},{6,4},{7,5},{8,10},{9,11},{10,... | collective-permute-start | bytes 208904 | tf_op jit(solution)/shard_map/ppermute | solution.py:239
  28.5 3.8 %collective-permute-start.3 = (f32[1,136,128]{2,1,0:T(8,128)S(1)}, f32[1,136,128]{2,1,0:T(8,128)S(1)}, u32[]{:S(2)}, u32[]{:S(2)}) collective-permute-start(f32[1,136,128]{2,1,0:T(8,128)S(1)} %get-tuple-element.16), channel_id=1, source_target_pairs={{0,3},{1,2},{2,1},{3,0},{4,7},{5,6},{6,5},{7,4},{8,11},{9,10},{10,... | collective-permute-start | bytes 208904 | tf_op jit(solution)/shard_map/ppermute | solution.py:239
  32.3 16.8 %all-to-all-done.base_ref = bf16[8,128,384]{2,1,0:T(8,128)(2,1)S(1)} async-done(((bf16[8,128,384]{2,1,0:T(8,128)(2,1)}), bf16[8,128,384]{2,1,0:T(8,128)(2,1)S(1)}, u32[]{:S(2)}, u32[]{:S(2)}) %all-to-all-start) | async-done | bytes 786464 | tf_op jit(solution)/shard_map/all_to_all | solution.py:230
  49.1 17.3 %collective-permute-start = (bf16[8,128,128]{2,1,0:T(8,128)(2,1)S(1)}, bf16[8,128,128]{2,1,0:T(8,128)(2,1)S(1)}, u32[]{:S(2)}, u32[]{:S(2)}) collective-permute-start(bf16[8,128,128]{2,1,0:T(8,128)(2,1)S(1)} %slice.44), channel_id=1, source_target_pairs={{0,1},{1,0},{2,3},{3,2},{4,5},{5,4},{6,7},{7,6},{8,9},{9,8},{10,11... | collective-permute-start | bytes 786440 | tf_op jit(solution)/shard_map/ppermute | solution.py:239
  67.1 3.7 %collective-permute-done = bf16[8,128,128]{2,1,0:T(8,128)(2,1)S(1)} collective-permute-done((bf16[8,128,128]{2,1,0:T(8,128)(2,1)S(1)}, bf16[8,128,128]{2,1,0:T(8,128)(2,1)S(1)}, u32[]{:S(2)}, u32[]{:S(2)}) %collective-permute-start) | collective-permute-done | bytes 262176 | tf_op jit(solution)/shard_map/ppermute | solution.py:239
  71.3 5.9 %all-to-all-start.1 = ((bf16[8,128,768]{2,1,0:T(8,128)(2,1)}), bf16[8,128,768]{2,1,0:T(8,128)(2,1)S(1)}, u32[]{:S(2)}, u32[]{:S(2)}) async-start(bf16[8,128,768]{2,1,0:T(8,128)(2,1)} %bitcast.36), calls=%async_computation.1 | async-start | bytes 3145728 | tf_op jit(solution)/shard_map/all_to_all | solution.py:230
  77.4 4.7 %collective-permute-start.6 = (bf16[8,128,256]{2,1,0:T(8,128)(2,1)S(1)}, bf16[8,128,256]{2,1,0:T(8,128)(2,1)S(1)}, u32[]{:S(2)}, u32[]{:S(2)}) collective-permute-start(bf16[8,128,256]{2,1,0:T(8,128)(2,1)S(1)} %maximum_maximum_fusion.refs_0_), channel_id=1, source_target_pairs={{0,12},{4,0},{8,4},{12,8},{1,13},{5,1},{9,5},{13,9},{2,14},{6,2},{... | collective-permute-start | bytes 1572872 | tf_op jit(solution)/shard_map/ppermute | solution.py:244
  82.0 2.7 %collective-permute-start.7 = (bf16[8,128,256]{2,1,0:T(8,128)(2,1)S(1)}, bf16[8,128,256]{2,1,0:T(8,128)(2,1)}, u32[]{:S(2)}, u32[]{:S(2)}) collective-permute-start(bf16[8,128,256]{2,1,0:T(8,128)(2,1)S(1)} %maximum_maximum_fusion.refs_0_), channel_id=1, source_target_pairs={{0,8},{4,12},{8,0},{12,4},{1,9},{5,13},{9,1},{13,5},{2,10},{6,14},... | collective-permute-start | bytes 1572872 | tf_op jit(solution)/shard_map/ppermute | solution.py:244
  84.7 2.8 %collective-permute-start.8 = (bf16[8,128,256]{2,1,0:T(8,128)(2,1)S(1)}, bf16[8,128,256]{2,1,0:T(8,128)(2,1)}, u32[]{:S(2)}, u32[]{:S(2)}) collective-permute-start(bf16[8,128,256]{2,1,0:T(8,128)(2,1)S(1)} %maximum_maximum_fusion.refs_0_), channel_id=1, source_target_pairs={{0,4},{4,8},{8,12},{12,0},{1,5},{5,9},{9,13},{13,1},{2,6},{6,10},{... | collective-permute-start | bytes 1572872 | tf_op jit(solution)/shard_map/ppermute | solution.py:244
  87.6 3.7 %collective-permute-start.4 = (f32[1,136,128]{2,1,0:T(8,128)S(1)}, f32[1,136,128]{2,1,0:T(8,128)S(1)}, u32[]{:S(2)}, u32[]{:S(2)}) collective-permute-start(f32[1,136,128]{2,1,0:T(8,128)S(1)} %add_add_fusion), channel_id=1, source_target_pairs={{0,4},{4,0},{8,12},{12,8},{1,5},{5,1},{9,13},{13,9},{2,6},{6,2},{1... | collective-permute-start | bytes 208904 | tf_op jit(solution)/shard_map/ppermute | solution.py:239
  91.3 14.7 %collective-permute-done.4 = f32[1,136,128]{2,1,0:T(8,128)S(1)} collective-permute-done((f32[1,136,128]{2,1,0:T(8,128)S(1)}, f32[1,136,128]{2,1,0:T(8,128)S(1)}, u32[]{:S(2)}, u32[]{:S(2)}) %collective-permute-start.4) | collective-permute-done | bytes 69664 | tf_op jit(solution)/shard_map/ppermute | solution.py:239
  106.0 5.4 %collective-permute-start.5 = (f32[1,136,128]{2,1,0:T(8,128)S(1)}, f32[1,136,128]{2,1,0:T(8,128)S(1)}, u32[]{:S(2)}, u32[]{:S(2)}) collective-permute-start(f32[1,136,128]{2,1,0:T(8,128)S(1)} %add.79), channel_id=1, source_target_pairs={{0,8},{4,12},{8,0},{12,4},{1,9},{5,13},{9,1},{13,5},{2,10},{6,14},... | collective-permute-start | bytes 208904 | tf_op jit(solution)/shard_map/ppermute | solution.py:239
  111.5 2.3 %collective-permute-done.5 = f32[1,136,128]{2,1,0:T(8,128)S(1)} collective-permute-done((f32[1,136,128]{2,1,0:T(8,128)S(1)}, f32[1,136,128]{2,1,0:T(8,128)S(1)}, u32[]{:S(2)}, u32[]{:S(2)}) %collective-permute-start.5) | collective-permute-done | bytes 69664 | tf_op jit(solution)/shard_map/ppermute | solution.py:239
  113.8 11.7 %shard_map.57 = f32[2,128,128]{2,1,0:T(8,128)S(1)} custom-call(s32[1]{0:T(128)} %bitcast.3.place_ref, s32[8]{0:T(128)S(1)} %copy-done.6, f32[1,136,128]{2,1,0:T(8,128)S(1)} %add.80.packed_ref), custom_call_target="tpu_custom_call" | custom-call | tf_op jit(solution)/shard_map/pallas_call | solution.py:98
  138.4 3.1 %collective-permute-done.10.paired_ref = bf16[8,128,768]{2,1,0:T(8,128)(2,1)S(1)} collective-permute-done((bf16[8,128,768]{2,1,0:T(8,128)(2,1)S(1)}, bf16[8,128,768]{2,1,0:T(8,128)(2,1)S(1)}, u32[]{:S(2)}, u32[]{:S(2)}) %collective-permute-start.10) | collective-permute-done | bytes 1572896 | tf_op jit(solution)/shard_map/ppermute | solution.py:239
  141.5 2.7 %shard_map.63 = f32[2,4,4,32,128]{4,3,2,1,0:T(8,128)S(1)} custom-call(bf16[2,8,128,256]{3,2,1,0:T(8,128)(2,1)S(1)} %pad_maximum_fusion.1.factors_ref, bf16[8,128,768]{2,1,0:T(8,128)(2,1)S(1)} %shard_map.62.level_ref, bf16[8,128,768]{2,1,0:T(8,128)(2,1)S(1)} %collective-permute-done.10.paired_ref, bf16[8,128,768]{2,1,0:T(8,128)(2,1)S(1)} %all-to-all-done.1.base_ref, ...), custom_call_target="tpu_custom_call" | custom-call | tf_op jit(solution)/shard_map/pallas_call | solution.py:200
  144.2 15.9 %all_to_all.25 = f32[8,4,32,128]{3,2,1,0:T(8,128)S(1)} all-to-all(f32[8,4,32,128]{3,2,1,0:T(8,128)S(1)} %bitcast.37), channel_id=1, replica_groups=mesh['yh'=2,'yl'=2,'zh'=4,'core'=2,'x'=4,'zl'=4] {'yl','x'}, dimensions={0} | all-to-all | bytes 1048576 | tf_op jit(solution)/shard_map/all_to_all | solution.py:230
  160.9 19.7 %all-to-all-start.3 = ((f32[16,16,128]{2,1,0:T(8,128)}), f32[16,16,128]{2,1,0:T(8,128)S(1)}, u32[]{:S(2)}, u32[]{:S(2)}) async-start(f32[16,16,128]{2,1,0:T(8,128)} %bitcast.16), calls=%async_computation.3 | async-start | bytes 262144 | tf_op jit(solution)/shard_map/all_to_all | solution.py:230
  180.5 3.8 %collective-permute-start.11 = (f32[2,128,128]{2,1,0:T(8,128)S(1)}, f32[2,128,128]{2,1,0:T(8,128)S(1)}, u32[]{:S(2)}, u32[]{:S(2)}) collective-permute-start(f32[2,128,128]{2,1,0:T(8,128)S(1)} %shard_map.57), channel_id=1, source_target_pairs={{0,1},{1,0},{2,3},{3,2},{4,5},{5,4},{6,7},{7,6},{8,9},{9,8},{10,11... | collective-permute-start | bytes 393224 | tf_op jit(solution)/shard_map/ppermute | solution.py:239
  184.4 6.7 %collective-permute-done.11 = f32[2,128,128]{2,1,0:T(8,128)S(1)} collective-permute-done((f32[2,128,128]{2,1,0:T(8,128)S(1)}, f32[2,128,128]{2,1,0:T(8,128)S(1)}, u32[]{:S(2)}, u32[]{:S(2)}) %collective-permute-start.11) | collective-permute-done | bytes 131104 | tf_op jit(solution)/shard_map/ppermute | solution.py:239
  191.1 4.0 %all-to-all-done.3 = f32[16,16,128]{2,1,0:T(8,128)S(1)} async-done(((f32[16,16,128]{2,1,0:T(8,128)}), f32[16,16,128]{2,1,0:T(8,128)S(1)}, u32[]{:S(2)}, u32[]{:S(2)}) %all-to-all-start.3) | async-done | bytes 131104 | tf_op jit(solution)/shard_map/all_to_all | solution.py:230
  195.8 13.1 %all_to_all.26 = f16[16,9,8,128]{3,2,1,0:T(8,128)(2,1)S(1)} all-to-all(f16[16,9,8,128]{3,2,1,0:T(8,128)(2,1)S(1)} %broadcast_in_dim.2), channel_id=1, replica_groups=mesh['yh'=2,'yl'=2,'zh'=4,'core'=2,'x'=4,'zl'=4] {'x','zl'}, dimensions={0} | all-to-all | bytes 589824 | tf_op jit(solution)/shard_map/all_to_all | solution.py:230
  (64 shorter events, 22.4 us)
Async XLA Ops:
  2.1 47.0 %all-to-all-start = ((bf16[8,128,384]{2,1,0:T(8,128)(2,1)}), bf16[8,128,384]{2,1,0:T(8,128)(2,1)S(1)}, u32[]{:S(2)}, u32[]{:S(2)}) async-start(bf16[8,128,384]{2,1,0:T(8,128)(2,1)} %shard_map.55), calls=%async_computation | async-start | bytes 1572864 | tf_op jit(solution)/shard_map/all_to_all | solution.py:230
  18.6 1.6 copy-start.2
  20.9 1.2 copy-start.3
  22.1 44.3 %collective-permute-start.1 = (f32[1,136,128]{2,1,0:T(8,128)S(1)}, f32[1,136,128]{2,1,0:T(8,128)S(1)}, u32[]{:S(2)}, u32[]{:S(2)}) collective-permute-start(f32[1,136,128]{2,1,0:T(8,128)S(1)} %get-tuple-element.15), channel_id=1, source_target_pairs={{0,1},{1,0},{2,3},{3,2},{4,5},{5,4},{6,7},{7,6},{8,9},{9,8},{10,11... | collective-permute-start | bytes 208904 | tf_op jit(solution)/shard_map/ppermute | solution.py:239
  25.1 41.3 %collective-permute-start.2 = (f32[1,136,128]{2,1,0:T(8,128)S(1)}, f32[1,136,128]{2,1,0:T(8,128)S(1)}, u32[]{:S(2)}, u32[]{:S(2)}) collective-permute-start(f32[1,136,128]{2,1,0:T(8,128)S(1)} %get-tuple-element.17), channel_id=1, source_target_pairs={{0,2},{1,3},{2,0},{3,1},{4,6},{5,7},{6,4},{7,5},{8,10},{9,11},{10,... | collective-permute-start | bytes 208904 | tf_op jit(solution)/shard_map/ppermute | solution.py:239
  28.5 38.0 %collective-permute-start.3 = (f32[1,136,128]{2,1,0:T(8,128)S(1)}, f32[1,136,128]{2,1,0:T(8,128)S(1)}, u32[]{:S(2)}, u32[]{:S(2)}) collective-permute-start(f32[1,136,128]{2,1,0:T(8,128)S(1)} %get-tuple-element.16), channel_id=1, source_target_pairs={{0,3},{1,2},{2,1},{3,0},{4,7},{5,6},{6,5},{7,4},{8,11},{9,10},{10,... | collective-permute-start | bytes 208904 | tf_op jit(solution)/shard_map/ppermute | solution.py:239
  49.1 21.6 %collective-permute-start = (bf16[8,128,128]{2,1,0:T(8,128)(2,1)S(1)}, bf16[8,128,128]{2,1,0:T(8,128)(2,1)S(1)}, u32[]{:S(2)}, u32[]{:S(2)}) collective-permute-start(bf16[8,128,128]{2,1,0:T(8,128)(2,1)S(1)} %slice.44), channel_id=1, source_target_pairs={{0,1},{1,0},{2,3},{3,2},{4,5},{5,4},{6,7},{7,6},{8,9},{9,8},{10,11... | collective-permute-start | bytes 786440 | tf_op jit(solution)/shard_map/ppermute | solution.py:239
  71.3 62.6 %all-to-all-start.1 = ((bf16[8,128,768]{2,1,0:T(8,128)(2,1)}), bf16[8,128,768]{2,1,0:T(8,128)(2,1)S(1)}, u32[]{:S(2)}, u32[]{:S(2)}) async-start(bf16[8,128,768]{2,1,0:T(8,128)(2,1)} %bitcast.36), calls=%async_computation.1 | async-start | bytes 3145728 | tf_op jit(solution)/shard_map/all_to_all | solution.py:230
  77.2 36.6 %copy-start.6 = (s32[8]{0:T(128)S(1)}, s32[8]{0:T(128)}, u32[]{:S(2)}) copy-start(s32[8]{0:T(128)} %ranks_ref.1) | copy-start | bytes 100
  77.3 48.8 %copy-start.7 = (bf16[8,128,256]{2,1,0:T(8,128)(2,1)}, bf16[8,128,256]{2,1,0:T(8,128)(2,1)S(1)}, u32[]{:S(2)}) copy-start(bf16[8,128,256]{2,1,0:T(8,128)(2,1)S(1)} %maximum_maximum_fusion.refs_0_) | copy-start | bytes 1572868
  77.4 48.8 %collective-permute-start.6 = (bf16[8,128,256]{2,1,0:T(8,128)(2,1)S(1)}, bf16[8,128,256]{2,1,0:T(8,128)(2,1)S(1)}, u32[]{:S(2)}, u32[]{:S(2)}) collective-permute-start(bf16[8,128,256]{2,1,0:T(8,128)(2,1)S(1)} %maximum_maximum_fusion.refs_0_), channel_id=1, source_target_pairs={{0,12},{4,0},{8,4},{12,8},{1,13},{5,1},{9,5},{13,9},{2,14},{6,2},{... | collective-permute-start | bytes 1572872 | tf_op jit(solution)/shard_map/ppermute | solution.py:244
  82.0 44.1 %collective-permute-start.7 = (bf16[8,128,256]{2,1,0:T(8,128)(2,1)S(1)}, bf16[8,128,256]{2,1,0:T(8,128)(2,1)}, u32[]{:S(2)}, u32[]{:S(2)}) collective-permute-start(bf16[8,128,256]{2,1,0:T(8,128)(2,1)S(1)} %maximum_maximum_fusion.refs_0_), channel_id=1, source_target_pairs={{0,8},{4,12},{8,0},{12,4},{1,9},{5,13},{9,1},{13,5},{2,10},{6,14},... | collective-permute-start | bytes 1572872 | tf_op jit(solution)/shard_map/ppermute | solution.py:244
  84.7 41.4 %collective-permute-start.8 = (bf16[8,128,256]{2,1,0:T(8,128)(2,1)S(1)}, bf16[8,128,256]{2,1,0:T(8,128)(2,1)}, u32[]{:S(2)}, u32[]{:S(2)}) collective-permute-start(bf16[8,128,256]{2,1,0:T(8,128)(2,1)S(1)} %maximum_maximum_fusion.refs_0_), channel_id=1, source_target_pairs={{0,4},{4,8},{8,12},{12,0},{1,5},{5,9},{9,13},{13,1},{2,6},{6,10},{... | collective-permute-start | bytes 1572872 | tf_op jit(solution)/shard_map/ppermute | solution.py:244
  87.6 18.5 %collective-permute-start.4 = (f32[1,136,128]{2,1,0:T(8,128)S(1)}, f32[1,136,128]{2,1,0:T(8,128)S(1)}, u32[]{:S(2)}, u32[]{:S(2)}) collective-permute-start(f32[1,136,128]{2,1,0:T(8,128)S(1)} %add_add_fusion), channel_id=1, source_target_pairs={{0,4},{4,0},{8,12},{12,8},{1,5},{5,1},{9,13},{13,9},{2,6},{6,2},{1... | collective-permute-start | bytes 208904 | tf_op jit(solution)/shard_map/ppermute | solution.py:239
  106.0 7.7 %collective-permute-start.5 = (f32[1,136,128]{2,1,0:T(8,128)S(1)}, f32[1,136,128]{2,1,0:T(8,128)S(1)}, u32[]{:S(2)}, u32[]{:S(2)}) collective-permute-start(f32[1,136,128]{2,1,0:T(8,128)S(1)} %add.79), channel_id=1, source_target_pairs={{0,8},{4,12},{8,0},{12,4},{1,9},{5,13},{9,1},{13,5},{2,10},{6,14},... | collective-permute-start | bytes 208904 | tf_op jit(solution)/shard_map/ppermute | solution.py:239
  128.1 2.6 %copy-start = (bf16[2,8,128,256]{3,2,1,0:T(8,128)(2,1)}, bf16[2,8,128,256]{3,2,1,0:T(8,128)(2,1)S(1)}, u32[]{:S(2)}) copy-start(bf16[2,8,128,256]{3,2,1,0:T(8,128)(2,1)S(1)} %pad_maximum_fusion.2.factors_ref) | copy-start | bytes 3145732
  128.6 3.8 %collective-permute-start.9 = (bf16[8,128,256]{2,1,0:T(8,128)(2,1)S(1)}, bf16[8,128,256]{2,1,0:T(8,128)(2,1)S(1)}, u32[]{:S(2)}, u32[]{:S(2)}) collective-permute-start(bf16[8,128,256]{2,1,0:T(8,128)(2,1)S(1)} %shard_map.60.level_ref), channel_id=1, source_target_pairs={{0,16},{16,0},{1,17},{17,1},{2,18},{18,2},{3,19},{19,3},{4,20},{20... | collective-permute-start | bytes 1572872 | tf_op jit(solution)/shard_map/ppermute | solution.py:239
  133.0 1.0 copy-start.4
  134.0 1.2 copy-start.1
  135.2 6.3 %copy-start.5 = (f32[4,256,256]{2,1,0:T(8,128)S(1)}, f32[4,256,256]{2,1,0:T(8,128)}, u32[]{:S(2)}) copy-start(f32[4,256,256]{2,1,0:T(8,128)} %copy-done.4) | copy-start | bytes 3145732
  136.2 5.3 %collective-permute-start.10 = (bf16[8,128,768]{2,1,0:T(8,128)(2,1)S(1)}, bf16[8,128,768]{2,1,0:T(8,128)(2,1)S(1)}, u32[]{:S(2)}, u32[]{:S(2)}) collective-permute-start(bf16[8,128,768]{2,1,0:T(8,128)(2,1)S(1)} %shard_map.62.level_ref), channel_id=1, source_target_pairs={{0,16},{16,0},{1,17},{17,1},{2,18},{18,2},{3,19},{19,3},{4,20},{20... | collective-permute-start | bytes 4718600 | tf_op jit(solution)/shard_map/ppermute | solution.py:239
  160.9 34.3 %all-to-all-start.3 = ((f32[16,16,128]{2,1,0:T(8,128)}), f32[16,16,128]{2,1,0:T(8,128)S(1)}, u32[]{:S(2)}, u32[]{:S(2)}) async-start(f32[16,16,128]{2,1,0:T(8,128)} %bitcast.16), calls=%async_computation.3 | async-start | bytes 262144 | tf_op jit(solution)/shard_map/all_to_all | solution.py:230
  180.5 10.6 %collective-permute-start.11 = (f32[2,128,128]{2,1,0:T(8,128)S(1)}, f32[2,128,128]{2,1,0:T(8,128)S(1)}, u32[]{:S(2)}, u32[]{:S(2)}) collective-permute-start(f32[2,128,128]{2,1,0:T(8,128)S(1)} %shard_map.57), channel_id=1, source_target_pairs={{0,1},{1,0},{2,3},{3,2},{4,5},{5,4},{6,7},{7,6},{8,9},{9,8},{10,11... | collective-permute-start | bytes 393224 | tf_op jit(solution)/shard_map/ppermute | solution.py:239

commit v8 on v6

--- a/solution.py
+++ b/solution.py
@@ -350,8 +350,8 @@
     cross = sums_call(cross_kernel, (2, 4, 4, 32, RANK), upper, level, paired, second, sums)
 
     cross = exchange(cross.reshape(2 * 4, 4, 32, RANK), ("yl", "x"))
-    cross = cross.reshape(2, 4, 4, 2, 16, RANK).sum(1)
-    cross = cross.transpose(1, 0, 2, 3, 4).reshape(16, 16, RANK)
+    cross = cross.reshape(2, 4, 4, 2, 16, RANK)
+    cross = jnp.stack([cross[0].sum(0), cross[1].sum(0)], axis=1).reshape(16, 16, RANK)
     cross = exchange(cross, ("zh", "zl")).reshape(4, 4, 16, RANK).sum(1)
     pairs = jnp.stack([inverse, swap(inverse, "zl", 1)])
     pairs = [lax.dynamic_index_in_dim(pairs, zl_at % 2 ^ p, 0, False) for p in range(2)]

time: 211 us -> 211 us (level)
  no operation moved by 1% of the time
where the time goes in v8:
time: 211 us; the launch traced here: 210 us
  starting transfers between devices  104 us (49%)
  waiting for transfers between devices  48.6 us (23%)
  blocking collectives  27.6 us (13%)
  Pallas kernels  20.2 us (10%)
  local copies, waits for them, and re-layouts  5.47 us (3%)
  other arithmetic  3.1 us (1%)
    all_to_all x3, starting transfers between devices, exchange(): return lax.all_to_all(blocks, axes, 0, 0, tiled=True)  51.9 us
    ppermute x9, starting transfers between devices, swap(): lax.ppermute(block, axis, [(i, i ^ bit) for i in range(lax.axis_size(axis...  41.8 us
    ppermute x9, waiting for transfers between devices, swap(): lax.ppermute(block, axis, [(i, i ^ bit) for i in range(lax.axis_size(axis...  32 us
    all_to_all x2, blocking collectives, exchange(): return lax.all_to_all(blocks, axes, 0, 0, tiled=True)  27.6 us
    all_to_all x3, waiting for transfers between devices, exchange(): return lax.all_to_all(blocks, axes, 0, 0, tiled=True)  16.6 us
    pallas_call x1, Pallas kernels, invert(): pl.pallas_call(invert_kernel, out_shape=jax.ShapeDtypeStruct((2, RANK, RA...  11.7 us
    ppermute x3, starting transfers between devices, along_x(): lax.ppermute(block, 'x', [(i, (i - d) % count) for i in range(count)])  10.2 us
  transfers between devices with their start and end apart: 15, of which 9 were waited for; matrix products, arithmetic and copies ran while one was open for 2% of the time, Pallas kernels for 7%

profile of v8, /device:TPU:24, one launch (start us, length us, event | category | flops | bytes accessed | tf_op | source)
XLA Modules:
  0.0 209.7 jit_solution(16105590825018468193)
XLA Ops:
  2.1 16.5 %all-to-all-start = ((bf16[8,128,256]{2,1,0:T(8,128)(2,1)}), bf16[8,128,256]{2,1,0:T(8,128)(2,1)S(1)}, u32[]{:S(2)}, u32[]{:S(2)}) async-start(bf16[8,128,256]{2,1,0:T(8,128)(2,1)} %shard_map.55), calls=%async_computation | async-start | bytes 1048576 | tf_op jit(solution)/shard_map/all_to_all | solution.py:230
  20.7 2.9 %collective-permute-start.1 = (f32[1,136,128]{2,1,0:T(8,128)S(1)}, f32[1,136,128]{2,1,0:T(8,128)S(1)}, u32[]{:S(2)}, u32[]{:S(2)}) collective-permute-start(f32[1,136,128]{2,1,0:T(8,128)S(1)} %get-tuple-element.17), channel_id=1, source_target_pairs={{0,1},{1,0},{2,3},{3,2},{4,5},{5,4},{6,7},{7,6},{8,9},{9,8},{10,11... | collective-permute-start | bytes 208904 | tf_op jit(solution)/shard_map/ppermute | solution.py:239
  23.6 3.4 %collective-permute-start.2 = (f32[1,136,128]{2,1,0:T(8,128)S(1)}, f32[1,136,128]{2,1,0:T(8,128)S(1)}, u32[]{:S(2)}, u32[]{:S(2)}) collective-permute-start(f32[1,136,128]{2,1,0:T(8,128)S(1)} %get-tuple-element.19), channel_id=1, source_target_pairs={{0,2},{1,3},{2,0},{3,1},{4,6},{5,7},{6,4},{7,5},{8,10},{9,11},{10,... | collective-permute-start | bytes 208904 | tf_op jit(solution)/shard_map/ppermute | solution.py:239
  27.0 3.8 %collective-permute-start.3 = (f32[1,136,128]{2,1,0:T(8,128)S(1)}, f32[1,136,128]{2,1,0:T(8,128)S(1)}, u32[]{:S(2)}, u32[]{:S(2)}) collective-permute-start(f32[1,136,128]{2,1,0:T(8,128)S(1)} %get-tuple-element.18), channel_id=1, source_target_pairs={{0,3},{1,2},{2,1},{3,0},{4,7},{5,6},{6,5},{7,4},{8,11},{9,10},{10,... | collective-permute-start | bytes 208904 | tf_op jit(solution)/shard_map/ppermute | solution.py:239
  30.8 9.7 %all-to-all-done.base_ref = bf16[8,128,256]{2,1,0:T(8,128)(2,1)S(1)} async-done(((bf16[8,128,256]{2,1,0:T(8,128)(2,1)}), bf16[8,128,256]{2,1,0:T(8,128)(2,1)S(1)}, u32[]{:S(2)}, u32[]{:S(2)}) %all-to-all-start) | async-done | bytes 524320 | tf_op jit(solution)/shard_map/all_to_all | solution.py:230
  40.5 14.8 %collective-permute-start = (bf16[8,128,128]{2,1,0:T(8,128)(2,1)S(1)}, bf16[8,128,128]{2,1,0:T(8,128)(2,1)S(1)}, u32[]{:S(2)}, u32[]{:S(2)}) collective-permute-start(bf16[8,128,128]{2,1,0:T(8,128)(2,1)S(1)} %slice.54), channel_id=1, source_target_pairs={{0,1},{1,0},{2,3},{3,2},{4,5},{5,4},{6,7},{7,6},{8,9},{9,8},{10,11... | collective-permute-start | bytes 786440 | tf_op jit(solution)/shard_map/ppermute | solution.py:239
  56.0 3.7 %collective-permute-done = bf16[8,128,128]{2,1,0:T(8,128)(2,1)S(1)} collective-permute-done((bf16[8,128,128]{2,1,0:T(8,128)(2,1)S(1)}, bf16[8,128,128]{2,1,0:T(8,128)(2,1)S(1)}, u32[]{:S(2)}, u32[]{:S(2)}) %collective-permute-start) | collective-permute-done | bytes 262176 | tf_op jit(solution)/shard_map/ppermute | solution.py:239
  60.2 5.5 %all-to-all-start.1 = ((bf16[8,128,896]{2,1,0:T(8,128)(2,1)}), bf16[8,128,896]{2,1,0:T(8,128)(2,1)S(1)}, u32[]{:S(2)}, u32[]{:S(2)}) async-start(bf16[8,128,896]{2,1,0:T(8,128)(2,1)} %bitcast.36), calls=%async_computation.1 | async-start | bytes 3670016 | tf_op jit(solution)/shard_map/all_to_all | solution.py:230
  65.9 4.7 %collective-permute-start.6 = (bf16[8,128,256]{2,1,0:T(8,128)(2,1)S(1)}, bf16[8,128,256]{2,1,0:T(8,128)(2,1)S(1)}, u32[]{:S(2)}, u32[]{:S(2)}) collective-permute-start(bf16[8,128,256]{2,1,0:T(8,128)(2,1)S(1)} %maximum_maximum_fusion.refs_0_), channel_id=1, source_target_pairs={{0,12},{4,0},{8,4},{12,8},{1,13},{5,1},{9,5},{13,9},{2,14},{6,2},{... | collective-permute-start | bytes 1572872 | tf_op jit(solution)/shard_map/ppermute | solution.py:244
  70.5 2.7 %collective-permute-start.7 = (bf16[8,128,256]{2,1,0:T(8,128)(2,1)S(1)}, bf16[8,128,256]{2,1,0:T(8,128)(2,1)}, u32[]{:S(2)}, u32[]{:S(2)}) collective-permute-start(bf16[8,128,256]{2,1,0:T(8,128)(2,1)S(1)} %maximum_maximum_fusion.refs_0_), channel_id=1, source_target_pairs={{0,8},{4,12},{8,0},{12,4},{1,9},{5,13},{9,1},{13,5},{2,10},{6,14},... | collective-permute-start | bytes 1572872 | tf_op jit(solution)/shard_map/ppermute | solution.py:244
  73.3 2.8 %collective-permute-start.8 = (bf16[8,128,256]{2,1,0:T(8,128)(2,1)S(1)}, bf16[8,128,256]{2,1,0:T(8,128)(2,1)}, u32[]{:S(2)}, u32[]{:S(2)}) collective-permute-start(bf16[8,128,256]{2,1,0:T(8,128)(2,1)S(1)} %maximum_maximum_fusion.refs_0_), channel_id=1, source_target_pairs={{0,4},{4,8},{8,12},{12,0},{1,5},{5,9},{9,13},{13,1},{2,6},{6,10},{... | collective-permute-start | bytes 1572872 | tf_op jit(solution)/shard_map/ppermute | solution.py:244
  76.1 3.7 %collective-permute-start.4 = (f32[1,136,128]{2,1,0:T(8,128)S(1)}, f32[1,136,128]{2,1,0:T(8,128)S(1)}, u32[]{:S(2)}, u32[]{:S(2)}) collective-permute-start(f32[1,136,128]{2,1,0:T(8,128)S(1)} %add_add_fusion), channel_id=1, source_target_pairs={{0,4},{4,0},{8,12},{12,8},{1,5},{5,1},{9,13},{13,9},{2,6},{6,2},{1... | collective-permute-start | bytes 208904 | tf_op jit(solution)/shard_map/ppermute | solution.py:239
  79.8 14.4 %collective-permute-done.4 = f32[1,136,128]{2,1,0:T(8,128)S(1)} collective-permute-done((f32[1,136,128]{2,1,0:T(8,128)S(1)}, f32[1,136,128]{2,1,0:T(8,128)S(1)}, u32[]{:S(2)}, u32[]{:S(2)}) %collective-permute-start.4) | collective-permute-done | bytes 69664 | tf_op jit(solution)/shard_map/ppermute | solution.py:239
  94.2 5.4 %collective-permute-start.5 = (f32[1,136,128]{2,1,0:T(8,128)S(1)}, f32[1,136,128]{2,1,0:T(8,128)S(1)}, u32[]{:S(2)}, u32[]{:S(2)}) collective-permute-start(f32[1,136,128]{2,1,0:T(8,128)S(1)} %add.79), channel_id=1, source_target_pairs={{0,8},{4,12},{8,0},{12,4},{1,9},{5,13},{9,1},{13,5},{2,10},{6,14},... | collective-permute-start | bytes 208904 | tf_op jit(solution)/shard_map/ppermute | solution.py:239
  101.9 11.7 %shard_map.57 = f32[2,128,128]{2,1,0:T(8,128)S(1)} custom-call(s32[1]{0:T(128)} %bitcast.3.place_ref, s32[8]{0:T(128)S(1)} %copy-done.6, f32[1,136,128]{2,1,0:T(8,128)S(1)} %add.80.packed_ref), custom_call_target="tpu_custom_call" | custom-call | tf_op jit(solution)/shard_map/pallas_call | solution.py:98
  121.9 2.9 %all-to-all-done.1.base_ref = bf16[8,128,896]{2,1,0:T(8,128)(2,1)S(1)} async-done(((bf16[8,128,896]{2,1,0:T(8,128)(2,1)}), bf16[8,128,896]{2,1,0:T(8,128)(2,1)S(1)}, u32[]{:S(2)}, u32[]{:S(2)}) %all-to-all-start.1) | async-done | bytes 1835040 | tf_op jit(solution)/shard_map/all_to_all | solution.py:230
  128.2 3.6 %collective-permute-done.10.paired_ref = bf16[8,128,896]{2,1,0:T(8,128)(2,1)S(1)} collective-permute-done((bf16[8,128,896]{2,1,0:T(8,128)(2,1)S(1)}, bf16[8,128,896]{2,1,0:T(8,128)(2,1)S(1)}, u32[]{:S(2)}, u32[]{:S(2)}) %collective-permute-start.10) | collective-permute-done | bytes 1835040 | tf_op jit(solution)/shard_map/ppermute | solution.py:239
  131.8 3.1 %shard_map.63 = f32[2,4,4,32,128]{4,3,2,1,0:T(8,128)S(1)} custom-call(bf16[2,8,128,256]{3,2,1,0:T(8,128)(2,1)S(1)} %copy-done.1, bf16[8,128,896]{2,1,0:T(8,128)(2,1)S(1)} %shard_map.62.level_ref, bf16[8,128,896]{2,1,0:T(8,128)(2,1)S(1)} %collective-permute-done.10.paired_ref, bf16[8,128,896]{2,1,0:T(8,128)(2,1)S(1)} %all-to-all-done.1.base_ref, ...), custom_call_target="tpu_custom_call" | custom-call | tf_op jit(solution)/shard_map/pallas_call | solution.py:200
  134.9 14.5 %all_to_all.25 = f32[8,4,32,128]{3,2,1,0:T(8,128)S(1)} all-to-all(f32[8,4,32,128]{3,2,1,0:T(8,128)S(1)} %bitcast.37), channel_id=1, replica_groups=mesh['yh'=2,'yl'=2,'zh'=4,'core'=2,'x'=4,'zl'=4] {'yl','x'}, dimensions={0} | all-to-all | bytes 1048576 | tf_op jit(solution)/shard_map/all_to_all | solution.py:230
  150.1 29.9 %all-to-all-start.3 = ((f32[16,16,128]{2,1,0:T(8,128)}), f32[16,16,128]{2,1,0:T(8,128)S(1)}, u32[]{:S(2)}, u32[]{:S(2)}) async-start(f32[16,16,128]{2,1,0:T(8,128)} %bitcast.16), calls=%async_computation.3 | async-start | bytes 262144 | tf_op jit(solution)/shard_map/all_to_all | solution.py:230
  180.0 3.8 %collective-permute-start.11 = (f32[2,128,128]{2,1,0:T(8,128)S(1)}, f32[2,128,128]{2,1,0:T(8,128)S(1)}, u32[]{:S(2)}, u32[]{:S(2)}) collective-permute-start(f32[2,128,128]{2,1,0:T(8,128)S(1)} %shard_map.57), channel_id=1, source_target_pairs={{0,1},{1,0},{2,3},{3,2},{4,5},{5,4},{6,7},{7,6},{8,9},{9,8},{10,11... | collective-permute-start | bytes 393224 | tf_op jit(solution)/shard_map/ppermute | solution.py:239
  183.9 6.7 %collective-permute-done.11 = f32[2,128,128]{2,1,0:T(8,128)S(1)} collective-permute-done((f32[2,128,128]{2,1,0:T(8,128)S(1)}, f32[2,128,128]{2,1,0:T(8,128)S(1)}, u32[]{:S(2)}, u32[]{:S(2)}) %collective-permute-start.11) | collective-permute-done | bytes 131104 | tf_op jit(solution)/shard_map/ppermute | solution.py:239
  190.6 4.0 %all-to-all-done.3 = f32[16,16,128]{2,1,0:T(8,128)S(1)} async-done(((f32[16,16,128]{2,1,0:T(8,128)}), f32[16,16,128]{2,1,0:T(8,128)S(1)}, u32[]{:S(2)}, u32[]{:S(2)}) %all-to-all-start.3) | async-done | bytes 131104 | tf_op jit(solution)/shard_map/all_to_all | solution.py:230
  195.3 13.1 %all_to_all.26 = f16[16,9,8,128]{3,2,1,0:T(8,128)(2,1)S(1)} all-to-all(f16[16,9,8,128]{3,2,1,0:T(8,128)(2,1)S(1)} %broadcast_in_dim.2), channel_id=1, replica_groups=mesh['yh'=2,'yl'=2,'zh'=4,'core'=2,'x'=4,'zl'=4] {'x','zl'}, dimensions={0} | all-to-all | bytes 589824 | tf_op jit(solution)/shard_map/all_to_all | solution.py:230
  (64 shorter events, 21.9 us)
Async XLA Ops:
  0.0 18.6 %copy-start.2 = (bf16[1024,1024]{1,0:T(8,128)(2,1)S(1)}, bf16[1024,1024]{1,0:T(8,128)(2,1)}, u32[]{:S(2)}) copy-start(bf16[1024,1024]{1,0:T(8,128)(2,1)} %panels_ref.3) | copy-start | bytes 6291460
  2.1 38.4 %all-to-all-start = ((bf16[8,128,256]{2,1,0:T(8,128)(2,1)}), bf16[8,128,256]{2,1,0:T(8,128)(2,1)S(1)}, u32[]{:S(2)}, u32[]{:S(2)}) async-start(bf16[8,128,256]{2,1,0:T(8,128)(2,1)} %shard_map.55), calls=%async_computation | async-start | bytes 1048576 | tf_op jit(solution)/shard_map/all_to_all | solution.py:230
  19.4 1.2 copy-start.3
  20.7 34.6 %collective-permute-start.1 = (f32[1,136,128]{2,1,0:T(8,128)S(1)}, f32[1,136,128]{2,1,0:T(8,128)S(1)}, u32[]{:S(2)}, u32[]{:S(2)}) collective-permute-start(f32[1,136,128]{2,1,0:T(8,128)S(1)} %get-tuple-element.17), channel_id=1, source_target_pairs={{0,1},{1,0},{2,3},{3,2},{4,5},{5,4},{6,7},{7,6},{8,9},{9,8},{10,11... | collective-permute-start | bytes 208904 | tf_op jit(solution)/shard_map/ppermute | solution.py:239
  23.6 31.7 %collective-permute-start.2 = (f32[1,136,128]{2,1,0:T(8,128)S(1)}, f32[1,136,128]{2,1,0:T(8,128)S(1)}, u32[]{:S(2)}, u32[]{:S(2)}) collective-permute-start(f32[1,136,128]{2,1,0:T(8,128)S(1)} %get-tuple-element.19), channel_id=1, source_target_pairs={{0,2},{1,3},{2,0},{3,1},{4,6},{5,7},{6,4},{7,5},{8,10},{9,11},{10,... | collective-permute-start | bytes 208904 | tf_op jit(solution)/shard_map/ppermute | solution.py:239
  27.0 28.3 %collective-permute-start.3 = (f32[1,136,128]{2,1,0:T(8,128)S(1)}, f32[1,136,128]{2,1,0:T(8,128)S(1)}, u32[]{:S(2)}, u32[]{:S(2)}) collective-permute-start(f32[1,136,128]{2,1,0:T(8,128)S(1)} %get-tuple-element.18), channel_id=1, source_target_pairs={{0,3},{1,2},{2,1},{3,0},{4,7},{5,6},{6,5},{7,4},{8,11},{9,10},{10,... | collective-permute-start | bytes 208904 | tf_op jit(solution)/shard_map/ppermute | solution.py:239
  40.5 19.1 %collective-permute-start = (bf16[8,128,128]{2,1,0:T(8,128)(2,1)S(1)}, bf16[8,128,128]{2,1,0:T(8,128)(2,1)S(1)}, u32[]{:S(2)}, u32[]{:S(2)}) collective-permute-start(bf16[8,128,128]{2,1,0:T(8,128)(2,1)S(1)} %slice.54), channel_id=1, source_target_pairs={{0,1},{1,0},{2,3},{3,2},{4,5},{5,4},{6,7},{7,6},{8,9},{9,8},{10,11... | collective-permute-start | bytes 786440 | tf_op jit(solution)/shard_map/ppermute | solution.py:239
  60.2 64.6 %all-to-all-start.1 = ((bf16[8,128,896]{2,1,0:T(8,128)(2,1)}), bf16[8,128,896]{2,1,0:T(8,128)(2,1)S(1)}, u32[]{:S(2)}, u32[]{:S(2)}) async-start(bf16[8,128,896]{2,1,0:T(8,128)(2,1)} %bitcast.36), calls=%async_computation.1 | async-start | bytes 3670016 | tf_op jit(solution)/shard_map/all_to_all | solution.py:230
  65.7 36.3 %copy-start.6 = (s32[8]{0:T(128)S(1)}, s32[8]{0:T(128)}, u32[]{:S(2)}) copy-start(s32[8]{0:T(128)} %ranks_ref.1) | copy-start | bytes 100
  65.9 48.4 %copy-start.7 = (bf16[8,128,256]{2,1,0:T(8,128)(2,1)}, bf16[8,128,256]{2,1,0:T(8,128)(2,1)S(1)}, u32[]{:S(2)}) copy-start(bf16[8,128,256]{2,1,0:T(8,128)(2,1)S(1)} %maximum_maximum_fusion.refs_0_) | copy-start | bytes 1572868
  65.9 48.4 %collective-permute-start.6 = (bf16[8,128,256]{2,1,0:T(8,128)(2,1)S(1)}, bf16[8,128,256]{2,1,0:T(8,128)(2,1)S(1)}, u32[]{:S(2)}, u32[]{:S(2)}) collective-permute-start(bf16[8,128,256]{2,1,0:T(8,128)(2,1)S(1)} %maximum_maximum_fusion.refs_0_), channel_id=1, source_target_pairs={{0,12},{4,0},{8,4},{12,8},{1,13},{5,1},{9,5},{13,9},{2,14},{6,2},{... | collective-permute-start | bytes 1572872 | tf_op jit(solution)/shard_map/ppermute | solution.py:244
  70.5 43.7 %collective-permute-start.7 = (bf16[8,128,256]{2,1,0:T(8,128)(2,1)S(1)}, bf16[8,128,256]{2,1,0:T(8,128)(2,1)}, u32[]{:S(2)}, u32[]{:S(2)}) collective-permute-start(bf16[8,128,256]{2,1,0:T(8,128)(2,1)S(1)} %maximum_maximum_fusion.refs_0_), channel_id=1, source_target_pairs={{0,8},{4,12},{8,0},{12,4},{1,9},{5,13},{9,1},{13,5},{2,10},{6,14},... | collective-permute-start | bytes 1572872 | tf_op jit(solution)/shard_map/ppermute | solution.py:244
  73.3 41.0 %collective-permute-start.8 = (bf16[8,128,256]{2,1,0:T(8,128)(2,1)S(1)}, bf16[8,128,256]{2,1,0:T(8,128)(2,1)}, u32[]{:S(2)}, u32[]{:S(2)}) collective-permute-start(bf16[8,128,256]{2,1,0:T(8,128)(2,1)S(1)} %maximum_maximum_fusion.refs_0_), channel_id=1, source_target_pairs={{0,4},{4,8},{8,12},{12,0},{1,5},{5,9},{9,13},{13,1},{2,6},{6,10},{... | collective-permute-start | bytes 1572872 | tf_op jit(solution)/shard_map/ppermute | solution.py:244
  76.1 18.1 %collective-permute-start.4 = (f32[1,136,128]{2,1,0:T(8,128)S(1)}, f32[1,136,128]{2,1,0:T(8,128)S(1)}, u32[]{:S(2)}, u32[]{:S(2)}) collective-permute-start(f32[1,136,128]{2,1,0:T(8,128)S(1)} %add_add_fusion), channel_id=1, source_target_pairs={{0,4},{4,0},{8,12},{12,8},{1,5},{5,1},{9,13},{13,9},{2,6},{6,2},{1... | collective-permute-start | bytes 208904 | tf_op jit(solution)/shard_map/ppermute | solution.py:239
  94.2 7.7 %collective-permute-start.5 = (f32[1,136,128]{2,1,0:T(8,128)S(1)}, f32[1,136,128]{2,1,0:T(8,128)S(1)}, u32[]{:S(2)}, u32[]{:S(2)}) collective-permute-start(f32[1,136,128]{2,1,0:T(8,128)S(1)} %add.79), channel_id=1, source_target_pairs={{0,8},{4,12},{8,0},{12,4},{1,9},{5,13},{9,1},{13,5},{2,10},{6,14},... | collective-permute-start | bytes 208904 | tf_op jit(solution)/shard_map/ppermute | solution.py:239
  116.8 3.4 %collective-permute-start.9 = (bf16[8,128,128]{2,1,0:T(8,128)(2,1)S(1)}, bf16[8,128,128]{2,1,0:T(8,128)(2,1)S(1)}, u32[]{:S(2)}, u32[]{:S(2)}) collective-permute-start(bf16[8,128,128]{2,1,0:T(8,128)(2,1)S(1)} %shard_map.60.level_ref), channel_id=1, source_target_pairs={{0,16},{16,0},{1,17},{17,1},{2,18},{18,2},{3,19},{19,3},{4,20},{20... | collective-permute-start | bytes 786440 | tf_op jit(solution)/shard_map/ppermute | solution.py:239
  118.9 2.0 copy-start
  120.9 1.0 copy-start.4
  124.8 6.9 %copy-start.1 = (bf16[2,8,128,256]{3,2,1,0:T(8,128)(2,1)S(1)}, bf16[2,8,128,256]{3,2,1,0:T(8,128)(2,1)}, u32[]{:S(2)}) copy-start(bf16[2,8,128,256]{3,2,1,0:T(8,128)(2,1)} %copy-done) | copy-start | bytes 3145732
  124.8 6.9 %copy-start.5 = (f32[4,256,256]{2,1,0:T(8,128)S(1)}, f32[4,256,256]{2,1,0:T(8,128)}, u32[]{:S(2)}) copy-start(f32[4,256,256]{2,1,0:T(8,128)} %copy-done.4) | copy-start | bytes 3145732
  126.1 5.7 %collective-permute-start.10 = (bf16[8,128,896]{2,1,0:T(8,128)(2,1)S(1)}, bf16[8,128,896]{2,1,0:T(8,128)(2,1)S(1)}, u32[]{:S(2)}, u32[]{:S(2)}) collective-permute-start(bf16[8,128,896]{2,1,0:T(8,128)(2,1)S(1)} %shard_map.62.level_ref), channel_id=1, source_target_pairs={{0,16},{16,0},{1,17},{17,1},{2,18},{18,2},{3,19},{19,3},{4,20},{20... | collective-permute-start | bytes 5505032 | tf_op jit(solution)/shard_map/ppermute | solution.py:239
  150.1 44.5 %all-to-all-start.3 = ((f32[16,16,128]{2,1,0:T(8,128)}), f32[16,16,128]{2,1,0:T(8,128)S(1)}, u32[]{:S(2)}, u32[]{:S(2)}) async-start(f32[16,16,128]{2,1,0:T(8,128)} %bitcast.16), calls=%async_computation.3 | async-start | bytes 262144 | tf_op jit(solution)/shard_map/all_to_all | solution.py:230
  180.0 10.5 %collective-permute-start.11 = (f32[2,128,128]{2,1,0:T(8,128)S(1)}, f32[2,128,128]{2,1,0:T(8,128)S(1)}, u32[]{:S(2)}, u32[]{:S(2)}) collective-permute-start(f32[2,128,128]{2,1,0:T(8,128)S(1)} %shard_map.57), channel_id=1, source_target_pairs={{0,1},{1,0},{2,3},{3,2},{4,5},{5,4},{6,7},{7,6},{8,9},{9,8},{10,11... | collective-permute-start | bytes 393224 | tf_op jit(solution)/shard_map/ppermute | solution.py:239
